TPU v7x, 32 devices: a whole 2x2x4 slice. The times are simulated.
32 devices in a mesh: dp: 8 (over y, x, core), ctx: 4 (over z).
Axes of the slice: x: 2, y: 2, z: 4, core: 2. Of those that a mesh axis runs over, the one named last changes fastest.
Arguments:
- tokens: bfloat16 [8, 896, 2048], P('dp', 'ctx'), may hold values from -6 to 6
- norm_gain: bfloat16 [2048], replicated, may hold values from 0.099609375 to 1.8984375
- q_weight: bfloat16 [2048, 2048], P('dp'), may hold values from -0.110927376 to 0.110927376
- k_weight: bfloat16 [2048, 2048], P('dp'), may hold values from -6.408155204503087 to 6.408155204503087
- v_weight: bfloat16 [2048, 2048], P('dp'), may hold values from -0.125 to 0.125
Outputs:
- attended: bfloat16 [8, 896, 2048], P('dp', 'ctx')
All inputs are finite; a program needn't handle non-finite values.
Results may differ from a plain program's by a relative error of at most 0.0055.
The roundings to bfloat16 on the way count: a program that leaves them out, or rounds other values in their place, can miss the bound.
Values may be sent and summed in bfloat16 or wider, within the bound.
No kernel may reach another device: no remote copies, remote signals or barrier semaphores. Data moves between devices by JAX's collectives and lax.ppermute only.
A program may use at most 128 MiB of HBM per device.

v0:
```python
import jax
import jax.numpy as jnp
from jax import lax
from jax.sharding import PartitionSpec as P

HEADS = 16
HEAD_DIM = 128


def rotate(values, positions):
    half = HEAD_DIM // 2
    shaped = values.reshape(values.shape[0], HEADS, HEAD_DIM)
    freqs = 10000.0 ** (-(jnp.arange(half).astype(jnp.float32) * 2.0) / HEAD_DIM)
    angles = positions[:, None] * freqs[None, :]
    cosine = jnp.cos(angles)[:, None, :]
    sine = jnp.sin(angles)[:, None, :]
    first = shaped[:, :, :half]
    second = shaped[:, :, half:]
    turned = jnp.concatenate(
        [first * cosine - second * sine, second * cosine + first * sine], axis=2
    )
    return turned.reshape(values.shape[0], HEADS * HEAD_DIM)


def shards(tokens, norm_gain, q_weight, k_weight, v_weight):
    seq_rows = tokens.shape[1]
    columns = q_weight.shape[1]
    own_block = lax.axis_index("ctx")
    rows = tokens[0].astype(jnp.float32)
    scale_rows = lax.rsqrt(jnp.mean(rows * rows, axis=1, keepdims=True) + 1e-05)
    normed = (rows * scale_rows * norm_gain.astype(jnp.float32)[None, :]).astype(jnp.bfloat16)
    pieces = (
        lax.all_gather(q_weight, "dp", axis=0, tiled=True),
        lax.all_gather(k_weight, "dp", axis=0, tiled=True),
        lax.all_gather(v_weight, "dp", axis=0, tiled=True),
    )
    count = pieces[0].shape[0]
    q_lin, k_lin, v_lin = tuple(
        (jnp.dot(normed, piece, preferred_element_type=jnp.float32) for piece in pieces)
    )
    values = v_lin.astype(jnp.bfloat16)
    own_positions = own_block * seq_rows + jnp.arange(seq_rows, dtype=jnp.int32)
    queries = rotate(q_lin, own_positions.astype(jnp.float32)).astype(jnp.bfloat16)
    keys = rotate(k_lin, own_positions.astype(jnp.float32)).astype(jnp.bfloat16)
    head_q = queries.reshape(seq_rows, HEADS, HEAD_DIM)
    factor = HEAD_DIM ** (-0.5)
    last_query = jnp.max(own_positions)
    start_state = (
        jnp.full((seq_rows, HEADS), -1e30, jnp.float32),
        jnp.zeros((seq_rows, HEADS), jnp.float32),
        jnp.zeros((seq_rows, HEADS, HEAD_DIM), jnp.float32),
    )
    key_block = lax.all_gather(keys, "ctx", axis=0, tiled=True)
    value_block = lax.all_gather(values, "ctx", axis=0, tiled=True)
    count = key_block.shape[0]
    key_pos = jnp.arange(count, dtype=jnp.int32)

    def work(state):
        peak, total, accum = state
        scores = (
            jnp.einsum(
                "qhd,khd->qhk",
                head_q,
                key_block.reshape(count, HEADS, HEAD_DIM),
                preferred_element_type=jnp.float32,
            )
            * factor
        )
        allowed = (key_pos[None, :] <= own_positions[:, None])[:, None, :]
        scores = jnp.where(allowed, scores, -1e30)
        new_peak = jnp.maximum(peak, jnp.max(scores, axis=2))
        expo = jnp.where(allowed, jnp.exp(scores - new_peak[:, :, None]), 0.0)
        total = jnp.sum(expo, axis=2)
        accum = jnp.einsum(
            "qhk,khd->qhd",
            expo.astype(jnp.bfloat16),
            value_block.reshape(count, HEADS, HEAD_DIM),
            preferred_element_type=jnp.float32,
        )
        return (new_peak, total, accum)

    peak, total, accum = lax.cond(
        jnp.int32(0) <= last_query, work, lambda state: state, start_state
    )
    attended = (accum / total[:, :, None]).reshape(seq_rows, columns).astype(jnp.bfloat16)
    return attended[None]


def solution(mesh):
    placed = (P("dp", "ctx", None), P(), P("dp", None), P("dp", None), P("dp", None))
    return jax.shard_map(
        shards, mesh=mesh, in_specs=placed, out_specs=P("dp", "ctx", None), check_vma=False
    )
```

profile of v0, /device:TPU:0, one launch (start us, length us, event | category | flops | bytes accessed | tf_op | source)
XLA Modules:
  0.0 347.0 jit_solution(8040718308278715805)
XLA Ops:
  6.5 0.0 copy-start.1
  6.5 0.0 all-gather.10.cloned.1.call-start
  6.5 0.7 all-gather.10.cloned.1.call-update
  7.3 0.0 all-gather.6.cloned.1.call-start
  7.3 0.7 all-gather.6.cloned.1.call-update
  8.0 0.0 all-gather.12.cloned.1.call-start
  8.1 0.7 all-gather.12.cloned.1.call-update
  8.7 0.0 all-gather.8.cloned.1.call-start
  8.8 0.7 convert_element_type.70
  9.5 0.7 fusion.34
  10.2 0.0 copy-done.1
  10.2 0.3 fusion.21
  10.4 0.5 multiply_cosine_fusion
  10.9 55.5 %all-gather.10.cloned.1.call-done = bf16[2048,2048]{1,0:T(8,128)(2,1)} async-done(((bf16[256,2048]{1,0:T(8,128)(2,1)}), bf16[2048,2048]{1,0:T(8,128)(2,1)}) %all-gather.10.cloned.1.call-update) | async-done | bytes 8388624 | tf_op jit(solution)/shard_map/all_gather | solution.py:33
  66.4 12.3 %copy.23 = bf16[2048,2048]{1,0:T(8,128)(2,1)} copy(bf16[2048,2048]{0,1:T(8,128)(2,1)} %bitcast.64) | data formatting | bytes 16777216 | tf_op jit(solution)/shard_map/dot_general | solution.py:39
  78.7 44.0 %all-gather.6.cloned.1.call-done = bf16[2048,2048]{1,0:T(8,128)(2,1)} async-done(((bf16[256,2048]{1,0:T(8,128)(2,1)}), bf16[2048,2048]{1,0:T(8,128)(2,1)}) %all-gather.6.cloned.1.call-update) | async-done | bytes 8388624 | tf_op jit(solution)/shard_map/all_gather | solution.py:34
  122.7 12.3 %copy.21 = bf16[2048,2048]{1,0:T(8,128)(2,1)} copy(bf16[2048,2048]{0,1:T(8,128)(2,1)} %bitcast.65) | data formatting | bytes 16777216 | tf_op jit(solution)/shard_map/dot_general | solution.py:39
  135.0 0.0 copy-start
  135.0 5.3 %fusion.30 = f32[224,16,128]{2,0,1:T(8,128)S(1)} fusion(bf16[16,128,2048]{2,1,0:T(8,128)(2,1)} %bitcast.66, bf16[1,224,2048]{2,1,0:T(8,128)(2,1)S(1)} %copy-done.1, f32[2048]{0:T(1024)S(1)} %convert_element_type.70, f32[224]{0:T(256)S(1)} %add_rsqrt_fusion), kind=kOutput, calls=%fused_computation.39 | convolution fusion | flops 1880883200 | bytes 11150208 | tf_op jit(solution)/shard_map/dot_general | solution.py:39
  140.4 0.5 copy-done
  140.9 2.8 fusion.32
  143.6 1.2 subtract_convert_fusion
  144.8 1.4 copy_bitcast_fusion
  146.2 0.0 all-gather.8.cloned.1.call-update
  146.2 0.0 all-gather.14.cloned.1.call-start
  146.3 32.7 %all-gather.12.cloned.1.call-done = bf16[2048,2048]{1,0:T(8,128)(2,1)} async-done(((bf16[256,2048]{1,0:T(8,128)(2,1)}), bf16[2048,2048]{1,0:T(8,128)(2,1)}) %all-gather.12.cloned.1.call-update) | async-done | bytes 8388624 | tf_op jit(solution)/shard_map/all_gather | solution.py:35
  179.0 6.5 %convolution_convert_fusion = bf16[224,2048]{1,0:T(8,128)(2,1)} fusion(bf16[2048,2048]{1,0:T(8,128)(2,1)} %all-gather.12.cloned.1.call-done, bf16[1,224,2048]{2,1,0:T(8,128)(2,1)S(1)} %copy-done.1, f32[2048]{0:T(1024)S(1)} %convert_element_type.70, f32[224]{0:T(256)S(1)} %add_rsqrt_fusion), kind=kOutput, calls=%fused_computation.18 | convolution fusion | flops 1881341952 | bytes 10232704 | tf_op jit(solution)/shard_map/dot_general | solution.py:39
  185.5 0.0 all-gather.14.cloned.1.call-update
  186.1 0.5 pad_maximum_fusion
  186.6 65.9 %all-gather.8.cloned.1.call-done = bf16[896,2048]{1,0:T(8,128)(2,1)} async-done(((bf16[224,2048]{1,0:T(8,128)(2,1)}), bf16[896,2048]{1,0:T(8,128)(2,1)}) %all-gather.8.cloned.1.call-update) | async-done | bytes 3670032 | tf_op jit(solution)/shard_map/all_gather | solution.py:53
  252.6 72.2 %all-gather.14.cloned.1.call-done = bf16[896,2048]{1,0:T(8,128)(2,1)} async-done(((bf16[224,2048]{1,0:T(8,128)(2,1)}), bf16[896,2048]{1,0:T(8,128)(2,1)}) %all-gather.14.cloned.1.call-update) | async-done | bytes 3670032 | tf_op jit(solution)/shard_map/all_gather | solution.py:54
  324.7 13.4 %conditional.1 = (f32[224,16]{0,1:T(8,128)S(1)}, f32[224,16,128]{2,0,1:T(8,128)S(1)}) conditional(s32[]{:T(128)} %convert_element_type.66, () %tuple.13, (s32[896]{0:T(1024)S(1)}, s32[224]{0:T(256)S(1)}, bf16[896,2048]{1,0:T(8,128)(2,1)}, bf16[224,16,128]{2,0,1:T(8,128)(2,1)S(1)}, bf16[896,2048]{1,0:T(8,128)(2,1)}) %tuple.14), branch_computations={%region_2.0_spmd, %region_3.6_spmd} | conditional | flops 1686110720 | bytes 64201132 | solution.py:82
  324.7 0.2 broadcast_compare_fusion
  324.9 0.0 copy-start.2
  324.9 4.7 %fusion = (f32[224,16]{0,1:T(8,128)S(1)}, f32[16,896,224]{1,2,0:T(8,128)S(1)}) fusion(pred[224,896]{1,0:T(8,128)(4,1)S(1)} %broadcast_compare_fusion, bf16[224,16,128]{2,0,1:T(8,128)(2,1)S(1)} %get-tuple-element.18, bf16[896,2048]{1,0:T(8,128)(2,1)} %get-tuple-element.17), kind=kOutput, calls=%fused_computation.2 | convolution fusion | flops 831713792 | bytes 17647616 | tf_op jit(solution)/shard_map/cond/branch_1_fun/qhd,khd->qhk/dot_general | solution.py:61
  329.7 0.0 copy-done.2
  329.7 4.1 %fusion.11 = f32[224,16,128]{2,0,1:T(8,128)S(1)} fusion(f32[16,896,224]{1,2,0:T(8,128)S(1)} %get-tuple-element.25, f32[224,16]{0,1:T(8,128)S(1)} %broadcast_maximum_fusion, pred[224,896]{1,0:T(8,128)(4,1)S(1)} %broadcast_compare_fusion, bf16[896,2048]{1,0:T(8,128)(2,1)S(1)} %copy-done.2), kind=kOutput, calls=%fused_computation.12 | convolution fusion | flops 838139904 | bytes 18565120 | tf_op jit(solution)/shard_map/cond/branch_1_fun/qhk,khd->qhd/dot_general | solution.py:74
  333.9 4.3 %fusion.2 = f32[224,16]{0,1:T(8,128)S(1)} fusion(f32[16,896,224]{1,2,0:T(8,128)S(1)} %get-tuple-element.25, f32[224,16]{0,1:T(8,128)S(1)} %broadcast_maximum_fusion, pred[224,896]{1,0:T(8,128)(4,1)S(1)} %broadcast_compare_fusion), kind=kLoop, calls=%fused_computation.4 | loop fusion | flops 16052736 | bytes 13074432 | tf_op jit(solution)/shard_map/cond/branch_1_fun/reduce_sum | solution.py:73
  338.2 0.5 divide_convert_fusion
  338.7 0.4 copy.24
  339.1 1.3 convert_element_type.79
  (5 shorter events, 0.0 us)
Async XLA Ops:
  6.5 3.6 %copy-start.1 = (bf16[1,224,2048]{2,1,0:T(8,128)(2,1)S(1)}, bf16[1,224,2048]{2,1,0:T(8,128)(2,1)}, u32[]{:S(2)}) copy-start(bf16[1,224,2048]{2,1,0:T(8,128)(2,1)} %param.7) | copy-start | bytes 2752516
  6.5 59.8 %all-gather.10.cloned.1.call-start = ((), (), s32[]{:S(2)}) async-start(), calls=%async_computation.2 | async-start | bytes 9437184 | tf_op jit(solution)/shard_map/all_gather | solution.py:33
  7.3 115.4 %all-gather.6.cloned.1.call-start = ((), (), s32[]{:S(2)}) async-start(), calls=%async_computation | async-start | bytes 9437184 | tf_op jit(solution)/shard_map/all_gather | solution.py:34
  8.0 171.0 %all-gather.12.cloned.1.call-start = ((), (), s32[]{:S(2)}) async-start(), calls=%async_computation.3 | async-start | bytes 9437184 | tf_op jit(solution)/shard_map/all_gather | solution.py:35
  8.7 243.8 %all-gather.8.cloned.1.call-start = ((), (), s32[]{:S(2)}) async-start(), calls=%async_computation.1 | async-start | bytes 4587520 | tf_op jit(solution)/shard_map/all_gather | solution.py:53
  135.0 5.8 %copy-start = (bf16[2048,2048]{1,0:T(8,128)(2,1)S(1)}, bf16[2048,2048]{1,0:T(8,128)(2,1)}, u32[]{:S(2)}) copy-start(bf16[2048,2048]{1,0:T(8,128)(2,1)} %copy.21) | copy-start | bytes 25165828
  146.2 178.5 %all-gather.14.cloned.1.call-start = ((), (), s32[]{:S(2)}) async-start(), calls=%async_computation.4 | async-start | bytes 4587520 | tf_op jit(solution)/shard_map/all_gather | solution.py:54
  324.9 4.8 %copy-start.2 = (bf16[896,2048]{1,0:T(8,128)(2,1)S(1)}, bf16[896,2048]{1,0:T(8,128)(2,1)}, u32[]{:S(2)}) copy-start(bf16[896,2048]{1,0:T(8,128)(2,1)} %get-tuple-element.19) | copy-start | bytes 11010052 | tf_op jit(solution)/shard_map/cond
Sparse Core Ops, SparseCore 0:
  9.2 57.0 all-gather.9
  68.3 54.3 all-gather.5
  124.6 54.3 all-gather.11
  180.4 72.1 all-gather.7
  254.0 70.7 all-gather.13
where the time goes:
time: 348 us; the launch traced here: 347 us
  waiting for transfers between devices  272 us (78%)
  local copies, waits for them, and re-layouts  26.8 us (8%)
  matrix products  23.5 us (7%)
  between operations  13.8 us (4%)
  other arithmetic  10.3 us (3%)
    all_gather x1, waiting for transfers between devices, shards(): value_block = lax.all_gather(values, 'ctx', axis=0, tiled=True)  72.2 us
    all_gather x1, waiting for transfers between devices, shards(): key_block = lax.all_gather(keys, 'ctx', axis=0, tiled=True)  65.9 us
    all_gather x1, waiting for transfers between devices, shards(): lax.all_gather(q_weight, 'dp', axis=0, tiled=True)  55.5 us
    all_gather x1, waiting for transfers between devices, shards(): lax.all_gather(k_weight, 'dp', axis=0, tiled=True)  44 us
    all_gather x1, waiting for transfers between devices, shards(): lax.all_gather(v_weight, 'dp', axis=0, tiled=True)  32.7 us
    dot_general x2, local copies, waits for them, and re-layouts, shards(): jnp.dot(normed, piece, preferred_element_type=jnp.float32)  24.7 us
    dot_general x3, matrix products, shards(): jnp.dot(normed, piece, preferred_element_type=jnp.float32)  14.6 us
  transfers between devices with their start and end apart: 5, of which 5 were waited for; matrix products, arithmetic and copies ran while one was open for 13% of the time, Pallas kernels for 0%

commit v1 on v0

v1 whole, which is shorter than its diff:
```python
import functools
import math

import jax
import jax.numpy as jnp
from jax import lax
from jax.experimental import pallas as pl
from jax.experimental.pallas import tpu as pltpu
from jax.sharding import PartitionSpec as P

HEADS = 16
HEAD_DIM = 128
HALF = HEAD_DIM // 2
EPS = 1e-05
VMEM_LIMIT = 56 * 1024 * 1024


def tables(length):
    freqs = 10000.0 ** (-(jnp.arange(HALF).astype(jnp.float32) * 2.0) / HEAD_DIM)
    angles = jnp.arange(length).astype(jnp.float32)[:, None] * freqs[None, :]
    cosine = jnp.cos(angles)
    sine = jnp.sin(angles)
    return (
        jnp.concatenate([cosine, cosine], axis=1),
        jnp.concatenate([-sine, sine], axis=1),
    )


def normalize(block, gain):
    rows = block.astype(jnp.float32)
    scale = lax.rsqrt(jnp.mean(rows * rows, axis=1, keepdims=True) + EPS)
    return (rows * scale * gain.astype(jnp.float32)).astype(jnp.bfloat16)


def project(normed, weights, cos_ref, sin_ref, starts, rows, cols, store):
    step = 2 * HEAD_DIM
    for first in range(0, 3 * cols, step):
        linear = jnp.dot(
            normed[...], weights[:, first : first + step], preferred_element_type=jnp.float32
        )
        for block, start in enumerate(starts):
            part = linear[block * rows : (block + 1) * rows]
            if first < 2 * cols:
                cosine = cos_ref[pl.ds(start, rows), :]
                sine = sin_ref[pl.ds(start, rows), :]
                heads = [part[:, h * HEAD_DIM : (h + 1) * HEAD_DIM] for h in range(2)]
                part = jnp.concatenate(
                    [x * cosine + pltpu.roll(x, HALF, 1) * sine for x in heads], axis=1
                )
            store(block, first, step, part.astype(jnp.bfloat16))


def start_weights(owners, shards, weights, sems):
    depth = shards[0].shape[0]
    copies = []
    for i, (owner, shard) in enumerate(zip(owners, shards)):
        copy = pltpu.make_async_copy(
            shard, weights.at[pl.ds(pl.multiple_of(owner * depth, depth), depth)], sems.at[i]
        )
        copy.start()
        copies.append(copy)
    return copies


def early_kernel(spec, *refs):
    n, m, rows, cols = spec["blocks"], spec["shards"], spec["rows"], spec["cols"]
    tokens, shards = refs[:n], refs[n : n + m]
    gain, cos_ref, sin_ref, out, held, normed, weights, token_sems, weight_sems = refs[n + m :]
    place, owners = spec["places"](), spec["owners"]()
    loads = []
    for i in range(n):
        load = pltpu.make_async_copy(
            tokens[i], held.at[pl.ds(i * rows, rows)], token_sems.at[i]
        )
        load.start()
        loads.append(load)
    weight_loads = start_weights(owners, shards, weights, weight_sems)
    for i in range(n):
        loads[i].wait()
        part = pl.ds(i * rows, rows)
        normed[part, :] = normalize(held[part, :], gain[...])
    for load in weight_loads:
        load.wait()
    starts = [pl.multiple_of(place[i] * rows, rows) for i in range(n)]

    def store(block, first, step, value):
        out[pl.ds(block * rows, rows), pl.ds(first, step)] = value

    project(normed, weights, cos_ref, sin_ref, starts, rows, cols, store)


def late_kernel(spec, *refs):
    n, m, rows, cols = spec["blocks"], spec["shards"], spec["rows"], spec["cols"]
    total = spec["total"]
    tokens, shards = refs[:2], refs[2 : 2 + m]
    early, gain, cos_ref, sin_ref = refs[2 + m : 6 + m]
    outs = refs[6 + m : 6 + m + total]
    held, normed, weights, qkv, result, token_sems, weight_sems, early_sems, out_sems = refs[6 + m + total :]
    place, owners = spec["places"](), spec["owners"]()
    me = spec["me"]()
    inner = spec["inner"]()
    weight_loads = start_weights(owners, shards, weights, weight_sems)

    @pl.when(inner)
    def _():
        pltpu.make_async_copy(tokens[0], held, token_sems.at[0]).start()

    @pl.when(jnp.logical_not(inner))
    def _():
        pltpu.make_async_copy(tokens[1], held, token_sems.at[0]).start()

    early_loads = []
    for i in range(n):
        load = pltpu.make_async_copy(
            early.at[pl.ds(i * rows, rows)],
            qkv.at[pl.ds(pl.multiple_of(place[i] * rows, rows), rows)],
            early_sems.at[i],
        )
        load.start()
        early_loads.append(load)
    pltpu.make_async_copy(tokens[0], held, token_sems.at[0]).wait()
    normed[...] = normalize(held[...], gain[...])
    for load in weight_loads:
        load.wait()
    last = pl.multiple_of(place[n] * rows, rows)

    def store(block, first, step, value):
        qkv[pl.ds(last, rows), pl.ds(first, step)] = value

    project(normed, weights, cos_ref, sin_ref, [last], rows, cols, store)
    for load in early_loads:
        load.wait()
    attend(qkv, result, me, total, rows, cols)
    copies = []
    for k in range(total):
        copy = pltpu.make_async_copy(result.at[k], outs[k], out_sems.at[k])
        copy.start()
        copies.append(copy)
    for copy in copies:
        copy.wait()


def attend(qkv, result, me, total, rows, cols):
    factor = HEAD_DIM ** (-0.5) * math.log2(math.e)
    below = lax.broadcasted_iota(jnp.int32, (rows, rows), 0) >= lax.broadcasted_iota(
        jnp.int32, (rows, rows), 1
    )
    for head in range(cols // HEAD_DIM):
        for block in range(total):
            size = (block + 1) * rows
            q = qkv[block * rows : size, head * HEAD_DIM : (head + 1) * HEAD_DIM]
            k = qkv[0:size, cols + head * HEAD_DIM : cols + (head + 1) * HEAD_DIM]
            v = qkv[0:size, 2 * cols + head * HEAD_DIM : 2 * cols + (head + 1) * HEAD_DIM]
            scores = lax.dot_general(
                q, k, (((1,), (1,)), ((), ())), preferred_element_type=jnp.float32
            )
            own = jnp.where(below, scores[:, block * rows :], -1e30)
            scores = jnp.concatenate([scores[:, : block * rows], own], axis=1) if block else own
            top = jnp.max(scores, axis=1, keepdims=True)
            expo = jnp.exp2((scores - top) * factor)
            bottom = jnp.sum(expo, axis=1, keepdims=True)
            numer = jnp.dot(expo.astype(jnp.bfloat16), v, preferred_element_type=jnp.float32)
            result[block ^ me, :, head * HEAD_DIM : (head + 1) * HEAD_DIM] = (
                numer / bottom
            ).astype(jnp.bfloat16)


def join_kernel(spec, *refs):
    total, cols = spec["total"], spec["cols"]
    pieces, out, sems = refs[:total], refs[total], refs[total + 1]
    me = spec["me"]()
    copies = []
    for k in range(total):
        copy = pltpu.make_async_copy(
            pieces[k],
            out.at[0, :, pl.ds(pl.multiple_of((me ^ k) * cols, cols), cols)],
            sems.at[k],
        )
        copy.start()
        copies.append(copy)
    for copy in copies:
        copy.wait()


def block_plan(dp, ctx):
    flat = lambda d, c: d * ctx + c
    every = [(d, c) for d in range(dp) for c in range(ctx)]
    make = lambda to: [
        (flat(d, c), flat(*to(d, c))) for d, c in every if to(d, c) is not None
    ]
    return make


def fast(dp, ctx, tokens, norm_gain, q_weight, k_weight, v_weight):
    rows, features = tokens.shape[1], tokens.shape[2]
    depth = q_weight.shape[0]
    cols = HEADS // ctx * HEAD_DIM
    make = block_plan(dp, ctx)
    axes = ("dp", "ctx")
    send = lambda value, perm: lax.ppermute(value, axes, perm)
    me = lax.axis_index("ctx")
    own = tokens[0]
    part = jnp.concatenate(
        [lax.dynamic_slice_in_dim(w, me * cols, cols, 1) for w in (q_weight, k_weight, v_weight)], axis=1
    )
    pair = make(lambda d, c: (d, c ^ 1))
    middle = make(lambda d, c: (d, 3 - c) if c in (1, 2) else None)
    outward = make(lambda d, c: (d, {1: 0, 2: 3}[c]) if c in (1, 2) else None)
    first = send(own, pair)
    second = send(own, middle)
    shards = {0: part}
    for k in range(2, dp, 2):
        shards[k] = send(part, make(lambda d, c: (d ^ k, c)))
    for k in range(0, dp, 2):
        shards[k + 1] = send(shards[k], make(lambda d, c: (d ^ 1, c)))
    shards = [shards[k] for k in range(dp)]
    third = send(first, middle)
    fourth = send(second, outward)
    fifth = send(third, outward)

    spec = {
        "shards": dp,
        "rows": rows,
        "cols": cols,
        "total": ctx,
        "me": lambda: lax.axis_index("ctx"),
        "owners": lambda: [lax.axis_index("dp") ^ k for k in range(dp)],
        "inner": lambda: jnp.logical_or(lax.axis_index("ctx") == 1, lax.axis_index("ctx") == 2),
    }

    def places():
        c = lax.axis_index("ctx")
        inner = jnp.logical_or(c == 1, c == 2)
        return [c, c ^ 1, c ^ jnp.where(inner, 3, 2), c ^ jnp.where(inner, 2, 3)]

    spec["places"] = places
    inner = spec["inner"]()
    third_block = jnp.where(inner, second, fourth)
    cosine, sine = tables(ctx * rows)
    gain = norm_gain[None, :]
    any_space = pl.BlockSpec(memory_space=pl.ANY)
    vmem = pl.BlockSpec(memory_space=pltpu.VMEM)
    n = 3
    early = pl.pallas_call(
        functools.partial(early_kernel, {**spec, "blocks": n}),
        out_shape=jax.ShapeDtypeStruct((n * rows, 3 * cols), jnp.bfloat16),
        in_specs=[any_space] * (n + dp) + [vmem] * 3,
        out_specs=vmem,
        scratch_shapes=[
            pltpu.VMEM((n * rows, features), jnp.bfloat16),
            pltpu.VMEM((n * rows, features), jnp.bfloat16),
            pltpu.VMEM((features, 3 * cols), jnp.bfloat16),
            pltpu.SemaphoreType.DMA((n,)),
            pltpu.SemaphoreType.DMA((dp,)),
        ],
        compiler_params=pltpu.CompilerParams(vmem_limit_bytes=VMEM_LIMIT),
        cost_estimate=pl.CostEstimate(
            flops=2 * n * rows * features * 3 * cols, bytes_accessed=10_000_000, transcendentals=0
        ),
        name="project_early",
    )(own, first, third_block, *shards, gain, cosine, sine)
    pieces = pl.pallas_call(
        functools.partial(late_kernel, {**spec, "blocks": n}),
        out_shape=[jax.ShapeDtypeStruct((rows, cols), jnp.bfloat16)] * ctx,
        in_specs=[any_space] * (2 + dp + 1) + [vmem] * 3,
        out_specs=[any_space] * ctx,
        scratch_shapes=[
            pltpu.VMEM((rows, features), jnp.bfloat16),
            pltpu.VMEM((rows, features), jnp.bfloat16),
            pltpu.VMEM((features, 3 * cols), jnp.bfloat16),
            pltpu.VMEM((ctx * rows, 3 * cols), jnp.bfloat16),
            pltpu.VMEM((ctx, rows, cols), jnp.bfloat16),
            pltpu.SemaphoreType.DMA((1,)),
            pltpu.SemaphoreType.DMA((dp,)),
            pltpu.SemaphoreType.DMA((n,)),
            pltpu.SemaphoreType.DMA((ctx,)),
        ],
        compiler_params=pltpu.CompilerParams(vmem_limit_bytes=VMEM_LIMIT),
        cost_estimate=pl.CostEstimate(
            flops=2 * rows * features * 3 * cols * 2, bytes_accessed=10_000_000, transcendentals=2_000_000
        ),
        name="attend",
    )(third, fifth, *shards, early, gain, cosine, sine)
    arrived = [pieces[0]]
    for k in range(1, ctx):
        arrived.append(send(pieces[k], make(lambda d, c: (d, c ^ k))))
    return pl.pallas_call(
        functools.partial(join_kernel, spec),
        out_shape=jax.ShapeDtypeStruct((1, rows, ctx * cols), jnp.bfloat16),
        in_specs=[any_space] * ctx,
        out_specs=any_space,
        scratch_shapes=[pltpu.SemaphoreType.DMA((ctx,))],
        compiler_params=pltpu.CompilerParams(vmem_limit_bytes=VMEM_LIMIT),
        name="join",
    )(*arrived)


def rotate(values, positions):
    heads = values.shape[1] // HEAD_DIM
    shaped = values.reshape(values.shape[0], heads, HEAD_DIM)
    freqs = 10000.0 ** (-(jnp.arange(HALF).astype(jnp.float32) * 2.0) / HEAD_DIM)
    angles = positions[:, None] * freqs[None, :]
    cosine = jnp.cos(angles)[:, None, :]
    sine = jnp.sin(angles)[:, None, :]
    first = shaped[:, :, :HALF]
    second = shaped[:, :, HALF:]
    return jnp.concatenate(
        [first * cosine - second * sine, second * cosine + first * sine], axis=2
    )


def general(dp, ctx, tokens, norm_gain, q_weight, k_weight, v_weight):
    rows = tokens.shape[1]
    heads = HEADS // ctx
    cols = heads * HEAD_DIM
    me = lax.axis_index("ctx")
    part = jnp.concatenate(
        [lax.dynamic_slice_in_dim(w, me * cols, cols, 1) for w in (q_weight, k_weight, v_weight)], axis=1
    )
    weights = lax.all_gather(part, "dp", axis=0, tiled=True)
    whole = lax.all_gather(tokens[0], "ctx", axis=0, tiled=True)
    normed = normalize(whole, norm_gain[None, :])
    linear = jnp.dot(normed, weights, preferred_element_type=jnp.float32)
    length = ctx * rows
    positions = jnp.arange(length).astype(jnp.float32)
    q = rotate(linear[:, :cols], positions).astype(jnp.bfloat16)
    k = rotate(linear[:, cols : 2 * cols], positions).astype(jnp.bfloat16)
    v = linear[:, 2 * cols :].astype(jnp.bfloat16).reshape(length, heads, HEAD_DIM)
    allowed = jnp.arange(length)[None, :] <= jnp.arange(length)[:, None]
    scores = jnp.einsum("qhd,khd->hqk", q, k, preferred_element_type=jnp.float32) * HEAD_DIM ** (-0.5)
    scores = jnp.where(allowed[None], scores, -1e30)
    top = jnp.max(scores, axis=2, keepdims=True)
    expo = jnp.where(allowed[None], jnp.exp(scores - top), 0.0)
    numer = jnp.einsum("hqk,khd->hqd", expo.astype(jnp.bfloat16), v, preferred_element_type=jnp.float32)
    result = (numer / jnp.sum(expo, axis=2, keepdims=True)).astype(jnp.bfloat16)
    result = result.reshape(heads, ctx, rows, HEAD_DIM).transpose(1, 2, 0, 3).reshape(ctx, rows, cols)
    back = lax.all_to_all(result, "ctx", 0, 0)
    return back.transpose(1, 0, 2).reshape(1, rows, ctx * cols)


def solution(mesh):
    dp, ctx = mesh.shape["dp"], mesh.shape["ctx"]
    body = fast if (dp, ctx) == (8, 4) else general
    placed = (P("dp", "ctx", None), P(), P("dp", None), P("dp", None), P("dp", None))
    return jax.shard_map(
        functools.partial(body, dp, ctx),
        mesh=mesh,
        in_specs=placed,
        out_specs=P("dp", "ctx", None),
        check_vma=False,
    )
```

time: 348 us -> 158 us (0.45)
  waiting for transfers between devices: 272 us -> 73.4 us
  Pallas kernels: 0 us -> 55.4 us
  matrix products: 23.5 us -> 0 us
  local copies, waits for them, and re-layouts: 26.8 us -> 3.42 us
  starting transfers between devices: 0.16 us -> 18.7 us
  between operations: 13.8 us -> 0.33 us
  other arithmetic: 10.3 us -> 5.17 us
    all_gather x5 -> x0, waiting for transfers between devices: 270 us -> none  [the longest x1 72.2 us: shards(): value_block = lax.all_gather(values, 'ctx', axis=0, tiled=True)]
    ppermute x0 -> x15, waiting for transfers between devices: none -> 73.4 us  [fast(): send = lambda value, perm: lax.ppermute(value, axes, perm)]
    pallas_call x0 -> x3, Pallas kernels: none -> 55.4 us  [the longest x1 28.9 us: fast(): pl.pallas_call(functools.partial(join_kernel, spec), out_shape=jax.ShapeD...]
    dot_general x2 -> x0, local copies, waits for them, and re-layouts: 24.7 us -> none  [shards(): jnp.dot(normed, piece, preferred_element_type=jnp.float32)]
    dot_general x5 -> x0, matrix products: 23.5 us -> none  [the longest x3 14.6 us: shards(): jnp.dot(normed, piece, preferred_element_type=jnp.float32)]
    ppermute x0 -> x15, starting transfers between devices: none -> 18.7 us  [fast(): send = lambda value, perm: lax.ppermute(value, axes, perm)]
    reduce_sum x2 -> x0, other arithmetic: 4.58 us -> none  [the longest x1 4.32 us: work(): total = jnp.sum(expo, axis=2)]
  transfers between devices with their start and end apart: 5 -> 15, of which waited for: 5 -> 7; matrix products, arithmetic and copies ran while one was open for 13% -> 4% of each run, Pallas kernels for 0% -> 7%
where the time goes in v1:
time: 158 us; the launch traced here: 156 us
  waiting for transfers between devices  73.4 us (46%)
  Pallas kernels  55.4 us (35%)
  starting transfers between devices  18.7 us (12%)
  other arithmetic  5.17 us (3%)
  local copies, waits for them, and re-layouts  3.42 us (2%)
    ppermute x15, waiting for transfers between devices, fast(): send = lambda value, perm: lax.ppermute(value, axes, perm)  73.4 us
    pallas_call x1, Pallas kernels, fast(): pl.pallas_call(functools.partial(join_kernel, spec), out_shape=jax.ShapeD...  28.9 us
    ppermute x15, starting transfers between devices, fast(): send = lambda value, perm: lax.ppermute(value, axes, perm)  18.7 us
    pallas_call x1, Pallas kernels, fast(): pl.pallas_call(functools.partial(late_kernel, {**spec, 'blocks': n}), out...  15.8 us
    pallas_call x1, Pallas kernels, fast(): pl.pallas_call(functools.partial(early_kernel, {**spec, 'blocks': n}), ou...  10.6 us
  transfers between devices with their start and end apart: 15, of which 7 were waited for; matrix products, arithmetic and copies ran while one was open for 4% of the time, Pallas kernels for 7%

profile of v1, /device:TPU:0, one launch (start us, length us, event | category | flops | bytes accessed | tf_op | source)
XLA Modules:
  0.0 156.4 jit_solution(11146256034019477890)
XLA Ops:
  0.0 0.0 copy-start
  0.0 1.7 %collective-permute-start.10 = (bf16[224,2048]{1,0:T(8,128)(2,1)}, bf16[224,2048]{1,0:T(8,128)(2,1)}, u32[]{:S(2)}, u32[]{:S(2)}) collective-permute-start(bf16[224,2048]{1,0:T(8,128)(2,1)} %bitcast.1), channel_id=1, source_target_pairs={{1,2},{2,1},{5,6},{6,5},{9,10},{10,9},{13,14},{14,13},{17,18},{18,... | collective-permute-start | bytes 2752520 | tf_op jit(solution)/shard_map/ppermute | solution.py:200
  1.7 5.0 %collective-permute-start = (bf16[224,2048]{1,0:T(8,128)(2,1)}, bf16[224,2048]{1,0:T(8,128)(2,1)}, u32[]{:S(2)}, u32[]{:S(2)}) collective-permute-start(bf16[224,2048]{1,0:T(8,128)(2,1)} %bitcast.2), channel_id=1, source_target_pairs={{0,1},{1,0},{2,3},{3,2},{4,5},{5,4},{6,7},{7,6},{8,9},{9,8},{10,11... | collective-permute-start | bytes 2752520 | tf_op jit(solution)/shard_map/ppermute | solution.py:200
  6.7 0.0 copy-done
  6.7 1.1 constant_dynamic-slice_fusion
  7.8 0.0 collective-permute-done.10
  7.8 1.3 collective-permute-start.11
  9.1 0.1 pad_maximum_fusion.refs_3_.refs_2_
  9.2 1.6 collective-permute-start.4
  10.7 1.5 collective-permute-start.6
  12.3 0.5 collective-permute-start.8
  12.7 14.3 %collective-permute-done.refs_1_ = bf16[224,2048]{1,0:T(8,128)(2,1)} collective-permute-done((bf16[224,2048]{1,0:T(8,128)(2,1)}, bf16[224,2048]{1,0:T(8,128)(2,1)}, u32[]{:S(2)}, u32[]{:S(2)}) %collective-permute-start) | collective-permute-done | bytes 917536 | tf_op jit(solution)/shard_map/ppermute | solution.py:200
  27.1 0.7 collective-permute-start.1
  27.8 0.0 copy-start.8
  27.8 1.9 %collective-permute-done.4.refs_5_.refs_4_ = bf16[256,1536]{1,0:T(8,128)(2,1)S(1)} collective-permute-done((bf16[256,1536]{1,0:T(8,128)(2,1)S(1)}, bf16[256,1536]{1,0:T(8,128)(2,1)S(1)}, u32[]{:S(2)}, u32[]{:S(2)}) %collective-permute-start.4) | collective-permute-done | bytes 786464 | tf_op jit(solution)/shard_map/ppermute | solution.py:200
  29.7 0.0 collective-permute-start.3
  29.7 16.4 %collective-permute-done.6.refs_7_.refs_6_ = bf16[256,1536]{1,0:T(8,128)(2,1)} collective-permute-done((bf16[256,1536]{1,0:T(8,128)(2,1)S(1)}, bf16[256,1536]{1,0:T(8,128)(2,1)}, u32[]{:S(2)}, u32[]{:S(2)}) %collective-permute-start.6) | collective-permute-done | bytes 786464 | tf_op jit(solution)/shard_map/ppermute | solution.py:200
  46.1 0.0 collective-permute-start.5
  46.2 0.0 collective-permute-done.8.refs_9_.refs_8_
  46.2 0.5 collective-permute-start.7
  46.7 1.7 %collective-permute-done.11 = bf16[224,2048]{1,0:T(8,128)(2,1)S(1)} collective-permute-done((bf16[224,2048]{1,0:T(8,128)(2,1)}, bf16[224,2048]{1,0:T(8,128)(2,1)S(1)}, u32[]{:S(2)}, u32[]{:S(2)}) %collective-permute-start.11) | collective-permute-done | bytes 917536 | tf_op jit(solution)/shard_map/ppermute | solution.py:200
  48.4 0.9 copy-done.3
  49.4 0.0 collective-permute-start.9
  49.4 1.7 %fusion = (f32[896,64]{1,0:T(8,128)S(1)}, f32[896,64]{1,0:T(8,128)S(1)}, f32[896,64]{1,0:T(8,128)S(1)}) fusion(f32[64]{0:T(128)S(1)} %multiply_power_fusion, f32[896]{0:T(1024)S(1)} %iota_convert_fusion), kind=kLoop, calls=%fused_computation.6 | loop fusion | flops 114688 | bytes 691968 | tf_op jit(solution)/shard_map/neg | solution.py:25
  51.0 0.0 collective-permute-done.1.refs_0_
  51.0 0.0 copy-start.2
  51.1 1.5 collective-permute-start.2
  52.5 1.2 pad_maximum_fusion.1
  53.8 0.0 copy-done.8
  53.8 0.6 broadcast_in_dim.2.refs_11_
  54.4 2.2 %broadcast_select_fusion.refs_2_ = bf16[224,2048]{1,0:T(8,128)(2,1)} fusion(bf16[224,2048]{1,0:T(8,128)(2,1)} %collective-permute-done.10, bf16[224,2048]{1,0:T(8,128)(2,1)} %copy-done.3, pred[]{:T(512)S(6)} %or.3), kind=kLoop, calls=%fused_computation | loop fusion | flops 458752 | bytes 2752513 | tf_op jit(solution)/shard_map/jit(_where)/select_n | solution.py:238
  56.6 0.0 collective-permute-done.3.refs_4_.refs_3_
  56.6 0.0 collective-permute-done.5.refs_6_.refs_5_
  56.6 0.0 collective-permute-done.7.refs_8_.refs_7_
  56.6 0.0 collective-permute-done.9.refs_10_.refs_9_
  56.6 0.0 copy-done.4
  56.6 10.6 %project_early.1.refs_10_ = bf16[672,1536]{1,0:T(8,128)(2,1)} custom-call(bf16[224,2048]{1,0:T(8,128)(2,1)} %bitcast.3, bf16[224,2048]{1,0:T(8,128)(2,1)} %collective-permute-done.refs_1_, bf16[224,2048]{1,0:T(8,128)(2,1)} %broadcast_select_fusion.refs_2_, bf16[256,1536]{1,0:T(8,128)(2,1)} %copy-done.1, ...), custom_call_target="tpu_custom_call" | custom-call | flops 4227858432 | bytes 10000000 | tf_op jit(solution)/shard_map/project_early/pallas_call | solution.py:244
  67.3 23.8 %collective-permute-done.2.refs_1_ = bf16[224,2048]{1,0:T(8,128)(2,1)} collective-permute-done((bf16[224,2048]{1,0:T(8,128)(2,1)S(1)}, bf16[224,2048]{1,0:T(8,128)(2,1)}, u32[]{:S(2)}, u32[]{:S(2)}) %collective-permute-start.2) | collective-permute-done | bytes 917536 | tf_op jit(solution)/shard_map/ppermute | solution.py:200
  91.1 15.8 %attend.1 = (bf16[224,512]{1,0:T(8,128)(2,1)}, bf16[224,512]{1,0:T(8,128)(2,1)}, bf16[224,512]{1,0:T(8,128)(2,1)}, bf16[224,512]{1,0:T(8,128)(2,1)}) custom-call(bf16[224,2048]{1,0:T(8,128)(2,1)} %copy-done.2, bf16[224,2048]{1,0:T(8,128)(2,1)} %collective-permute-done.2.refs_1_, bf16[256,1536]{1,0:T(8,128)(2,1)} %copy-done.1, ...), custom_call_target="tpu_custom_call" | custom-call | flops 2818572288 | bytes 10000000 | tf_op jit(solution)/shard_map/attend/pallas_call | solution.py:262
  106.9 0.1 collective-permute-start.12
  107.0 3.0 %collective-permute-start.13 = (bf16[224,512]{1,0:T(8,128)(2,1)}, bf16[224,512]{1,0:T(8,128)(2,1)S(1)}, u32[]{:S(2)}, u32[]{:S(2)}) collective-permute-start(bf16[224,512]{1,0:T(8,128)(2,1)} %get-tuple-element.11), channel_id=1, source_target_pairs={{0,2},{1,3},{2,0},{3,1},{4,6},{5,7},{6,4},{7,5},{8,10},{9,11},{10,... | collective-permute-start | bytes 688136 | tf_op jit(solution)/shard_map/ppermute | solution.py:200
  110.0 1.3 collective-permute-start.14
  111.4 7.6 %collective-permute-done.12.refs_1_ = bf16[224,512]{1,0:T(8,128)(2,1)S(1)} collective-permute-done((bf16[224,512]{1,0:T(8,128)(2,1)}, bf16[224,512]{1,0:T(8,128)(2,1)S(1)}, u32[]{:S(2)}, u32[]{:S(2)}) %collective-permute-start.12) | collective-permute-done | bytes 229408 | tf_op jit(solution)/shard_map/ppermute | solution.py:200
  118.9 7.6 %collective-permute-done.13.refs_2_ = bf16[224,512]{1,0:T(8,128)(2,1)S(1)} collective-permute-done((bf16[224,512]{1,0:T(8,128)(2,1)}, bf16[224,512]{1,0:T(8,128)(2,1)S(1)}, u32[]{:S(2)}, u32[]{:S(2)}) %collective-permute-start.13) | collective-permute-done | bytes 229408 | tf_op jit(solution)/shard_map/ppermute | solution.py:200
  126.5 0.0 collective-permute-done.14.refs_3_
  126.5 0.7 copy-done.6
  127.2 0.1 copy-done.7
  127.3 28.9 %join.1 = bf16[1,224,2048]{2,1,0:T(8,128)(2,1)} custom-call(bf16[224,512]{1,0:T(8,128)(2,1)} %get-tuple-element.9.refs_0_, bf16[224,512]{1,0:T(8,128)(2,1)} %copy-done.5, bf16[224,512]{1,0:T(8,128)(2,1)} %copy-done.6, bf16[224,512]{1,0:T(8,128)(2,1)} %copy-done.7), custom_call_target="tpu_custom_call" | custom-call | tf_op jit(solution)/shard_map/join/pallas_call | solution.py:287
  (12 shorter events, 0.0 us)
Async XLA Ops:
  0.0 6.7 %copy-start = (bf16[256,2048]{1,0:T(8,128)(2,1)S(1)}, bf16[256,2048]{1,0:T(8,128)(2,1)}, u32[]{:S(2)}) copy-start(bf16[256,2048]{1,0:T(8,128)(2,1)} %param.7) | copy-start | bytes 3145732
  0.0 7.8 %collective-permute-start.10 = (bf16[224,2048]{1,0:T(8,128)(2,1)}, bf16[224,2048]{1,0:T(8,128)(2,1)}, u32[]{:S(2)}, u32[]{:S(2)}) collective-permute-start(bf16[224,2048]{1,0:T(8,128)(2,1)} %bitcast.1), channel_id=1, source_target_pairs={{1,2},{2,1},{5,6},{6,5},{9,10},{10,9},{13,14},{14,13},{17,18},{18,... | collective-permute-start | bytes 2752520 | tf_op jit(solution)/shard_map/ppermute | solution.py:200
  1.7 25.4 %collective-permute-start = (bf16[224,2048]{1,0:T(8,128)(2,1)}, bf16[224,2048]{1,0:T(8,128)(2,1)}, u32[]{:S(2)}, u32[]{:S(2)}) collective-permute-start(bf16[224,2048]{1,0:T(8,128)(2,1)} %bitcast.2), channel_id=1, source_target_pairs={{0,1},{1,0},{2,3},{3,2},{4,5},{5,4},{6,7},{7,6},{8,9},{9,8},{10,11... | collective-permute-start | bytes 2752520 | tf_op jit(solution)/shard_map/ppermute | solution.py:200
  7.8 40.6 %collective-permute-start.11 = (bf16[224,2048]{1,0:T(8,128)(2,1)}, bf16[224,2048]{1,0:T(8,128)(2,1)S(1)}, u32[]{:S(2)}, u32[]{:S(2)}) collective-permute-start(bf16[224,2048]{1,0:T(8,128)(2,1)} %collective-permute-done.10), channel_id=1, source_target_pairs={{1,0},{2,3},{5,4},{6,7},{9,8},{10,11},{13,12},{14,15},{17,16},{18,... | collective-permute-start | bytes 2752520 | tf_op jit(solution)/shard_map/ppermute | solution.py:200
  9.2 44.6 %copy-start.1 = (bf16[256,1536]{1,0:T(8,128)(2,1)}, bf16[256,1536]{1,0:T(8,128)(2,1)S(1)}, u32[]{:S(2)}) copy-start(bf16[256,1536]{1,0:T(8,128)(2,1)S(1)} %pad_maximum_fusion.refs_3_.refs_2_) | copy-start | bytes 2359300
  9.2 20.5 %collective-permute-start.4 = (bf16[256,1536]{1,0:T(8,128)(2,1)S(1)}, bf16[256,1536]{1,0:T(8,128)(2,1)S(1)}, u32[]{:S(2)}, u32[]{:S(2)}) collective-permute-start(bf16[256,1536]{1,0:T(8,128)(2,1)S(1)} %pad_maximum_fusion.refs_3_.refs_2_), channel_id=1, source_target_pairs={{0,8},{1,9},{2,10},{3,11},{4,12},{5,13},{6,14},{7,15},{8,0},{9,1},... | collective-permute-start | bytes 2359304 | tf_op jit(solution)/shard_map/ppermute | solution.py:200
  10.7 35.4 %collective-permute-start.6 = (bf16[256,1536]{1,0:T(8,128)(2,1)S(1)}, bf16[256,1536]{1,0:T(8,128)(2,1)}, u32[]{:S(2)}, u32[]{:S(2)}) collective-permute-start(bf16[256,1536]{1,0:T(8,128)(2,1)S(1)} %pad_maximum_fusion.refs_3_.refs_2_), channel_id=1, source_target_pairs={{0,16},{1,17},{2,18},{3,19},{4,20},{5,21},{6,22},{7,23},{8,24},{9,... | collective-permute-start | bytes 2359304 | tf_op jit(solution)/shard_map/ppermute | solution.py:200
  12.3 33.9 %collective-permute-start.8 = (bf16[256,1536]{1,0:T(8,128)(2,1)S(1)}, bf16[256,1536]{1,0:T(8,128)(2,1)}, u32[]{:S(2)}, u32[]{:S(2)}) collective-permute-start(bf16[256,1536]{1,0:T(8,128)(2,1)S(1)} %pad_maximum_fusion.refs_3_.refs_2_), channel_id=1, source_target_pairs={{0,24},{1,25},{2,26},{3,27},{4,28},{5,29},{6,30},{7,31},{8,16},{9,... | collective-permute-start | bytes 2359304 | tf_op jit(solution)/shard_map/ppermute | solution.py:200
  27.1 23.9 %collective-permute-start.1 = (bf16[224,2048]{1,0:T(8,128)(2,1)}, bf16[224,2048]{1,0:T(8,128)(2,1)S(1)}, u32[]{:S(2)}, u32[]{:S(2)}) collective-permute-start(bf16[224,2048]{1,0:T(8,128)(2,1)} %collective-permute-done.refs_1_), channel_id=1, source_target_pairs={{1,2},{2,1},{5,6},{6,5},{9,10},{10,9},{13,14},{14,13},{17,18},{18,... | collective-permute-start | bytes 2752520 | tf_op jit(solution)/shard_map/ppermute | solution.py:200
  27.8 25.9 %copy-start.8 = (bf16[2048]{0:T(1024)(128)(2,1)S(1)}, bf16[2048]{0:T(1024)(128)(2,1)}, u32[]{:S(2)}) copy-start(bf16[2048]{0:T(1024)(128)(2,1)} %param.6) | copy-start | bytes 12292
  29.7 26.9 %copy-start.4 = (bf16[256,1536]{1,0:T(8,128)(2,1)}, bf16[256,1536]{1,0:T(8,128)(2,1)S(1)}, u32[]{:S(2)}) copy-start(bf16[256,1536]{1,0:T(8,128)(2,1)S(1)} %collective-permute-done.4.refs_5_.refs_4_) | copy-start | bytes 2359300
  29.7 26.8 %collective-permute-start.3 = (bf16[256,1536]{1,0:T(8,128)(2,1)S(1)}, bf16[256,1536]{1,0:T(8,128)(2,1)}, u32[]{:S(2)}, u32[]{:S(2)}) collective-permute-start(bf16[256,1536]{1,0:T(8,128)(2,1)S(1)} %pad_maximum_fusion.refs_3_.refs_2_), channel_id=1, source_target_pairs={{0,4},{1,5},{2,6},{3,7},{4,0},{5,1},{6,2},{7,3},{8,12},{9,13},{10,... | collective-permute-start | bytes 2359304 | tf_op jit(solution)/shard_map/ppermute | solution.py:200
  46.1 10.4 %collective-permute-start.5 = (bf16[256,1536]{1,0:T(8,128)(2,1)S(1)}, bf16[256,1536]{1,0:T(8,128)(2,1)}, u32[]{:S(2)}, u32[]{:S(2)}) collective-permute-start(bf16[256,1536]{1,0:T(8,128)(2,1)S(1)} %collective-permute-done.4.refs_5_.refs_4_), channel_id=1, source_target_pairs={{0,4},{1,5},{2,6},{3,7},{4,0},{5,1},{6,2},{7,3},{8,12},{9,13},{10,... | collective-permute-start | bytes 2359304 | tf_op jit(solution)/shard_map/ppermute | solution.py:200
  46.2 10.4 %collective-permute-start.7 = (bf16[256,1536]{1,0:T(8,128)(2,1)}, bf16[256,1536]{1,0:T(8,128)(2,1)}, u32[]{:S(2)}, u32[]{:S(2)}) collective-permute-start(bf16[256,1536]{1,0:T(8,128)(2,1)} %collective-permute-done.6.refs_7_.refs_6_), channel_id=1, source_target_pairs={{0,4},{1,5},{2,6},{3,7},{4,0},{5,1},{6,2},{7,3},{8,12},{9,13},{10,... | collective-permute-start | bytes 2359304 | tf_op jit(solution)/shard_map/ppermute | solution.py:200
  48.4 0.9 copy-start.3
  49.4 7.3 %collective-permute-start.9 = (bf16[256,1536]{1,0:T(8,128)(2,1)}, bf16[256,1536]{1,0:T(8,128)(2,1)}, u32[]{:S(2)}, u32[]{:S(2)}) collective-permute-start(bf16[256,1536]{1,0:T(8,128)(2,1)} %collective-permute-done.8.refs_9_.refs_8_), channel_id=1, source_target_pairs={{0,4},{1,5},{2,6},{3,7},{4,0},{5,1},{6,2},{7,3},{8,12},{9,13},{10,... | collective-permute-start | bytes 2359304 | tf_op jit(solution)/shard_map/ppermute | solution.py:200
  51.0 5.5 %copy-start.2 = (bf16[224,2048]{1,0:T(8,128)(2,1)}, bf16[224,2048]{1,0:T(8,128)(2,1)S(1)}, u32[]{:S(2)}) copy-start(bf16[224,2048]{1,0:T(8,128)(2,1)S(1)} %collective-permute-done.1.refs_0_) | copy-start | bytes 2752516
  51.1 40.0 %collective-permute-start.2 = (bf16[224,2048]{1,0:T(8,128)(2,1)S(1)}, bf16[224,2048]{1,0:T(8,128)(2,1)}, u32[]{:S(2)}, u32[]{:S(2)}) collective-permute-start(bf16[224,2048]{1,0:T(8,128)(2,1)S(1)} %collective-permute-done.1.refs_0_), channel_id=1, source_target_pairs={{1,0},{2,3},{5,4},{6,7},{9,8},{10,11},{13,12},{14,15},{17,16},{18,... | collective-permute-start | bytes 2752520 | tf_op jit(solution)/shard_map/ppermute | solution.py:200
  106.9 12.0 %collective-permute-start.12 = (bf16[224,512]{1,0:T(8,128)(2,1)}, bf16[224,512]{1,0:T(8,128)(2,1)S(1)}, u32[]{:S(2)}, u32[]{:S(2)}) collective-permute-start(bf16[224,512]{1,0:T(8,128)(2,1)} %get-tuple-element.10), channel_id=1, source_target_pairs={{0,1},{1,0},{2,3},{3,2},{4,5},{5,4},{6,7},{7,6},{8,9},{9,8},{10,11... | collective-permute-start | bytes 688136 | tf_op jit(solution)/shard_map/ppermute | solution.py:200
  107.0 19.5 %collective-permute-start.13 = (bf16[224,512]{1,0:T(8,128)(2,1)}, bf16[224,512]{1,0:T(8,128)(2,1)S(1)}, u32[]{:S(2)}, u32[]{:S(2)}) collective-permute-start(bf16[224,512]{1,0:T(8,128)(2,1)} %get-tuple-element.11), channel_id=1, source_target_pairs={{0,2},{1,3},{2,0},{3,1},{4,6},{5,7},{6,4},{7,5},{8,10},{9,11},{10,... | collective-permute-start | bytes 688136 | tf_op jit(solution)/shard_map/ppermute | solution.py:200
  110.0 16.5 %collective-permute-start.14 = (bf16[224,512]{1,0:T(8,128)(2,1)}, bf16[224,512]{1,0:T(8,128)(2,1)S(1)}, u32[]{:S(2)}, u32[]{:S(2)}) collective-permute-start(bf16[224,512]{1,0:T(8,128)(2,1)} %get-tuple-element.12), channel_id=1, source_target_pairs={{0,3},{1,2},{2,1},{3,0},{4,7},{5,6},{6,5},{7,4},{8,11},{9,10},{10,... | collective-permute-start | bytes 688136 | tf_op jit(solution)/shard_map/ppermute | solution.py:200
  118.9 7.6 %copy-start.5 = (bf16[224,512]{1,0:T(8,128)(2,1)}, bf16[224,512]{1,0:T(8,128)(2,1)S(1)}, u32[]{:S(2)}) copy-start(bf16[224,512]{1,0:T(8,128)(2,1)S(1)} %collective-permute-done.12.refs_1_) | copy-start | bytes 688132
  126.5 0.7 copy-start.6
  126.5 0.8 copy-start.7

commit v2 on v1

--- a/solution.py
+++ b/solution.py
@@ -12,7 +12,7 @@
 HEAD_DIM = 128
 HALF = HEAD_DIM // 2
 EPS = 1e-05
-VMEM_LIMIT = 56 * 1024 * 1024
+VMEM_LIMIT = 28 * 1024 * 1024
 
 
 def tables(length):
@@ -64,16 +64,24 @@
 
 def early_kernel(spec, *refs):
     n, m, rows, cols = spec["blocks"], spec["shards"], spec["rows"], spec["cols"]
-    tokens, shards = refs[:n], refs[n : n + m]
-    gain, cos_ref, sin_ref, out, held, normed, weights, token_sems, weight_sems = refs[n + m :]
+    tokens, shards = refs[: n + 1], refs[n + 1 : n + 1 + m]
+    gain, cos_ref, sin_ref, out, held, normed, weights, token_sems, weight_sems = refs[n + 1 + m :]
     place, owners = spec["places"](), spec["owners"]()
+    inner = spec["inner"]()
     loads = []
     for i in range(n):
         load = pltpu.make_async_copy(
             tokens[i], held.at[pl.ds(i * rows, rows)], token_sems.at[i]
         )
-        load.start()
         loads.append(load)
+        if i < n - 1:
+            load.start()
+        else:
+            pl.when(inner)(load.start)
+            other = pltpu.make_async_copy(
+                tokens[n], held.at[pl.ds(i * rows, rows)], token_sems.at[i]
+            )
+            pl.when(jnp.logical_not(inner))(other.start)
     weight_loads = start_weights(owners, shards, weights, weight_sems)
     for i in range(n):
         loads[i].wait()
@@ -145,41 +153,40 @@
     below = lax.broadcasted_iota(jnp.int32, (rows, rows), 0) >= lax.broadcasted_iota(
         jnp.int32, (rows, rows), 1
     )
-    for head in range(cols // HEAD_DIM):
-        for block in range(total):
-            size = (block + 1) * rows
-            q = qkv[block * rows : size, head * HEAD_DIM : (head + 1) * HEAD_DIM]
-            k = qkv[0:size, cols + head * HEAD_DIM : cols + (head + 1) * HEAD_DIM]
-            v = qkv[0:size, 2 * cols + head * HEAD_DIM : 2 * cols + (head + 1) * HEAD_DIM]
-            scores = lax.dot_general(
-                q, k, (((1,), (1,)), ((), ())), preferred_element_type=jnp.float32
-            )
-            own = jnp.where(below, scores[:, block * rows :], -1e30)
-            scores = jnp.concatenate([scores[:, : block * rows], own], axis=1) if block else own
-            top = jnp.max(scores, axis=1, keepdims=True)
-            expo = jnp.exp2((scores - top) * factor)
+
+    def scored(q, k):
+        return lax.dot_general(q, k, (((1,), (1,)), ((), ())), preferred_element_type=jnp.float32)
+
+    for block in range(total):
+        own, past = slice(block * rows, (block + 1) * rows), slice(0, block * rows)
+        for head in range(cols // HEAD_DIM):
+            lane = slice(head * HEAD_DIM, (head + 1) * HEAD_DIM)
+            k_lane = slice(cols + lane.start, cols + lane.stop)
+            v_lane = slice(2 * cols + lane.start, 2 * cols + lane.stop)
+            q = qkv[own, lane]
+            near = jnp.where(below, scored(q, qkv[own, k_lane]), -1e30)
+            top = jnp.max(near, axis=1, keepdims=True)
+            if block:
+                far = scored(q, qkv[past, k_lane])
+                top = jnp.maximum(top, jnp.max(far, axis=1, keepdims=True))
+            top = top * factor
+            expo = jnp.exp2(near * factor - top)
             bottom = jnp.sum(expo, axis=1, keepdims=True)
-            numer = jnp.dot(expo.astype(jnp.bfloat16), v, preferred_element_type=jnp.float32)
-            result[block ^ me, :, head * HEAD_DIM : (head + 1) * HEAD_DIM] = (
-                numer / bottom
-            ).astype(jnp.bfloat16)
+            numer = jnp.dot(expo.astype(jnp.bfloat16), qkv[own, v_lane], preferred_element_type=jnp.float32)
+            if block:
+                expo = jnp.exp2(far * factor - top)
+                bottom += jnp.sum(expo, axis=1, keepdims=True)
+                numer += jnp.dot(
+                    expo.astype(jnp.bfloat16), qkv[past, v_lane], preferred_element_type=jnp.float32
+                )
+            result[block ^ me, :, lane] = (numer / bottom).astype(jnp.bfloat16)
 
 
 def join_kernel(spec, *refs):
     total, cols = spec["total"], spec["cols"]
-    pieces, out, sems = refs[:total], refs[total], refs[total + 1]
     me = spec["me"]()
-    copies = []
     for k in range(total):
-        copy = pltpu.make_async_copy(
-            pieces[k],
-            out.at[0, :, pl.ds(pl.multiple_of((me ^ k) * cols, cols), cols)],
-            sems.at[k],
-        )
-        copy.start()
-        copies.append(copy)
-    for copy in copies:
-        copy.wait()
+        refs[total][0, :, pl.ds(pl.multiple_of((me ^ k) * cols, cols), cols)] = refs[k][...]
 
 
 def block_plan(dp, ctx):
@@ -208,6 +215,8 @@
     outward = make(lambda d, c: (d, {1: 0, 2: 3}[c]) if c in (1, 2) else None)
     first = send(own, pair)
     second = send(own, middle)
+    cosine, sine = tables(ctx * rows)
+    first, cosine, sine = lax.optimization_barrier((first, cosine, sine))
     shards = {0: part}
     for k in range(2, dp, 2):
         shards[k] = send(part, make(lambda d, c: (d ^ k, c)))
@@ -234,9 +243,6 @@
         return [c, c ^ 1, c ^ jnp.where(inner, 3, 2), c ^ jnp.where(inner, 2, 3)]
 
     spec["places"] = places
-    inner = spec["inner"]()
-    third_block = jnp.where(inner, second, fourth)
-    cosine, sine = tables(ctx * rows)
     gain = norm_gain[None, :]
     any_space = pl.BlockSpec(memory_space=pl.ANY)
     vmem = pl.BlockSpec(memory_space=pltpu.VMEM)
@@ -244,7 +250,7 @@
     early = pl.pallas_call(
         functools.partial(early_kernel, {**spec, "blocks": n}),
         out_shape=jax.ShapeDtypeStruct((n * rows, 3 * cols), jnp.bfloat16),
-        in_specs=[any_space] * (n + dp) + [vmem] * 3,
+        in_specs=[any_space] * (n + 1 + dp) + [vmem] * 3,
         out_specs=vmem,
         scratch_shapes=[
             pltpu.VMEM((n * rows, features), jnp.bfloat16),
@@ -258,7 +264,7 @@
             flops=2 * n * rows * features * 3 * cols, bytes_accessed=10_000_000, transcendentals=0
         ),
         name="project_early",
-    )(own, first, third_block, *shards, gain, cosine, sine)
+    )(own, first, second, fourth, *shards, gain, cosine, sine)
     pieces = pl.pallas_call(
         functools.partial(late_kernel, {**spec, "blocks": n}),
         out_shape=[jax.ShapeDtypeStruct((rows, cols), jnp.bfloat16)] * ctx,
@@ -287,10 +293,9 @@
     return pl.pallas_call(
         functools.partial(join_kernel, spec),
         out_shape=jax.ShapeDtypeStruct((1, rows, ctx * cols), jnp.bfloat16),
-        in_specs=[any_space] * ctx,
-        out_specs=any_space,
-        scratch_shapes=[pltpu.SemaphoreType.DMA((ctx,))],
-        compiler_params=pltpu.CompilerParams(vmem_limit_bytes=VMEM_LIMIT),
+        in_specs=[vmem] * ctx,
+        out_specs=vmem,
+        compiler_params=pltpu.CompilerParams(vmem_limit_bytes=8 * 1024 * 1024),
         name="join",
     )(*arrived)
 

time: 158 us -> 102 us (0.65); the launches traced: 156 us -> 102 us
  Pallas kernels: 55.4 us -> 17.7 us
  waiting for transfers between devices: 73.4 us -> 65.4 us
  starting transfers between devices: 18.7 us -> 15.5 us
  other arithmetic: 5.17 us -> 2.04 us
  local copies, waits for them, and re-layouts: 3.42 us -> 1.2 us
    pallas_call x1, Pallas kernels: 28.9 us -> 1 us  [fast(): pl.pallas_call(functools.partial(join_kernel, spec), out_shape=jax.ShapeD...]
    ppermute x15, waiting for transfers between devices: 73.4 us -> 65.4 us  [fast(): send = lambda value, perm: lax.ppermute(value, axes, perm)]
    pallas_call x1, Pallas kernels: 15.8 us -> 9.98 us  [fast(): pl.pallas_call(functools.partial(late_kernel, {**spec, 'blocks': n}), out...]
    pallas_call x1, Pallas kernels: 10.6 us -> 6.73 us  [fast(): pl.pallas_call(functools.partial(early_kernel, {**spec, 'blocks': n}), ou...]
    ppermute x15, starting transfers between devices: 18.7 us -> 15.5 us  [fast(): send = lambda value, perm: lax.ppermute(value, axes, perm)]
    select_n x1 -> x0, other arithmetic: 2.2 us -> none  [fast(): third_block = jnp.where(inner, second, fourth)]
    unnamed x18 -> x6, local copies, waits for them, and re-layouts: 1.73 us -> 0.01 us
  transfers between devices with their start and end apart: 15 -> 15, of which waited for: 7 -> 11; matrix products, arithmetic and copies ran while one was open for 4% -> 3% of each run, Pallas kernels for 7% -> 7%
where the time goes in v2:
time: 102 us
  waiting for transfers between devices  65.4 us (64%)
  Pallas kernels  17.7 us (17%)
  starting transfers between devices  15.5 us (15%)
  other arithmetic  2.04 us (2%)
  local copies, waits for them, and re-layouts  1.2 us (1%)
    ppermute x15, waiting for transfers between devices, fast(): send = lambda value, perm: lax.ppermute(value, axes, perm)  65.4 us
    ppermute x15, starting transfers between devices, fast(): send = lambda value, perm: lax.ppermute(value, axes, perm)  15.5 us
    pallas_call x1, Pallas kernels, fast(): pl.pallas_call(functools.partial(late_kernel, {**spec, 'blocks': n}), out...  9.98 us
    pallas_call x1, Pallas kernels, fast(): pl.pallas_call(functools.partial(early_kernel, {**spec, 'blocks': n}), ou...  6.73 us
  transfers between devices with their start and end apart: 15, of which 11 were waited for; matrix products, arithmetic and copies ran while one was open for 3% of the time, Pallas kernels for 7%

profile of v2, /device:TPU:0, one launch (start us, length us, event | category | flops | bytes accessed | tf_op | source)
XLA Modules:
  0.0 102.1 jit_solution(4490033713699662166)
XLA Ops:
  0.0 0.0 copy-start
  0.0 3.0 %collective-permute-start = (bf16[224,2048]{1,0:T(8,128)(2,1)}, bf16[224,2048]{1,0:T(8,128)(2,1)S(1)}, u32[]{:S(2)}, u32[]{:S(2)}) collective-permute-start(bf16[224,2048]{1,0:T(8,128)(2,1)} %bitcast.1), channel_id=1, source_target_pairs={{0,1},{1,0},{2,3},{3,2},{4,5},{5,4},{6,7},{7,6},{8,9},{9,8},{10,11... | collective-permute-start | bytes 2752520 | tf_op jit(solution)/shard_map/ppermute | solution.py:207
  3.0 0.0 copy-start.1
  3.0 1.1 %constant_dynamic-slice_fusion = (bf16[256,512]{1,0:T(8,128)(2,1)S(1)}, bf16[256,512]{1,0:T(8,128)(2,1)S(1)}) fusion(bf16[256,2048]{1,0:T(8,128)(2,1)} %param.9, s32[]{:T(128)S(6)} %select_n.2, bf16[256,2048]{1,0:T(8,128)(2,1)} %param.8), kind=kLoop, calls=%fused_computation.7 | loop fusion | bytes 1048580 | tf_op jit(solution)/shard_map/dynamic_slice | solution.py:211
  4.2 0.0 copy-done
  4.2 0.1 pad_maximum_fusion.refs_4_.refs_2_
  4.3 2.5 %collective-permute-start.8 = (bf16[256,1536]{1,0:T(8,128)(2,1)S(1)}, bf16[256,1536]{1,0:T(8,128)(2,1)S(1)}, u32[]{:S(2)}, u32[]{:S(2)}) collective-permute-start(bf16[256,1536]{1,0:T(8,128)(2,1)S(1)} %pad_maximum_fusion.refs_4_.refs_2_), channel_id=1, source_target_pairs={{0,24},{1,25},{2,26},{3,27},{4,28},{5,29},{6,30},{7,31},{8,16},{9,... | collective-permute-start | bytes 2359304 | tf_op jit(solution)/shard_map/ppermute | solution.py:207
  6.8 0.5 collective-permute-start.6
  7.3 0.5 collective-permute-start.4
  7.8 0.0 copy-done.1
  7.8 0.7 collective-permute-start.10
  8.6 0.0 copy-start.2
  8.6 1.7 %fusion = (f32[896,64]{1,0:T(8,128)S(1)}, f32[896,64]{1,0:T(8,128)S(1)}, f32[896,64]{1,0:T(8,128)S(1)}) fusion(f32[64]{0:T(128)S(1)} %multiply_power_fusion, f32[896]{0:T(1024)S(1)} %iota_convert_fusion), kind=kLoop, calls=%fused_computation.5 | loop fusion | flops 114688 | bytes 691968 | tf_op jit(solution)/shard_map/neg | solution.py:25
  10.3 13.3 %collective-permute-done.refs_1_ = bf16[224,2048]{1,0:T(8,128)(2,1)S(1)} collective-permute-done((bf16[224,2048]{1,0:T(8,128)(2,1)}, bf16[224,2048]{1,0:T(8,128)(2,1)S(1)}, u32[]{:S(2)}, u32[]{:S(2)}) %collective-permute-start) | collective-permute-done | bytes 917536 | tf_op jit(solution)/shard_map/ppermute | solution.py:207
  23.6 0.0 collective-permute-start.3
  23.6 0.3 pad_maximum_fusion.1
  23.9 1.9 %collective-permute-done.8.refs_10_.refs_8_ = bf16[256,1536]{1,0:T(8,128)(2,1)S(1)} collective-permute-done((bf16[256,1536]{1,0:T(8,128)(2,1)S(1)}, bf16[256,1536]{1,0:T(8,128)(2,1)S(1)}, u32[]{:S(2)}, u32[]{:S(2)}) %collective-permute-start.8) | collective-permute-done | bytes 786464 | tf_op jit(solution)/shard_map/ppermute | solution.py:207
  25.8 0.7 collective-permute-start.1
  26.5 0.0 collective-permute-done.10.refs_2_
  26.5 1.3 %collective-permute-start.11 = (bf16[224,2048]{1,0:T(8,128)(2,1)S(1)}, bf16[224,2048]{1,0:T(8,128)(2,1)S(1)}, u32[]{:S(2)}, u32[]{:S(2)}) collective-permute-start(bf16[224,2048]{1,0:T(8,128)(2,1)S(1)} %collective-permute-done.10.refs_2_), channel_id=1, source_target_pairs={{1,0},{2,3},{5,4},{6,7},{9,8},{10,11},{13,12},{14,15},{17,16},{18,... | collective-permute-start | bytes 2752520 | tf_op jit(solution)/shard_map/ppermute | solution.py:207
  27.8 13.3 %collective-permute-done.6.refs_8_.refs_6_ = bf16[256,1536]{1,0:T(8,128)(2,1)S(1)} collective-permute-done((bf16[256,1536]{1,0:T(8,128)(2,1)S(1)}, bf16[256,1536]{1,0:T(8,128)(2,1)S(1)}, u32[]{:S(2)}, u32[]{:S(2)}) %collective-permute-start.6) | collective-permute-done | bytes 786464 | tf_op jit(solution)/shard_map/ppermute | solution.py:207
  41.1 0.0 collective-permute-start.9
  41.1 0.1 collective-permute-done.4.refs_6_.refs_4_
  41.2 0.4 collective-permute-start.7
  41.6 0.0 collective-permute-done.3.refs_5_.refs_3_
  41.6 0.1 collective-permute-start.5
  41.7 0.0 collective-permute-done.1.refs_0_
  41.7 1.3 %collective-permute-start.2 = (bf16[224,2048]{1,0:T(8,128)(2,1)S(1)}, bf16[224,2048]{1,0:T(8,128)(2,1)S(1)}, u32[]{:S(2)}, u32[]{:S(2)}) collective-permute-start(bf16[224,2048]{1,0:T(8,128)(2,1)S(1)} %collective-permute-done.1.refs_0_), channel_id=1, source_target_pairs={{1,0},{2,3},{5,4},{6,7},{9,8},{10,11},{13,12},{14,15},{17,16},{18,... | collective-permute-start | bytes 2752520 | tf_op jit(solution)/shard_map/ppermute | solution.py:207
  43.0 0.0 copy-done.2
  43.0 0.4 collective-permute-done.9.refs_11_.refs_9_
  43.4 1.1 %collective-permute-done.7.refs_9_.refs_7_ = bf16[256,1536]{1,0:T(8,128)(2,1)S(1)} collective-permute-done((bf16[256,1536]{1,0:T(8,128)(2,1)S(1)}, bf16[256,1536]{1,0:T(8,128)(2,1)S(1)}, u32[]{:S(2)}, u32[]{:S(2)}) %collective-permute-start.7) | collective-permute-done | bytes 786464 | tf_op jit(solution)/shard_map/ppermute | solution.py:207
  44.5 1.1 %collective-permute-done.5.refs_7_.refs_5_ = bf16[256,1536]{1,0:T(8,128)(2,1)S(1)} collective-permute-done((bf16[256,1536]{1,0:T(8,128)(2,1)S(1)}, bf16[256,1536]{1,0:T(8,128)(2,1)S(1)}, u32[]{:S(2)}, u32[]{:S(2)}) %collective-permute-start.5) | collective-permute-done | bytes 786464 | tf_op jit(solution)/shard_map/ppermute | solution.py:207
  45.6 6.3 %collective-permute-done.11.refs_3_ = bf16[224,2048]{1,0:T(8,128)(2,1)S(1)} collective-permute-done((bf16[224,2048]{1,0:T(8,128)(2,1)S(1)}, bf16[224,2048]{1,0:T(8,128)(2,1)S(1)}, u32[]{:S(2)}, u32[]{:S(2)}) %collective-permute-start.11) | collective-permute-done | bytes 917536 | tf_op jit(solution)/shard_map/ppermute | solution.py:207
  52.0 6.7 %project_early.1.refs_10_ = bf16[672,1536]{1,0:T(8,128)(2,1)S(1)} custom-call(bf16[224,2048]{1,0:T(8,128)(2,1)S(1)} %bitcast.3, bf16[224,2048]{1,0:T(8,128)(2,1)S(1)} %collective-permute-done.refs_1_, bf16[224,2048]{1,0:T(8,128)(2,1)S(1)} %collective-permute-done.10.refs_2_, bf16[224,2048]{1,0:T(8,128)(2,1)S(1)} %collective-permute-done.11.refs_3_, ...), custom_call_target="tpu_custom_call" | custom-call | flops 4227858432 | bytes 10000000 | tf_op jit(solution)/shard_map/project_early/pallas_call | solution.py:250
  58.7 13.6 %collective-permute-done.2.refs_1_ = bf16[224,2048]{1,0:T(8,128)(2,1)S(1)} collective-permute-done((bf16[224,2048]{1,0:T(8,128)(2,1)S(1)}, bf16[224,2048]{1,0:T(8,128)(2,1)S(1)}, u32[]{:S(2)}, u32[]{:S(2)}) %collective-permute-start.2) | collective-permute-done | bytes 917536 | tf_op jit(solution)/shard_map/ppermute | solution.py:207
  72.3 10.0 %attend.1 = (bf16[224,512]{1,0:T(8,128)(2,1)S(1)}, bf16[224,512]{1,0:T(8,128)(2,1)S(1)}, bf16[224,512]{1,0:T(8,128)(2,1)S(1)}, bf16[224,512]{1,0:T(8,128)(2,1)S(1)}) custom-call(bf16[224,2048]{1,0:T(8,128)(2,1)S(1)} %collective-permute-done.1.refs_0_, bf16[224,2048]{1,0:T(8,128)(2,1)S(1)} %collective-permute-done.2.refs_1_, ...), custom_call_target="tpu_custom_call" | custom-call | flops 2818572288 | bytes 10000000 | tf_op jit(solution)/shard_map/attend/pallas_call | solution.py:268
  82.3 0.1 collective-permute-start.12
  82.3 3.0 %collective-permute-start.13 = (bf16[224,512]{1,0:T(8,128)(2,1)S(1)}, bf16[224,512]{1,0:T(8,128)(2,1)S(1)}, u32[]{:S(2)}, u32[]{:S(2)}) collective-permute-start(bf16[224,512]{1,0:T(8,128)(2,1)S(1)} %get-tuple-element.17), channel_id=1, source_target_pairs={{0,2},{1,3},{2,0},{3,1},{4,6},{5,7},{6,4},{7,5},{8,10},{9,11},{10,... | collective-permute-start | bytes 688136 | tf_op jit(solution)/shard_map/ppermute | solution.py:207
  85.4 1.3 %collective-permute-start.14 = (bf16[224,512]{1,0:T(8,128)(2,1)S(1)}, bf16[224,512]{1,0:T(8,128)(2,1)S(1)}, u32[]{:S(2)}, u32[]{:S(2)}) collective-permute-start(bf16[224,512]{1,0:T(8,128)(2,1)S(1)} %get-tuple-element.18), channel_id=1, source_target_pairs={{0,3},{1,2},{2,1},{3,0},{4,7},{5,6},{6,5},{7,4},{8,11},{9,10},{10,... | collective-permute-start | bytes 688136 | tf_op jit(solution)/shard_map/ppermute | solution.py:207
  86.7 5.6 %collective-permute-done.12.refs_1_ = bf16[224,512]{1,0:T(8,128)(2,1)S(1)} collective-permute-done((bf16[224,512]{1,0:T(8,128)(2,1)S(1)}, bf16[224,512]{1,0:T(8,128)(2,1)S(1)}, u32[]{:S(2)}, u32[]{:S(2)}) %collective-permute-start.12) | collective-permute-done | bytes 229408 | tf_op jit(solution)/shard_map/ppermute | solution.py:207
  92.3 8.8 %collective-permute-done.13.refs_2_ = bf16[224,512]{1,0:T(8,128)(2,1)S(1)} collective-permute-done((bf16[224,512]{1,0:T(8,128)(2,1)S(1)}, bf16[224,512]{1,0:T(8,128)(2,1)S(1)}, u32[]{:S(2)}, u32[]{:S(2)}) %collective-permute-start.13) | collective-permute-done | bytes 229408 | tf_op jit(solution)/shard_map/ppermute | solution.py:207
  101.1 0.0 collective-permute-done.14.refs_3_
  101.1 1.0 join.1
  (4 shorter events, 0.0 us)
Async XLA Ops:
  0.0 4.2 %copy-start = (bf16[256,2048]{1,0:T(8,128)(2,1)S(1)}, bf16[256,2048]{1,0:T(8,128)(2,1)}, u32[]{:S(2)}) copy-start(bf16[256,2048]{1,0:T(8,128)(2,1)} %param.7) | copy-start | bytes 3145732
  0.0 23.6 %collective-permute-start = (bf16[224,2048]{1,0:T(8,128)(2,1)}, bf16[224,2048]{1,0:T(8,128)(2,1)S(1)}, u32[]{:S(2)}, u32[]{:S(2)}) collective-permute-start(bf16[224,2048]{1,0:T(8,128)(2,1)} %bitcast.1), channel_id=1, source_target_pairs={{0,1},{1,0},{2,3},{3,2},{4,5},{5,4},{6,7},{7,6},{8,9},{9,8},{10,11... | collective-permute-start | bytes 2752520 | tf_op jit(solution)/shard_map/ppermute | solution.py:207
  3.0 4.8 %copy-start.1 = (bf16[1,224,2048]{2,1,0:T(8,128)(2,1)S(1)}, bf16[1,224,2048]{2,1,0:T(8,128)(2,1)}, u32[]{:S(2)}) copy-start(bf16[1,224,2048]{2,1,0:T(8,128)(2,1)} %param.5) | copy-start | bytes 2752516
  4.3 21.5 %collective-permute-start.8 = (bf16[256,1536]{1,0:T(8,128)(2,1)S(1)}, bf16[256,1536]{1,0:T(8,128)(2,1)S(1)}, u32[]{:S(2)}, u32[]{:S(2)}) collective-permute-start(bf16[256,1536]{1,0:T(8,128)(2,1)S(1)} %pad_maximum_fusion.refs_4_.refs_2_), channel_id=1, source_target_pairs={{0,24},{1,25},{2,26},{3,27},{4,28},{5,29},{6,30},{7,31},{8,16},{9,... | collective-permute-start | bytes 2359304 | tf_op jit(solution)/shard_map/ppermute | solution.py:207
  6.8 34.3 %collective-permute-start.6 = (bf16[256,1536]{1,0:T(8,128)(2,1)S(1)}, bf16[256,1536]{1,0:T(8,128)(2,1)S(1)}, u32[]{:S(2)}, u32[]{:S(2)}) collective-permute-start(bf16[256,1536]{1,0:T(8,128)(2,1)S(1)} %pad_maximum_fusion.refs_4_.refs_2_), channel_id=1, source_target_pairs={{0,16},{1,17},{2,18},{3,19},{4,20},{5,21},{6,22},{7,23},{8,24},{9,... | collective-permute-start | bytes 2359304 | tf_op jit(solution)/shard_map/ppermute | solution.py:207
  7.3 33.9 %collective-permute-start.4 = (bf16[256,1536]{1,0:T(8,128)(2,1)S(1)}, bf16[256,1536]{1,0:T(8,128)(2,1)S(1)}, u32[]{:S(2)}, u32[]{:S(2)}) collective-permute-start(bf16[256,1536]{1,0:T(8,128)(2,1)S(1)} %pad_maximum_fusion.refs_4_.refs_2_), channel_id=1, source_target_pairs={{0,8},{1,9},{2,10},{3,11},{4,12},{5,13},{6,14},{7,15},{8,0},{9,1},... | collective-permute-start | bytes 2359304 | tf_op jit(solution)/shard_map/ppermute | solution.py:207
  7.8 18.6 %collective-permute-start.10 = (bf16[224,2048]{1,0:T(8,128)(2,1)S(1)}, bf16[224,2048]{1,0:T(8,128)(2,1)S(1)}, u32[]{:S(2)}, u32[]{:S(2)}) collective-permute-start(bf16[224,2048]{1,0:T(8,128)(2,1)S(1)} %bitcast.2), channel_id=1, source_target_pairs={{1,2},{2,1},{5,6},{6,5},{9,10},{10,9},{13,14},{14,13},{17,18},{18,... | collective-permute-start | bytes 2752520 | tf_op jit(solution)/shard_map/ppermute | solution.py:207
  8.6 34.4 %copy-start.2 = (bf16[2048]{0:T(1024)(128)(2,1)S(1)}, bf16[2048]{0:T(1024)(128)(2,1)}, u32[]{:S(2)}) copy-start(bf16[2048]{0:T(1024)(128)(2,1)} %param.6) | copy-start | bytes 12292
  23.6 18.0 %collective-permute-start.3 = (bf16[256,1536]{1,0:T(8,128)(2,1)S(1)}, bf16[256,1536]{1,0:T(8,128)(2,1)S(1)}, u32[]{:S(2)}, u32[]{:S(2)}) collective-permute-start(bf16[256,1536]{1,0:T(8,128)(2,1)S(1)} %pad_maximum_fusion.refs_4_.refs_2_), channel_id=1, source_target_pairs={{0,4},{1,5},{2,6},{3,7},{4,0},{5,1},{6,2},{7,3},{8,12},{9,13},{10,... | collective-permute-start | bytes 2359304 | tf_op jit(solution)/shard_map/ppermute | solution.py:207
  25.8 16.0 %collective-permute-start.1 = (bf16[224,2048]{1,0:T(8,128)(2,1)S(1)}, bf16[224,2048]{1,0:T(8,128)(2,1)S(1)}, u32[]{:S(2)}, u32[]{:S(2)}) collective-permute-start(bf16[224,2048]{1,0:T(8,128)(2,1)S(1)} %collective-permute-done.refs_1_), channel_id=1, source_target_pairs={{1,2},{2,1},{5,6},{6,5},{9,10},{10,9},{13,14},{14,13},{17,18},{18,... | collective-permute-start | bytes 2752520 | tf_op jit(solution)/shard_map/ppermute | solution.py:207
  26.5 25.5 %collective-permute-start.11 = (bf16[224,2048]{1,0:T(8,128)(2,1)S(1)}, bf16[224,2048]{1,0:T(8,128)(2,1)S(1)}, u32[]{:S(2)}, u32[]{:S(2)}) collective-permute-start(bf16[224,2048]{1,0:T(8,128)(2,1)S(1)} %collective-permute-done.10.refs_2_), channel_id=1, source_target_pairs={{1,0},{2,3},{5,4},{6,7},{9,8},{10,11},{13,12},{14,15},{17,16},{18,... | collective-permute-start | bytes 2752520 | tf_op jit(solution)/shard_map/ppermute | solution.py:207
  41.1 2.3 %collective-permute-start.9 = (bf16[256,1536]{1,0:T(8,128)(2,1)S(1)}, bf16[256,1536]{1,0:T(8,128)(2,1)S(1)}, u32[]{:S(2)}, u32[]{:S(2)}) collective-permute-start(bf16[256,1536]{1,0:T(8,128)(2,1)S(1)} %collective-permute-done.8.refs_10_.refs_8_), channel_id=1, source_target_pairs={{0,4},{1,5},{2,6},{3,7},{4,0},{5,1},{6,2},{7,3},{8,12},{9,13},{10,... | collective-permute-start | bytes 2359304 | tf_op jit(solution)/shard_map/ppermute | solution.py:207
  41.2 3.3 %collective-permute-start.7 = (bf16[256,1536]{1,0:T(8,128)(2,1)S(1)}, bf16[256,1536]{1,0:T(8,128)(2,1)S(1)}, u32[]{:S(2)}, u32[]{:S(2)}) collective-permute-start(bf16[256,1536]{1,0:T(8,128)(2,1)S(1)} %collective-permute-done.6.refs_8_.refs_6_), channel_id=1, source_target_pairs={{0,4},{1,5},{2,6},{3,7},{4,0},{5,1},{6,2},{7,3},{8,12},{9,13},{10,... | collective-permute-start | bytes 2359304 | tf_op jit(solution)/shard_map/ppermute | solution.py:207
  41.6 4.0 %collective-permute-start.5 = (bf16[256,1536]{1,0:T(8,128)(2,1)S(1)}, bf16[256,1536]{1,0:T(8,128)(2,1)S(1)}, u32[]{:S(2)}, u32[]{:S(2)}) collective-permute-start(bf16[256,1536]{1,0:T(8,128)(2,1)S(1)} %collective-permute-done.4.refs_6_.refs_4_), channel_id=1, source_target_pairs={{0,4},{1,5},{2,6},{3,7},{4,0},{5,1},{6,2},{7,3},{8,12},{9,13},{10,... | collective-permute-start | bytes 2359304 | tf_op jit(solution)/shard_map/ppermute | solution.py:207
  41.7 30.5 %collective-permute-start.2 = (bf16[224,2048]{1,0:T(8,128)(2,1)S(1)}, bf16[224,2048]{1,0:T(8,128)(2,1)S(1)}, u32[]{:S(2)}, u32[]{:S(2)}) collective-permute-start(bf16[224,2048]{1,0:T(8,128)(2,1)S(1)} %collective-permute-done.1.refs_0_), channel_id=1, source_target_pairs={{1,0},{2,3},{5,4},{6,7},{9,8},{10,11},{13,12},{14,15},{17,16},{18,... | collective-permute-start | bytes 2752520 | tf_op jit(solution)/shard_map/ppermute | solution.py:207
  82.3 10.0 %collective-permute-start.12 = (bf16[224,512]{1,0:T(8,128)(2,1)S(1)}, bf16[224,512]{1,0:T(8,128)(2,1)S(1)}, u32[]{:S(2)}, u32[]{:S(2)}) collective-permute-start(bf16[224,512]{1,0:T(8,128)(2,1)S(1)} %get-tuple-element.16), channel_id=1, source_target_pairs={{0,1},{1,0},{2,3},{3,2},{4,5},{5,4},{6,7},{7,6},{8,9},{9,8},{10,11... | collective-permute-start | bytes 688136 | tf_op jit(solution)/shard_map/ppermute | solution.py:207
  82.3 18.7 %collective-permute-start.13 = (bf16[224,512]{1,0:T(8,128)(2,1)S(1)}, bf16[224,512]{1,0:T(8,128)(2,1)S(1)}, u32[]{:S(2)}, u32[]{:S(2)}) collective-permute-start(bf16[224,512]{1,0:T(8,128)(2,1)S(1)} %get-tuple-element.17), channel_id=1, source_target_pairs={{0,2},{1,3},{2,0},{3,1},{4,6},{5,7},{6,4},{7,5},{8,10},{9,11},{10,... | collective-permute-start | bytes 688136 | tf_op jit(solution)/shard_map/ppermute | solution.py:207
  85.4 15.7 %collective-permute-start.14 = (bf16[224,512]{1,0:T(8,128)(2,1)S(1)}, bf16[224,512]{1,0:T(8,128)(2,1)S(1)}, u32[]{:S(2)}, u32[]{:S(2)}) collective-permute-start(bf16[224,512]{1,0:T(8,128)(2,1)S(1)} %get-tuple-element.18), channel_id=1, source_target_pairs={{0,3},{1,2},{2,1},{3,0},{4,7},{5,6},{6,5},{7,4},{8,11},{9,10},{10,... | collective-permute-start | bytes 688136 | tf_op jit(solution)/shard_map/ppermute | solution.py:207

commit v3 on v2

v3 whole, which is shorter than its diff:
```python
import functools
import math

import jax
import jax.numpy as jnp
from jax import lax
from jax.experimental import pallas as pl
from jax.experimental.pallas import tpu as pltpu
from jax.sharding import PartitionSpec as P

HEADS = 16
HEAD_DIM = 128
HALF = HEAD_DIM // 2
EPS = 1e-05
VMEM_LIMIT = 28 * 1024 * 1024


def tables(length):
    freqs = 10000.0 ** (-(jnp.arange(HALF).astype(jnp.float32) * 2.0) / HEAD_DIM)
    angles = jnp.arange(length).astype(jnp.float32)[:, None] * freqs[None, :]
    cosine = jnp.cos(angles)
    sine = jnp.sin(angles)
    return (
        jnp.concatenate([cosine, cosine], axis=1),
        jnp.concatenate([-sine, sine], axis=1),
    )


def normalize(block, gain):
    rows = block.astype(jnp.float32)
    scale = lax.rsqrt(jnp.mean(rows * rows, axis=1, keepdims=True) + EPS)
    return (rows * scale * gain.astype(jnp.float32)).astype(jnp.bfloat16)


def project(normed, weights, cos_ref, sin_ref, parts, cols, store):
    step = 2 * HEAD_DIM
    for first in range(0, 3 * cols, step):
        linear = jnp.dot(
            normed[...], weights[:, first : first + step], preferred_element_type=jnp.float32
        )
        for row, rows, start in parts:
            part = linear[row : row + rows]
            if first < 2 * cols:
                cosine = cos_ref[pl.ds(start, rows), :]
                sine = sin_ref[pl.ds(start, rows), :]
                heads = [part[:, h * HEAD_DIM : (h + 1) * HEAD_DIM] for h in range(2)]
                part = jnp.concatenate(
                    [x * cosine + pltpu.roll(x, HALF, 1) * sine for x in heads], axis=1
                )
            store(row, rows, start, first, step, part.astype(jnp.bfloat16))


def start_weights(owners, shards, weights, sems):
    depth = shards[0].shape[0]
    copies = []
    for i, (owner, shard) in enumerate(zip(owners, shards)):
        copy = pltpu.make_async_copy(
            shard, weights.at[pl.ds(pl.multiple_of(owner * depth, depth), depth)], sems.at[i]
        )
        copy.start()
        copies.append(copy)
    return copies


def role(rows):
    d, c = lax.axis_index("dp"), lax.axis_index("ctx")
    y, core = d // 4, d % 2
    lone = core == 0
    inner = jnp.logical_or(c == 1, c == 2)
    home = c // 2 == y
    half = rows // 2
    near = c ^ jnp.where(inner, 3, 2)
    far = c ^ jnp.where(inner, 2, 3)
    mine, other = y * half, (1 - y) * half
    hint = lambda value: pl.multiple_of(value, half)
    early = [
        (0, rows, hint(c * rows)),
        (rows, rows, hint((c ^ 1) * rows)),
        (2 * rows, half, hint(jnp.where(lone, near * rows, (c ^ 2) * rows + mine))),
        (2 * rows + half, half, hint(jnp.where(lone, near * rows + half, (c ^ 3) * rows + mine))),
    ]
    late = [
        (0, half, hint(jnp.where(lone, far * rows, (c ^ 2) * rows + other))),
        (half, half, hint(jnp.where(lone, far * rows + half, (c ^ 3) * rows + other))),
    ]
    return {
        "lone": lone,
        "inner": inner,
        "home": home,
        "mine": hint(mine),
        "other": hint(other),
        "early": early,
        "late": late,
        "base": jnp.where(lone, c, 2 * y + c % 2),
        "owners": [d ^ k for k in range(8)],
    }


def begin(cases):
    for condition, copies in cases:

        @pl.when(condition)
        def _(copies=copies):
            for source, target, sem in copies:
                pltpu.make_async_copy(source, target, sem).start()


def early_kernel(rows, cols, *refs):
    own, first, second, fourth, swap0, swap1, r1, r2, r3, x1 = refs[:10]
    shards = refs[10:18]
    gain, cos_ref, sin_ref, out, held, normed, weights, token_sems, weight_sems = refs[18:]
    me = role(rows)
    half = rows // 2
    slot = lambda i: held.at[pl.ds(i * rows, rows)]
    part = lambda i, start: held.at[pl.ds(i * rows + start, half)]
    sems = [token_sems.at[i] for i in range(3)]
    mine, other = me["mine"], me["other"]
    both = jnp.logical_and
    paired = jnp.logical_not(me["lone"])
    away = jnp.logical_not(me["home"])
    begin(
        [
            (jnp.logical_or(me["lone"], me["home"]), [(own, slot(0), sems[0])]),
            (
                both(paired, away),
                [(swap0, part(0, mine), sems[0]), (swap1, part(0, other), sems[0])],
            ),
            (me["lone"], [(first, slot(1), sems[1])]),
            (paired, [(r1, part(1, mine), sems[1]), (x1, part(1, other), sems[1])]),
            (both(me["lone"], me["inner"]), [(second, slot(2), sems[2])]),
            (both(me["lone"], jnp.logical_not(me["inner"])), [(fourth, slot(2), sems[2])]),
            (paired, [(r2, part(2, 0), sems[2]), (r3, part(2, half), sems[2])]),
        ]
    )
    weight_loads = start_weights(me["owners"], shards, weights, weight_sems)
    for i in range(3):
        pltpu.make_async_copy(own, slot(i), sems[i]).wait()
        normed[pl.ds(i * rows, rows), :] = normalize(slot(i)[...], gain[...])
    for load in weight_loads:
        load.wait()

    def store(row, count, start, lane, step, value):
        out[pl.ds(row, count), pl.ds(lane, step)] = value

    project(normed, weights, cos_ref, sin_ref, me["early"], cols, store)


def late_kernel(rows, cols, total, *refs):
    third, fifth, x2, x3 = refs[:4]
    shards = refs[4:12]
    early, gain, cos_ref, sin_ref = refs[12:16]
    outs = refs[16 : 16 + total]
    held, normed, weights, qkv, result, token_sem, weight_sems, early_sems, out_sems = refs[16 + total :]
    me = role(rows)
    half = rows // 2
    paired = jnp.logical_not(me["lone"])
    begin(
        [
            (jnp.logical_and(me["lone"], me["inner"]), [(third, held, token_sem)]),
            (jnp.logical_and(me["lone"], jnp.logical_not(me["inner"])), [(fifth, held, token_sem)]),
            (
                paired,
                [
                    (x2, held.at[pl.ds(0, half)], token_sem),
                    (x3, held.at[pl.ds(half, half)], token_sem),
                ],
            ),
        ]
    )
    weight_loads = start_weights(me["owners"], shards, weights, weight_sems)
    early_loads = []
    for i, (row, count, start) in enumerate(me["early"]):
        load = pltpu.make_async_copy(
            early.at[pl.ds(row, count)], qkv.at[pl.ds(start, count)], early_sems.at[i]
        )
        load.start()
        early_loads.append(load)
    pltpu.make_async_copy(third, held, token_sem).wait()
    normed[...] = normalize(held[...], gain[...])
    for load in weight_loads:
        load.wait()

    def store(row, count, start, lane, step, value):
        qkv[pl.ds(start, count), pl.ds(lane, step)] = value

    project(normed, weights, cos_ref, sin_ref, me["late"], cols, store)
    for load in early_loads:
        load.wait()
    attend(qkv, result, me["base"], total, rows, cols)
    copies = []
    for k in range(total):
        copy = pltpu.make_async_copy(result.at[k], outs[k], out_sems.at[k])
        copy.start()
        copies.append(copy)
    for copy in copies:
        copy.wait()


def attend(qkv, result, me, total, rows, cols):
    factor = HEAD_DIM ** (-0.5) * math.log2(math.e)
    below = lax.broadcasted_iota(jnp.int32, (rows, rows), 0) >= lax.broadcasted_iota(
        jnp.int32, (rows, rows), 1
    )

    def scored(q, k):
        return lax.dot_general(q, k, (((1,), (1,)), ((), ())), preferred_element_type=jnp.float32)

    for block in range(total):
        own, past = slice(block * rows, (block + 1) * rows), slice(0, block * rows)
        for head in range(cols // HEAD_DIM):
            lane = slice(head * HEAD_DIM, (head + 1) * HEAD_DIM)
            k_lane = slice(cols + lane.start, cols + lane.stop)
            v_lane = slice(2 * cols + lane.start, 2 * cols + lane.stop)
            q = qkv[own, lane]
            near = jnp.where(below, scored(q, qkv[own, k_lane]), -1e30)
            top = jnp.max(near, axis=1, keepdims=True)
            if block:
                far = scored(q, qkv[past, k_lane])
                top = jnp.maximum(top, jnp.max(far, axis=1, keepdims=True))
            top = top * factor
            expo = jnp.exp2(near * factor - top)
            bottom = jnp.sum(expo, axis=1, keepdims=True)
            numer = jnp.dot(expo.astype(jnp.bfloat16), qkv[own, v_lane], preferred_element_type=jnp.float32)
            if block:
                expo = jnp.exp2(far * factor - top)
                bottom += jnp.sum(expo, axis=1, keepdims=True)
                numer += jnp.dot(
                    expo.astype(jnp.bfloat16), qkv[past, v_lane], preferred_element_type=jnp.float32
                )
            result[block ^ me, :, lane] = (numer / bottom).astype(jnp.bfloat16)


def join_kernel(cols, total, own, *refs):
    pieces, out = refs[:total], refs[total]
    d, c = lax.axis_index("dp"), lax.axis_index("ctx")
    y, lone = d // 4, d % 2 == 0
    for k in range(total):
        source = c ^ k
        heads = jnp.where(lone, source ^ (2 * y), (2 * y + source % 2) ^ (2 * (source // 2)))
        lane = pl.ds(pl.multiple_of(heads * cols, cols), cols)
        if k:
            out[0, :, lane] = pieces[k][...]
        else:
            kept = jnp.logical_or(lone, c // 2 == y)
            out[0, :, lane] = jnp.where(kept, own[...], pieces[k][...])


def fast(dp, ctx, tokens, norm_gain, q_weight, k_weight, v_weight):
    rows, features = tokens.shape[1], tokens.shape[2]
    half = rows // 2
    cols = HEADS // ctx * HEAD_DIM
    every = [(d, c) for d in range(dp) for c in range(ctx)]

    def send(value, to):
        perm = [
            (d * ctx + c, to(d, c)[0] * ctx + to(d, c)[1]) for d, c in every if to(d, c) is not None
        ]
        return lax.ppermute(value, ("dp", "ctx"), perm)

    def lone(to):
        return lambda d, c: None if d & 1 else to(d, c)

    def paired(to):
        return lambda d, c: to(d, c) if d & 1 else None

    pair = lone(lambda d, c: (d, c ^ 1))
    middle = lone(lambda d, c: (d, 3 - c) if c in (1, 2) else None)
    outward = lone(lambda d, c: (d, {1: 0, 2: 3}[c]) if c in (1, 2) else None)
    across = paired(lambda d, c: (d ^ 4, c))
    d, c = lax.axis_index("dp"), lax.axis_index("ctx")
    y = d // 4
    own = tokens[0]
    mine = lax.dynamic_slice_in_dim(own, y * half, half, 0)
    other = lax.dynamic_slice_in_dim(own, (1 - y) * half, half, 0)
    first = send(own, pair)
    second = send(own, middle)
    swap0 = send(other, across)

    def columns(heads):
        return jnp.concatenate(
            [lax.dynamic_slice_in_dim(w, heads * cols, cols, 1) for w in (q_weight, k_weight, v_weight)],
            axis=1,
        )

    heads = c ^ (2 * y)
    shards = {0: columns(heads)}
    shards[2] = send(shards[0], lambda d, c: (d ^ 2, c))
    shards[4] = send(columns(heads ^ 2), lambda d, c: (d ^ 4, c))
    swap1 = send(mine, paired(lambda d, c: (d ^ 4, c) if c // 2 == d >> 2 else None))
    cosine, sine = tables(ctx * rows)
    first, cosine, sine = lax.optimization_barrier((first, cosine, sine))
    third = send(first, middle)
    fourth = send(second, outward)
    home = c // 2 == y
    r1 = send(jnp.where(home, mine, swap0), paired(lambda d, c: (d, c ^ 1)))
    cross = jnp.where(home, swap0, mine)
    r2 = send(cross, paired(lambda d, c: (d, c ^ 2)))
    r3 = send(cross, paired(lambda d, c: (d, c ^ 3)))
    shards[6] = send(shards[4], lambda d, c: (d ^ 2, c))
    x1 = send(r1, across)
    x2 = send(r2, across)
    x3 = send(r3, across)
    fifth = send(third, outward)
    for k in range(0, dp, 2):
        shards[k + 1] = send(shards[k], lambda d, c: (d ^ 1, c))
    shards = [shards[k] for k in range(dp)]

    gain = norm_gain[None, :]
    any_space = pl.BlockSpec(memory_space=pl.ANY)
    vmem = pl.BlockSpec(memory_space=pltpu.VMEM)
    early = pl.pallas_call(
        functools.partial(early_kernel, rows, cols),
        out_shape=jax.ShapeDtypeStruct((3 * rows, 3 * cols), jnp.bfloat16),
        in_specs=[any_space] * 18 + [vmem] * 3,
        out_specs=vmem,
        scratch_shapes=[
            pltpu.VMEM((3 * rows, features), jnp.bfloat16),
            pltpu.VMEM((3 * rows, features), jnp.bfloat16),
            pltpu.VMEM((features, 3 * cols), jnp.bfloat16),
            pltpu.SemaphoreType.DMA((3,)),
            pltpu.SemaphoreType.DMA((dp,)),
        ],
        compiler_params=pltpu.CompilerParams(vmem_limit_bytes=VMEM_LIMIT),
        cost_estimate=pl.CostEstimate(
            flops=2 * 3 * rows * features * 3 * cols, bytes_accessed=10_000_000, transcendentals=0
        ),
        name="project_early",
    )(own, first, second, fourth, swap0, swap1, r1, r2, r3, x1, *shards, gain, cosine, sine)
    pieces = pl.pallas_call(
        functools.partial(late_kernel, rows, cols, ctx),
        out_shape=[jax.ShapeDtypeStruct((rows, cols), jnp.bfloat16)] * ctx,
        in_specs=[any_space] * 13 + [vmem] * 3,
        out_specs=[any_space] * ctx,
        scratch_shapes=[
            pltpu.VMEM((rows, features), jnp.bfloat16),
            pltpu.VMEM((rows, features), jnp.bfloat16),
            pltpu.VMEM((features, 3 * cols), jnp.bfloat16),
            pltpu.VMEM((ctx * rows, 3 * cols), jnp.bfloat16),
            pltpu.VMEM((ctx, rows, cols), jnp.bfloat16),
            pltpu.SemaphoreType.DMA,
            pltpu.SemaphoreType.DMA((dp,)),
            pltpu.SemaphoreType.DMA((4,)),
            pltpu.SemaphoreType.DMA((ctx,)),
        ],
        compiler_params=pltpu.CompilerParams(vmem_limit_bytes=VMEM_LIMIT),
        cost_estimate=pl.CostEstimate(
            flops=2 * rows * features * 3 * cols * 2, bytes_accessed=10_000_000, transcendentals=2_000_000
        ),
        name="attend",
    )(third, fifth, x2, x3, *shards, early, gain, cosine, sine)

    def back(k):
        def to(d, c):
            if d & 1:
                target = ((d & 3) | (c // 2) << 2, (2 * (d >> 2) + c % 2) ^ k)
            else:
                target = (d, c ^ k)
            return None if target == (d, c) else target

        return to

    arrived = [send(pieces[k], back(k)) for k in range(ctx)]
    return pl.pallas_call(
        functools.partial(join_kernel, cols, ctx),
        out_shape=jax.ShapeDtypeStruct((1, rows, ctx * cols), jnp.bfloat16),
        in_specs=[vmem] * (ctx + 1),
        out_specs=vmem,
        compiler_params=pltpu.CompilerParams(vmem_limit_bytes=8 * 1024 * 1024),
        name="join",
    )(pieces[0], *arrived)


def rotate(values, positions):
    heads = values.shape[1] // HEAD_DIM
    shaped = values.reshape(values.shape[0], heads, HEAD_DIM)
    freqs = 10000.0 ** (-(jnp.arange(HALF).astype(jnp.float32) * 2.0) / HEAD_DIM)
    angles = positions[:, None] * freqs[None, :]
    cosine = jnp.cos(angles)[:, None, :]
    sine = jnp.sin(angles)[:, None, :]
    first = shaped[:, :, :HALF]
    second = shaped[:, :, HALF:]
    return jnp.concatenate(
        [first * cosine - second * sine, second * cosine + first * sine], axis=2
    )


def general(dp, ctx, tokens, norm_gain, q_weight, k_weight, v_weight):
    rows = tokens.shape[1]
    heads = HEADS // ctx
    cols = heads * HEAD_DIM
    me = lax.axis_index("ctx")
    part = jnp.concatenate(
        [lax.dynamic_slice_in_dim(w, me * cols, cols, 1) for w in (q_weight, k_weight, v_weight)], axis=1
    )
    weights = lax.all_gather(part, "dp", axis=0, tiled=True)
    whole = lax.all_gather(tokens[0], "ctx", axis=0, tiled=True)
    normed = normalize(whole, norm_gain[None, :])
    linear = jnp.dot(normed, weights, preferred_element_type=jnp.float32)
    length = ctx * rows
    positions = jnp.arange(length).astype(jnp.float32)
    q = rotate(linear[:, :cols], positions).astype(jnp.bfloat16)
    k = rotate(linear[:, cols : 2 * cols], positions).astype(jnp.bfloat16)
    v = linear[:, 2 * cols :].astype(jnp.bfloat16).reshape(length, heads, HEAD_DIM)
    allowed = jnp.arange(length)[None, :] <= jnp.arange(length)[:, None]
    scores = jnp.einsum("qhd,khd->hqk", q, k, preferred_element_type=jnp.float32) * HEAD_DIM ** (-0.5)
    scores = jnp.where(allowed[None], scores, -1e30)
    top = jnp.max(scores, axis=2, keepdims=True)
    expo = jnp.where(allowed[None], jnp.exp(scores - top), 0.0)
    numer = jnp.einsum("hqk,khd->hqd", expo.astype(jnp.bfloat16), v, preferred_element_type=jnp.float32)
    result = (numer / jnp.sum(expo, axis=2, keepdims=True)).astype(jnp.bfloat16)
    result = result.reshape(heads, ctx, rows, HEAD_DIM).transpose(1, 2, 0, 3).reshape(ctx, rows, cols)
    back = lax.all_to_all(result, "ctx", 0, 0)
    return back.transpose(1, 0, 2).reshape(1, rows, ctx * cols)


def solution(mesh):
    dp, ctx = mesh.shape["dp"], mesh.shape["ctx"]
    body = fast if (dp, ctx) == (8, 4) else general
    placed = (P("dp", "ctx", None), P(), P("dp", None), P("dp", None), P("dp", None))
    return jax.shard_map(
        functools.partial(body, dp, ctx),
        mesh=mesh,
        in_specs=placed,
        out_specs=P("dp", "ctx", None),
        check_vma=False,
    )
```

time: 102 us -> 129 us (1.26)
  the two profiles are of different devices: /device:TPU:0 before, /device:TPU:17 now
where the time goes in v3:
time: 129 us; the launch traced here: 128 us
  waiting for transfers between devices  63.8 us (49%)
  starting transfers between devices  36.6 us (28%)
  Pallas kernels  19.2 us (15%)
  local copies, waits for them, and re-layouts  4.98 us (4%)
  other arithmetic  3.2 us (2%)
    ppermute x24, waiting for transfers between devices, send(): return lax.ppermute(value, ('dp', 'ctx'), perm)  63.8 us
    ppermute x24, starting transfers between devices, send(): return lax.ppermute(value, ('dp', 'ctx'), perm)  36.6 us
    pallas_call x1, Pallas kernels, fast(): pl.pallas_call(functools.partial(late_kernel, rows, cols, ctx), out_shape...  10.4 us
    pallas_call x1, Pallas kernels, fast(): pl.pallas_call(functools.partial(early_kernel, rows, cols), out_shape=jax...  7.76 us
    dynamic_slice x2, local copies, waits for them, and re-layouts, columns(): lax.dynamic_slice_in_dim(w, heads * cols, cols, 1)  3.14 us
  transfers between devices with their start and end apart: 24, of which 9 were waited for; matrix products, arithmetic and copies ran while one was open for 5% of the time, Pallas kernels for 6%

profile of v3, /device:TPU:17, one launch (start us, length us, event | category | flops | bytes accessed | tf_op | source)
XLA Modules:
  0.0 128.2 jit_solution(10995937218762123859)
XLA Ops:
  0.0 1.8 %dynamic-slice_bitcast_fusion.1 = bf16[112,2048]{1,0:T(8,128)(2,1)} fusion(bf16[1,224,2048]{2,1,0:T(8,128)(2,1)} %param.5, s32[]{:T(128)S(6)} %select_n.39), kind=kLoop, calls=%fused_computation.7 | loop fusion | bytes 917508 | tf_op jit(solution)/shard_map/dynamic_slice | solution.py:274
  1.8 3.1 %collective-permute-start.3 = (bf16[112,2048]{1,0:T(8,128)(2,1)}, bf16[112,2048]{1,0:T(8,128)(2,1)S(1)}, u32[]{:S(2)}, u32[]{:S(2)}) collective-permute-start(bf16[112,2048]{1,0:T(8,128)(2,1)} %dynamic-slice_bitcast_fusion.1), channel_id=1, source_target_pairs={{4,20},{5,21},{6,22},{7,23},{12,28},{13,29},{14,30},{15,31},{20,4}... | collective-permute-start | bytes 1376264 | tf_op jit(solution)/shard_map/ppermute | solution.py:258
  5.0 1.1 constant_dynamic-slice_fusion.2
  6.1 0.0 copy-start
  6.1 2.1 %constant_dynamic-slice_fusion = (bf16[256,512]{1,0:T(8,128)(2,1)S(1)}, bf16[256,512]{1,0:T(8,128)(2,1)S(1)}, bf16[256,512]{1,0:T(8,128)(2,1)S(1)}, bf16[256,512]{1,0:T(8,128)(2,1)}) fusion(bf16[256,2048]{1,0:T(8,128)(2,1)} %param.9, s32[]{:T(128)S(6)} %select_n.43, s32[]{:T(128)S(6)} %select_n.42, bf16[256,2048]{1,0:T(8,128)(2,1)} %param.8), kind=kLoop, calls=%fused_computation.12 | loop fusion | bytes 2097160 | tf_op jit(solution)/shard_map/dynamic_slice | solution.py:281
  8.1 0.1 pad_maximum_fusion.refs_10_.refs_4_
  8.2 1.3 collective-permute-start.9
  9.5 1.6 %collective-permute-start = (bf16[224,2048]{1,0:T(8,128)(2,1)S(1)}, bf16[224,2048]{1,0:T(8,128)(2,1)}, u32[]{:S(2)}, u32[]{:S(2)}) collective-permute-start(bf16[224,2048]{1,0:T(8,128)(2,1)S(1)} %bitcast.6), channel_id=1, source_target_pairs={{0,1},{1,0},{2,3},{3,2},{8,9},{9,8},{10,11},{11,10},{16,17},{17,16... | collective-permute-start | bytes 2752520 | tf_op jit(solution)/shard_map/ppermute | solution.py:258
  11.1 1.6 %collective-permute-start.15 = (bf16[224,2048]{1,0:T(8,128)(2,1)S(1)}, bf16[224,2048]{1,0:T(8,128)(2,1)}, u32[]{:S(2)}, u32[]{:S(2)}) collective-permute-start(bf16[224,2048]{1,0:T(8,128)(2,1)S(1)} %bitcast.7), channel_id=1, source_target_pairs={{1,2},{2,1},{9,10},{10,9},{17,18},{18,17},{25,26},{26,25}} | collective-permute-start | bytes 2752520 | tf_op jit(solution)/shard_map/ppermute | solution.py:258
  12.7 1.0 pad_maximum_fusion.1
  13.7 0.0 collective-permute-done.3.refs_4_
  13.7 0.3 collective-permute-start.11
  14.0 0.1 broadcast_select_fusion
  14.1 0.1 broadcast_select_fusion.1
  14.1 15.9 %collective-permute-done.11.refs_14_.refs_8_ = bf16[256,1536]{1,0:T(8,128)(2,1)S(1)} collective-permute-done((bf16[256,1536]{1,0:T(8,128)(2,1)S(1)}, bf16[256,1536]{1,0:T(8,128)(2,1)S(1)}, u32[]{:S(2)}, u32[]{:S(2)}) %collective-permute-start.11) | collective-permute-done | bytes 786464 | tf_op jit(solution)/shard_map/ppermute | solution.py:258
  30.0 2.3 %collective-permute-start.4 = (bf16[112,2048]{1,0:T(8,128)(2,1)S(1)}, bf16[112,2048]{1,0:T(8,128)(2,1)S(1)}, u32[]{:S(2)}, u32[]{:S(2)}) collective-permute-start(bf16[112,2048]{1,0:T(8,128)(2,1)S(1)} %broadcast_select_fusion.1), channel_id=1, source_target_pairs={{4,6},{5,7},{6,4},{7,5},{12,14},{13,15},{14,12},{15,13},{20,22},{2... | collective-permute-start | bytes 1376264 | tf_op jit(solution)/shard_map/ppermute | solution.py:258
  32.4 5.5 %collective-permute-start.6 = (bf16[112,2048]{1,0:T(8,128)(2,1)S(1)}, bf16[112,2048]{1,0:T(8,128)(2,1)S(1)}, u32[]{:S(2)}, u32[]{:S(2)}) collective-permute-start(bf16[112,2048]{1,0:T(8,128)(2,1)S(1)} %broadcast_select_fusion.1), channel_id=1, source_target_pairs={{4,7},{5,6},{6,5},{7,4},{12,15},{13,14},{14,13},{15,12},{20,23},{2... | collective-permute-start | bytes 1376264 | tf_op jit(solution)/shard_map/ppermute | solution.py:258
  37.8 0.0 collective-permute-done.8.refs_11_.refs_5_
  37.8 0.0 copy-start.1
  37.8 1.9 %collective-permute-start.18 = (bf16[112,2048]{1,0:T(8,128)(2,1)S(1)}, bf16[112,2048]{1,0:T(8,128)(2,1)S(1)}, u32[]{:S(2)}, u32[]{:S(2)}) collective-permute-start(bf16[112,2048]{1,0:T(8,128)(2,1)S(1)} %get-tuple-element.19), channel_id=1, source_target_pairs={{4,5},{5,4},{6,7},{7,6},{12,13},{13,12},{14,15},{15,14},{20,21},{2... | collective-permute-start | bytes 1376264 | tf_op jit(solution)/shard_map/ppermute | solution.py:258
  39.8 1.7 %fusion = (f32[896,64]{1,0:T(8,128)S(1)}, f32[896,64]{1,0:T(8,128)S(1)}, f32[896,64]{1,0:T(8,128)S(1)}) fusion(f32[64]{0:T(128)S(1)} %multiply_power_fusion, f32[896]{0:T(1024)S(1)} %iota_convert_fusion), kind=kLoop, calls=%fused_computation.10 | loop fusion | flops 114688 | bytes 691968 | tf_op jit(solution)/shard_map/neg | solution.py:25
  41.5 0.3 collective-permute-start.13
  41.8 0.3 pad_maximum_fusion.2
  42.1 8.2 %collective-permute-done.4.refs_7_ = bf16[112,2048]{1,0:T(8,128)(2,1)S(1)} collective-permute-done((bf16[112,2048]{1,0:T(8,128)(2,1)S(1)}, bf16[112,2048]{1,0:T(8,128)(2,1)S(1)}, u32[]{:S(2)}, u32[]{:S(2)}) %collective-permute-start.4) | collective-permute-done | bytes 458784 | tf_op jit(solution)/shard_map/ppermute | solution.py:258
  50.3 0.7 collective-permute-start.1
  51.0 14.0 %collective-permute-done.6.refs_8_ = bf16[112,2048]{1,0:T(8,128)(2,1)S(1)} collective-permute-done((bf16[112,2048]{1,0:T(8,128)(2,1)S(1)}, bf16[112,2048]{1,0:T(8,128)(2,1)S(1)}, u32[]{:S(2)}, u32[]{:S(2)}) %collective-permute-start.6) | collective-permute-done | bytes 458784 | tf_op jit(solution)/shard_map/ppermute | solution.py:258
  64.9 1.3 collective-permute-start.17
  66.2 0.0 collective-permute-done.18.refs_6_
  66.2 4.0 %collective-permute-start.19 = (bf16[112,2048]{1,0:T(8,128)(2,1)S(1)}, bf16[112,2048]{1,0:T(8,128)(2,1)S(1)}, u32[]{:S(2)}, u32[]{:S(2)}) collective-permute-start(bf16[112,2048]{1,0:T(8,128)(2,1)S(1)} %collective-permute-done.18.refs_6_), channel_id=1, source_target_pairs={{4,20},{5,21},{6,22},{7,23},{12,28},{13,29},{14,30},{15,31},{20,4}... | collective-permute-start | bytes 1376264 | tf_op jit(solution)/shard_map/ppermute | solution.py:258
  70.3 0.0 collective-permute-done.15.refs_2_
  70.3 0.7 collective-permute-start.16
  71.0 3.2 %collective-permute-done.17.refs_5_ = bf16[112,2048]{1,0:T(8,128)(2,1)S(1)} collective-permute-done((bf16[112,2048]{1,0:T(8,128)(2,1)S(1)}, bf16[112,2048]{1,0:T(8,128)(2,1)S(1)}, u32[]{:S(2)}, u32[]{:S(2)}) %collective-permute-start.17) | collective-permute-done | bytes 458784 | tf_op jit(solution)/shard_map/ppermute | solution.py:258
  74.2 4.9 %collective-permute-done.19.refs_9_ = bf16[112,2048]{1,0:T(8,128)(2,1)S(1)} collective-permute-done((bf16[112,2048]{1,0:T(8,128)(2,1)S(1)}, bf16[112,2048]{1,0:T(8,128)(2,1)S(1)}, u32[]{:S(2)}, u32[]{:S(2)}) %collective-permute-start.19) | collective-permute-done | bytes 458784 | tf_op jit(solution)/shard_map/ppermute | solution.py:258
  79.1 0.5 collective-permute-start.14
  79.6 0.7 collective-permute-start.2
  80.3 1.9 %collective-permute-start.5 = (bf16[112,2048]{1,0:T(8,128)(2,1)S(1)}, bf16[112,2048]{1,0:T(8,128)(2,1)S(1)}, u32[]{:S(2)}, u32[]{:S(2)}) collective-permute-start(bf16[112,2048]{1,0:T(8,128)(2,1)S(1)} %collective-permute-done.4.refs_7_), channel_id=1, source_target_pairs={{4,20},{5,21},{6,22},{7,23},{12,28},{13,29},{14,30},{15,31},{20,4}... | collective-permute-start | bytes 1376264 | tf_op jit(solution)/shard_map/ppermute | solution.py:258
  82.2 3.4 %collective-permute-start.7 = (bf16[112,2048]{1,0:T(8,128)(2,1)S(1)}, bf16[112,2048]{1,0:T(8,128)(2,1)S(1)}, u32[]{:S(2)}, u32[]{:S(2)}) collective-permute-start(bf16[112,2048]{1,0:T(8,128)(2,1)S(1)} %collective-permute-done.6.refs_8_), channel_id=1, source_target_pairs={{4,20},{5,21},{6,22},{7,23},{12,28},{13,29},{14,30},{15,31},{20,4}... | collective-permute-start | bytes 1376264 | tf_op jit(solution)/shard_map/ppermute | solution.py:258
  85.7 7.8 %project_early.1.refs_12_ = bf16[672,1536]{1,0:T(8,128)(2,1)S(1)} custom-call(bf16[224,2048]{1,0:T(8,128)(2,1)S(1)} %bitcast.8, bf16[224,2048]{1,0:T(8,128)(2,1)} %collective-permute-done.refs_1_, bf16[224,2048]{1,0:T(8,128)(2,1)} %collective-permute-done.15.refs_2_, bf16[224,2048]{1,0:T(8,128)(2,1)S(1)} %collective-permute-done.16.refs_3_, ...), custom_call_target="tpu_custom_call" | custom-call | flops 4227858432 | bytes 10000000 | tf_op jit(solution)/shard_map/project_early/pallas_call | solution.py:311
  93.4 1.0 collective-permute-done.7.refs_3_
  94.4 10.4 %attend.1 = (bf16[224,512]{1,0:T(8,128)(2,1)S(1)}, bf16[224,512]{1,0:T(8,128)(2,1)S(1)}, bf16[224,512]{1,0:T(8,128)(2,1)S(1)}, bf16[224,512]{1,0:T(8,128)(2,1)S(1)}) custom-call(bf16[224,2048]{1,0:T(8,128)(2,1)S(1)} %collective-permute-done.1.refs_0_, bf16[224,2048]{1,0:T(8,128)(2,1)S(1)} %collective-permute-done.2.refs_1_, ...), custom_call_target="tpu_custom_call" | custom-call | flops 2818572288 | bytes 10000000 | tf_op jit(solution)/shard_map/attend/pallas_call | solution.py:329
  104.8 1.9 %collective-permute-start.20 = (bf16[224,512]{1,0:T(8,128)(2,1)S(1)}, bf16[224,512]{1,0:T(8,128)(2,1)S(1)}, u32[]{:S(2)}, u32[]{:S(2)}) collective-permute-start(bf16[224,512]{1,0:T(8,128)(2,1)S(1)} %get-tuple-element.15.own), channel_id=1, source_target_pairs={{6,20},{7,21},{14,28},{15,29},{20,6},{21,7},{28,14},{29,15}} | collective-permute-start | bytes 688136 | tf_op jit(solution)/shard_map/ppermute | solution.py:258
  106.8 0.1 collective-permute-start.21
  106.8 0.1 collective-permute-start.22
  106.9 3.5 %collective-permute-start.23 = (bf16[224,512]{1,0:T(8,128)(2,1)S(1)}, bf16[224,512]{1,0:T(8,128)(2,1)S(1)}, u32[]{:S(2)}, u32[]{:S(2)}) collective-permute-start(bf16[224,512]{1,0:T(8,128)(2,1)S(1)} %get-tuple-element.18), channel_id=1, source_target_pairs={{0,3},{1,2},{2,1},{3,0},{4,7},{5,6},{6,23},{7,22},{8,11},{9,10},{1... | collective-permute-start | bytes 688136 | tf_op jit(solution)/shard_map/ppermute | solution.py:258
  110.4 11.7 %collective-permute-done.20.refs_0_ = bf16[224,512]{1,0:T(8,128)(2,1)S(1)} collective-permute-done((bf16[224,512]{1,0:T(8,128)(2,1)S(1)}, bf16[224,512]{1,0:T(8,128)(2,1)S(1)}, u32[]{:S(2)}, u32[]{:S(2)}) %collective-permute-start.20) | collective-permute-done | bytes 229408 | tf_op jit(solution)/shard_map/ppermute | solution.py:258
  122.1 4.3 %collective-permute-done.21.refs_1_ = bf16[224,512]{1,0:T(8,128)(2,1)S(1)} collective-permute-done((bf16[224,512]{1,0:T(8,128)(2,1)S(1)}, bf16[224,512]{1,0:T(8,128)(2,1)S(1)}, u32[]{:S(2)}, u32[]{:S(2)}) %collective-permute-start.21) | collective-permute-done | bytes 229408 | tf_op jit(solution)/shard_map/ppermute | solution.py:258
  126.4 0.8 collective-permute-done.23.refs_3_
  127.1 1.0 join.1
  (19 shorter events, 0.1 us)
Async XLA Ops:
  1.8 11.8 %collective-permute-start.3 = (bf16[112,2048]{1,0:T(8,128)(2,1)}, bf16[112,2048]{1,0:T(8,128)(2,1)S(1)}, u32[]{:S(2)}, u32[]{:S(2)}) collective-permute-start(bf16[112,2048]{1,0:T(8,128)(2,1)} %dynamic-slice_bitcast_fusion.1), channel_id=1, source_target_pairs={{4,20},{5,21},{6,22},{7,23},{12,28},{13,29},{14,30},{15,31},{20,4}... | collective-permute-start | bytes 1376264 | tf_op jit(solution)/shard_map/ppermute | solution.py:258
  6.1 3.4 %copy-start = (bf16[1,224,2048]{2,1,0:T(8,128)(2,1)S(1)}, bf16[1,224,2048]{2,1,0:T(8,128)(2,1)}, u32[]{:S(2)}) copy-start(bf16[1,224,2048]{2,1,0:T(8,128)(2,1)} %param.5) | copy-start | bytes 2752516
  8.2 24.2 %collective-permute-start.9 = (bf16[256,1536]{1,0:T(8,128)(2,1)S(1)}, bf16[256,1536]{1,0:T(8,128)(2,1)S(1)}, u32[]{:S(2)}, u32[]{:S(2)}) collective-permute-start(bf16[256,1536]{1,0:T(8,128)(2,1)S(1)} %pad_maximum_fusion.refs_10_.refs_4_), channel_id=1, source_target_pairs={{0,8},{1,9},{2,10},{3,11},{4,12},{5,13},{6,14},{7,15},{8,0},{9,1},... | collective-permute-start | bytes 2359304 | tf_op jit(solution)/shard_map/ppermute | solution.py:258
  9.5 28.4 %collective-permute-start.8 = (bf16[256,1536]{1,0:T(8,128)(2,1)S(1)}, bf16[256,1536]{1,0:T(8,128)(2,1)}, u32[]{:S(2)}, u32[]{:S(2)}) collective-permute-start(bf16[256,1536]{1,0:T(8,128)(2,1)S(1)} %pad_maximum_fusion.refs_10_.refs_4_), channel_id=1, source_target_pairs={{0,4},{1,5},{2,6},{3,7},{4,0},{5,1},{6,2},{7,3},{8,12},{9,13},{10,... | collective-permute-start | bytes 2359304 | tf_op jit(solution)/shard_map/ppermute | solution.py:258
  9.5 32.0 %collective-permute-start = (bf16[224,2048]{1,0:T(8,128)(2,1)S(1)}, bf16[224,2048]{1,0:T(8,128)(2,1)}, u32[]{:S(2)}, u32[]{:S(2)}) collective-permute-start(bf16[224,2048]{1,0:T(8,128)(2,1)S(1)} %bitcast.6), channel_id=1, source_target_pairs={{0,1},{1,0},{2,3},{3,2},{8,9},{9,8},{10,11},{11,10},{16,17},{17,16... | collective-permute-start | bytes 2752520 | tf_op jit(solution)/shard_map/ppermute | solution.py:258
  11.1 59.2 %collective-permute-start.15 = (bf16[224,2048]{1,0:T(8,128)(2,1)S(1)}, bf16[224,2048]{1,0:T(8,128)(2,1)}, u32[]{:S(2)}, u32[]{:S(2)}) collective-permute-start(bf16[224,2048]{1,0:T(8,128)(2,1)S(1)} %bitcast.7), channel_id=1, source_target_pairs={{1,2},{2,1},{9,10},{10,9},{17,18},{18,17},{25,26},{26,25}} | collective-permute-start | bytes 2752520 | tf_op jit(solution)/shard_map/ppermute | solution.py:258
  13.7 16.3 %collective-permute-start.11 = (bf16[256,1536]{1,0:T(8,128)(2,1)S(1)}, bf16[256,1536]{1,0:T(8,128)(2,1)S(1)}, u32[]{:S(2)}, u32[]{:S(2)}) collective-permute-start(bf16[256,1536]{1,0:T(8,128)(2,1)S(1)} %pad_maximum_fusion.1), channel_id=1, source_target_pairs={{0,16},{1,17},{2,18},{3,19},{4,20},{5,21},{6,22},{7,23},{8,24},{9,... | collective-permute-start | bytes 2359304 | tf_op jit(solution)/shard_map/ppermute | solution.py:258
  30.0 20.2 %collective-permute-start.4 = (bf16[112,2048]{1,0:T(8,128)(2,1)S(1)}, bf16[112,2048]{1,0:T(8,128)(2,1)S(1)}, u32[]{:S(2)}, u32[]{:S(2)}) collective-permute-start(bf16[112,2048]{1,0:T(8,128)(2,1)S(1)} %broadcast_select_fusion.1), channel_id=1, source_target_pairs={{4,6},{5,7},{6,4},{7,5},{12,14},{13,15},{14,12},{15,13},{20,22},{2... | collective-permute-start | bytes 1376264 | tf_op jit(solution)/shard_map/ppermute | solution.py:258
  32.4 32.6 %collective-permute-start.6 = (bf16[112,2048]{1,0:T(8,128)(2,1)S(1)}, bf16[112,2048]{1,0:T(8,128)(2,1)S(1)}, u32[]{:S(2)}, u32[]{:S(2)}) collective-permute-start(bf16[112,2048]{1,0:T(8,128)(2,1)S(1)} %broadcast_select_fusion.1), channel_id=1, source_target_pairs={{4,7},{5,6},{6,5},{7,4},{12,15},{13,14},{14,13},{15,12},{20,23},{2... | collective-permute-start | bytes 1376264 | tf_op jit(solution)/shard_map/ppermute | solution.py:258
  37.8 47.8 %copy-start.1 = (bf16[2048]{0:T(1024)(128)(2,1)S(1)}, bf16[2048]{0:T(1024)(128)(2,1)}, u32[]{:S(2)}) copy-start(bf16[2048]{0:T(1024)(128)(2,1)} %param.6) | copy-start | bytes 12292
  37.8 28.4 %collective-permute-start.18 = (bf16[112,2048]{1,0:T(8,128)(2,1)S(1)}, bf16[112,2048]{1,0:T(8,128)(2,1)S(1)}, u32[]{:S(2)}, u32[]{:S(2)}) collective-permute-start(bf16[112,2048]{1,0:T(8,128)(2,1)S(1)} %get-tuple-element.19), channel_id=1, source_target_pairs={{4,5},{5,4},{6,7},{7,6},{12,13},{13,12},{14,15},{15,14},{20,21},{2... | collective-permute-start | bytes 1376264 | tf_op jit(solution)/shard_map/ppermute | solution.py:258
  41.5 37.6 %collective-permute-start.13 = (bf16[256,1536]{1,0:T(8,128)(2,1)S(1)}, bf16[256,1536]{1,0:T(8,128)(2,1)S(1)}, u32[]{:S(2)}, u32[]{:S(2)}) collective-permute-start(bf16[256,1536]{1,0:T(8,128)(2,1)S(1)} %collective-permute-done.11.refs_14_.refs_8_), channel_id=1, source_target_pairs={{0,8},{1,9},{2,10},{3,11},{4,12},{5,13},{6,14},{7,15},{8,0},{9,1},... | collective-permute-start | bytes 2359304 | tf_op jit(solution)/shard_map/ppermute | solution.py:258
  50.3 29.3 %collective-permute-start.1 = (bf16[224,2048]{1,0:T(8,128)(2,1)}, bf16[224,2048]{1,0:T(8,128)(2,1)S(1)}, u32[]{:S(2)}, u32[]{:S(2)}) collective-permute-start(bf16[224,2048]{1,0:T(8,128)(2,1)} %collective-permute-done.refs_1_), channel_id=1, source_target_pairs={{1,2},{2,1},{9,10},{10,9},{17,18},{18,17},{25,26},{26,25}} | collective-permute-start | bytes 2752520 | tf_op jit(solution)/shard_map/ppermute | solution.py:258
  64.9 9.2 %collective-permute-start.17 = (bf16[112,2048]{1,0:T(8,128)(2,1)S(1)}, bf16[112,2048]{1,0:T(8,128)(2,1)S(1)}, u32[]{:S(2)}, u32[]{:S(2)}) collective-permute-start(bf16[112,2048]{1,0:T(8,128)(2,1)S(1)} %get-tuple-element.20), channel_id=1, source_target_pairs={{4,20},{5,21},{12,28},{13,29},{22,6},{23,7},{30,14},{31,15}} | collective-permute-start | bytes 1376264 | tf_op jit(solution)/shard_map/ppermute | solution.py:258
  66.2 12.8 %collective-permute-start.19 = (bf16[112,2048]{1,0:T(8,128)(2,1)S(1)}, bf16[112,2048]{1,0:T(8,128)(2,1)S(1)}, u32[]{:S(2)}, u32[]{:S(2)}) collective-permute-start(bf16[112,2048]{1,0:T(8,128)(2,1)S(1)} %collective-permute-done.18.refs_6_), channel_id=1, source_target_pairs={{4,20},{5,21},{6,22},{7,23},{12,28},{13,29},{14,30},{15,31},{20,4}... | collective-permute-start | bytes 1376264 | tf_op jit(solution)/shard_map/ppermute | solution.py:258
  70.3 15.4 %collective-permute-start.16 = (bf16[224,2048]{1,0:T(8,128)(2,1)}, bf16[224,2048]{1,0:T(8,128)(2,1)S(1)}, u32[]{:S(2)}, u32[]{:S(2)}) collective-permute-start(bf16[224,2048]{1,0:T(8,128)(2,1)} %collective-permute-done.15.refs_2_), channel_id=1, source_target_pairs={{1,0},{2,3},{9,8},{10,11},{17,16},{18,19},{25,24},{26,27}} | collective-permute-start | bytes 2752520 | tf_op jit(solution)/shard_map/ppermute | solution.py:258
  74.1 6.2 %collective-permute-start.10 = (bf16[256,1536]{1,0:T(8,128)(2,1)S(1)}, bf16[256,1536]{1,0:T(8,128)(2,1)S(1)}, u32[]{:S(2)}, u32[]{:S(2)}) collective-permute-start(bf16[256,1536]{1,0:T(8,128)(2,1)S(1)} %collective-permute-done.9.refs_12_.refs_6_), channel_id=1, source_target_pairs={{0,4},{1,5},{2,6},{3,7},{4,0},{5,1},{6,2},{7,3},{8,12},{9,13},{10,... | collective-permute-start | bytes 2359304 | tf_op jit(solution)/shard_map/ppermute | solution.py:258
  79.1 3.2 %collective-permute-start.12 = (bf16[256,1536]{1,0:T(8,128)(2,1)S(1)}, bf16[256,1536]{1,0:T(8,128)(2,1)S(1)}, u32[]{:S(2)}, u32[]{:S(2)}) collective-permute-start(bf16[256,1536]{1,0:T(8,128)(2,1)S(1)} %collective-permute-done.11.refs_14_.refs_8_), channel_id=1, source_target_pairs={{0,4},{1,5},{2,6},{3,7},{4,0},{5,1},{6,2},{7,3},{8,12},{9,13},{10,... | collective-permute-start | bytes 2359304 | tf_op jit(solution)/shard_map/ppermute | solution.py:258
  79.1 6.6 %collective-permute-start.14 = (bf16[256,1536]{1,0:T(8,128)(2,1)S(1)}, bf16[256,1536]{1,0:T(8,128)(2,1)S(1)}, u32[]{:S(2)}, u32[]{:S(2)}) collective-permute-start(bf16[256,1536]{1,0:T(8,128)(2,1)S(1)} %collective-permute-done.13.refs_16_.refs_10_), channel_id=1, source_target_pairs={{0,4},{1,5},{2,6},{3,7},{4,0},{5,1},{6,2},{7,3},{8,12},{9,13},{10,... | collective-permute-start | bytes 2359304 | tf_op jit(solution)/shard_map/ppermute | solution.py:258
  79.6 14.9 %collective-permute-start.2 = (bf16[224,2048]{1,0:T(8,128)(2,1)S(1)}, bf16[224,2048]{1,0:T(8,128)(2,1)S(1)}, u32[]{:S(2)}, u32[]{:S(2)}) collective-permute-start(bf16[224,2048]{1,0:T(8,128)(2,1)S(1)} %collective-permute-done.1.refs_0_), channel_id=1, source_target_pairs={{1,0},{2,3},{9,8},{10,11},{17,16},{18,19},{25,24},{26,27}} | collective-permute-start | bytes 2752520 | tf_op jit(solution)/shard_map/ppermute | solution.py:258
  80.3 13.1 %collective-permute-start.5 = (bf16[112,2048]{1,0:T(8,128)(2,1)S(1)}, bf16[112,2048]{1,0:T(8,128)(2,1)S(1)}, u32[]{:S(2)}, u32[]{:S(2)}) collective-permute-start(bf16[112,2048]{1,0:T(8,128)(2,1)S(1)} %collective-permute-done.4.refs_7_), channel_id=1, source_target_pairs={{4,20},{5,21},{6,22},{7,23},{12,28},{13,29},{14,30},{15,31},{20,4}... | collective-permute-start | bytes 1376264 | tf_op jit(solution)/shard_map/ppermute | solution.py:258
  82.2 12.2 %collective-permute-start.7 = (bf16[112,2048]{1,0:T(8,128)(2,1)S(1)}, bf16[112,2048]{1,0:T(8,128)(2,1)S(1)}, u32[]{:S(2)}, u32[]{:S(2)}) collective-permute-start(bf16[112,2048]{1,0:T(8,128)(2,1)S(1)} %collective-permute-done.6.refs_8_), channel_id=1, source_target_pairs={{4,20},{5,21},{6,22},{7,23},{12,28},{13,29},{14,30},{15,31},{20,4}... | collective-permute-start | bytes 1376264 | tf_op jit(solution)/shard_map/ppermute | solution.py:258
  104.8 17.2 %collective-permute-start.20 = (bf16[224,512]{1,0:T(8,128)(2,1)S(1)}, bf16[224,512]{1,0:T(8,128)(2,1)S(1)}, u32[]{:S(2)}, u32[]{:S(2)}) collective-permute-start(bf16[224,512]{1,0:T(8,128)(2,1)S(1)} %get-tuple-element.15.own), channel_id=1, source_target_pairs={{6,20},{7,21},{14,28},{15,29},{20,6},{21,7},{28,14},{29,15}} | collective-permute-start | bytes 688136 | tf_op jit(solution)/shard_map/ppermute | solution.py:258
  106.8 19.6 %collective-permute-start.21 = (bf16[224,512]{1,0:T(8,128)(2,1)S(1)}, bf16[224,512]{1,0:T(8,128)(2,1)S(1)}, u32[]{:S(2)}, u32[]{:S(2)}) collective-permute-start(bf16[224,512]{1,0:T(8,128)(2,1)S(1)} %get-tuple-element.16), channel_id=1, source_target_pairs={{0,1},{1,0},{2,3},{3,2},{4,5},{5,4},{6,21},{7,20},{8,9},{9,8},{10,... | collective-permute-start | bytes 688136 | tf_op jit(solution)/shard_map/ppermute | solution.py:258
  106.8 19.5 %collective-permute-start.22 = (bf16[224,512]{1,0:T(8,128)(2,1)S(1)}, bf16[224,512]{1,0:T(8,128)(2,1)S(1)}, u32[]{:S(2)}, u32[]{:S(2)}) collective-permute-start(bf16[224,512]{1,0:T(8,128)(2,1)S(1)} %get-tuple-element.17), channel_id=1, source_target_pairs={{0,2},{1,3},{2,0},{3,1},{4,6},{5,7},{6,22},{7,23},{8,10},{9,11},{1... | collective-permute-start | bytes 688136 | tf_op jit(solution)/shard_map/ppermute | solution.py:258
  106.9 20.2 %collective-permute-start.23 = (bf16[224,512]{1,0:T(8,128)(2,1)S(1)}, bf16[224,512]{1,0:T(8,128)(2,1)S(1)}, u32[]{:S(2)}, u32[]{:S(2)}) collective-permute-start(bf16[224,512]{1,0:T(8,128)(2,1)S(1)} %get-tuple-element.18), channel_id=1, source_target_pairs={{0,3},{1,2},{2,1},{3,0},{4,7},{5,6},{6,23},{7,22},{8,11},{9,10},{1... | collective-permute-start | bytes 688136 | tf_op jit(solution)/shard_map/ppermute | solution.py:258

commit v4 on v2

v4 whole, which is shorter than its diff:
```python
import functools
import math

import jax
import jax.numpy as jnp
from jax import lax
from jax.experimental import pallas as pl
from jax.experimental.pallas import tpu as pltpu
from jax.sharding import PartitionSpec as P

HEADS = 16
HEAD_DIM = 128
HALF = HEAD_DIM // 2
EPS = 1e-05
VMEM_LIMIT = 28 * 1024 * 1024


def tables(length):
    freqs = 10000.0 ** (-(jnp.arange(HALF).astype(jnp.float32) * 2.0) / HEAD_DIM)
    angles = jnp.arange(length).astype(jnp.float32)[:, None] * freqs[None, :]
    cosine = jnp.cos(angles)
    sine = jnp.sin(angles)
    return (
        jnp.concatenate([cosine, cosine], axis=1),
        jnp.concatenate([-sine, sine], axis=1),
    )


def normalize(block, gain):
    rows = block.astype(jnp.float32)
    scale = lax.rsqrt(jnp.mean(rows * rows, axis=1, keepdims=True) + EPS)
    return (rows * scale * gain.astype(jnp.float32)).astype(jnp.bfloat16)


def role(rows):
    d, c = lax.axis_index("dp"), lax.axis_index("ctx")
    home = c // 2 == d % 2
    return {
        "home": home,
        "starts": [pl.multiple_of((c ^ i) * rows, rows) for i in range(4)],
        "base": jnp.where(home, c, c ^ 2),
        "owner": d,
    }


def early_kernel(rows, cols, *refs):
    kept, sent, shards = refs[:4], refs[4:8], refs[8:14]
    gain, out, tail, held, normed, weights, token_sems, weight_sems = refs[14:]
    me = role(rows)
    depth = shards[0].shape[0]
    loads = []
    for i in range(4):
        slot = held.at[pl.ds(i * rows, rows)]
        for condition, source in ((me["home"], kept[i]), (jnp.logical_not(me["home"]), sent[i])):

            @pl.when(condition)
            def _(source=source, slot=slot, i=i):
                pltpu.make_async_copy(source, slot, token_sems.at[i]).start()

        loads.append(pltpu.make_async_copy(kept[i], slot, token_sems.at[i]))
    weight_loads = []
    for i, shard in enumerate(shards):
        load = pltpu.make_async_copy(shard, weights.at[pl.ds(i * depth, depth)], weight_sems.at[i])
        load.start()
        weight_loads.append(load)
    for i in range(4):
        loads[i].wait()
        part = pl.ds(i * rows, rows)
        value = normalize(held[part, :], gain[...])
        for owner in range(8):
            offset = me["owner"] ^ owner
            place = jnp.where(offset < 3, offset, jnp.where(offset < 5, offset + 3, offset - 2))
            lane = pl.ds(pl.multiple_of(place * depth, depth), depth)
            normed[part, lane] = value[:, owner * depth : (owner + 1) * depth]
    for load in weight_loads:
        load.wait()
    first = len(shards) * depth
    tail[...] = normed[:, first:]
    step = 2 * HEAD_DIM
    for lane in range(0, 3 * cols, step):
        out[:, lane : lane + step] = jnp.dot(
            normed[:, :first], weights[:, lane : lane + step], preferred_element_type=jnp.float32
        )


def late_kernel(rows, cols, total, *refs):
    shards = refs[:2]
    partial, tail, cos_ref, sin_ref = refs[2:6]
    outs = refs[6 : 6 + total]
    weights, qkv, result, weight_sems, out_sems = refs[6 + total :]
    me = role(rows)
    depth = shards[0].shape[0]
    loads = []
    for i, shard in enumerate(shards):
        load = pltpu.make_async_copy(shard, weights.at[pl.ds(i * depth, depth)], weight_sems.at[i])
        load.start()
        loads.append(load)
    for load in loads:
        load.wait()
    step = 2 * HEAD_DIM
    for first in range(0, 3 * cols, step):
        linear = partial[:, first : first + step] + jnp.dot(
            tail[...], weights[:, first : first + step], preferred_element_type=jnp.float32
        )
        for i, start in enumerate(me["starts"]):
            part = linear[i * rows : (i + 1) * rows]
            if first < 2 * cols:
                cosine = cos_ref[pl.ds(start, rows), :]
                sine = sin_ref[pl.ds(start, rows), :]
                heads = [part[:, h * HEAD_DIM : (h + 1) * HEAD_DIM] for h in range(2)]
                part = jnp.concatenate(
                    [x * cosine + pltpu.roll(x, HALF, 1) * sine for x in heads], axis=1
                )
            qkv[pl.ds(start, rows), first : first + step] = part.astype(jnp.bfloat16)
    attend(qkv, result, me["base"], total, rows, cols)
    copies = []
    for k in range(total):
        copy = pltpu.make_async_copy(result.at[k], outs[k], out_sems.at[k])
        copy.start()
        copies.append(copy)
    for copy in copies:
        copy.wait()


def attend(qkv, result, me, total, rows, cols):
    factor = HEAD_DIM ** (-0.5) * math.log2(math.e)
    below = lax.broadcasted_iota(jnp.int32, (rows, rows), 0) >= lax.broadcasted_iota(
        jnp.int32, (rows, rows), 1
    )

    def scored(q, k):
        return lax.dot_general(q, k, (((1,), (1,)), ((), ())), preferred_element_type=jnp.float32)

    for block in range(total):
        own, past = slice(block * rows, (block + 1) * rows), slice(0, block * rows)
        for head in range(cols // HEAD_DIM):
            lane = slice(head * HEAD_DIM, (head + 1) * HEAD_DIM)
            k_lane = slice(cols + lane.start, cols + lane.stop)
            v_lane = slice(2 * cols + lane.start, 2 * cols + lane.stop)
            q = qkv[own, lane]
            near = jnp.where(below, scored(q, qkv[own, k_lane]), -1e30)
            top = jnp.max(near, axis=1, keepdims=True)
            if block:
                far = scored(q, qkv[past, k_lane])
                top = jnp.maximum(top, jnp.max(far, axis=1, keepdims=True))
            top = top * factor
            expo = jnp.exp2(near * factor - top)
            bottom = jnp.sum(expo, axis=1, keepdims=True)
            numer = jnp.dot(expo.astype(jnp.bfloat16), qkv[own, v_lane], preferred_element_type=jnp.float32)
            if block:
                expo = jnp.exp2(far * factor - top)
                bottom += jnp.sum(expo, axis=1, keepdims=True)
                numer += jnp.dot(
                    expo.astype(jnp.bfloat16), qkv[past, v_lane], preferred_element_type=jnp.float32
                )
            result[block ^ me, :, lane] = (numer / bottom).astype(jnp.bfloat16)


def join_kernel(cols, total, own, *refs):
    pieces, out = refs[:total], refs[total]
    d, c = lax.axis_index("dp"), lax.axis_index("ctx")
    group = d % 2
    for k in range(total):
        base = c ^ k
        same = base // 2 == group
        plane = jnp.where(same, base, base ^ 2)
        core = jnp.where(same, group, 1 - group)
        lane = pl.ds(pl.multiple_of((2 * (plane % 2) + core) * cols, cols), cols)
        if k:
            out[0, :, lane] = pieces[k][...]
        else:
            out[0, :, lane] = jnp.where(c // 2 == group, own[...], pieces[k][...])


def fast(dp, ctx, tokens, norm_gain, q_weight, k_weight, v_weight):
    rows, features = tokens.shape[1], tokens.shape[2]
    cols = HEADS // ctx * HEAD_DIM
    every = [(d, c) for d in range(dp) for c in range(ctx)]

    def send(name, value, to):
        perm = [
            (d * ctx + c, to(d, c)[0] * ctx + to(d, c)[1]) for d, c in every if to(d, c) is not None
        ]
        with jax.named_scope(name):
            return lax.ppermute(value, ("dp", "ctx"), perm)

    def home(to):
        return lambda d, c: to(d, c) if c // 2 == d % 2 else None

    def away(to):
        return lambda d, c: to(d, c) if c // 2 != d % 2 else None

    d, c = lax.axis_index("dp"), lax.axis_index("ctx")

    def columns(heads):
        return jnp.concatenate(
            [lax.dynamic_slice_in_dim(w, heads * cols, cols, 1) for w in (q_weight, k_weight, v_weight)],
            axis=1,
        )

    own = tokens[0]
    heads = 2 * (c % 2) + d % 2
    core = lambda d, c: (d ^ 1, c)
    along_x = lambda d, c: (d ^ 2, c)
    along_y = lambda d, c: (d ^ 4, c)
    barrier = lambda *values: lax.optimization_barrier(values)
    kept, sent, w = {0: own}, {}, {}
    kept[1] = send("tokens_1", own, home(lambda d, c: (d, c ^ 1)))
    kept[2] = send("tokens_2", own, away(lambda d, c: (d, c ^ 2)))
    w[1] = send("weights_core", columns(heads ^ 1), core)
    w[0] = columns(heads)
    w[2] = send("weights_x", w[0], along_x)
    w[5] = send("weights_core_y", w[1], along_y)
    sent[0] = send("tokens_core_0", own, home(core))
    w[2], w[5], kept[1], sent[0] = barrier(w[2], w[5], kept[1], sent[0])
    w[6] = send("weights_xy", w[2], along_y)
    w[7] = send("weights_core_yx", w[5], along_x)
    sent[1] = send("tokens_core_1", kept[1], home(core))
    kept[2], w[2] = barrier(kept[2], w[2])
    kept[3] = send("tokens_3", kept[2], home(lambda d, c: (d, c ^ 1)))
    sent[2] = send("tokens_core_2", kept[2], home(core))
    sent[1], sent[2], w[0], w[1] = barrier(sent[1], sent[2], w[0], w[1])
    w[4] = send("weights_y", w[0], along_y)
    w[3] = send("weights_core_x", w[1], along_x)
    sent[3] = send("tokens_core_3", kept[3], home(core))
    kept, sent = [kept[i] for i in range(4)], [sent[i] for i in range(4)]
    cosine, sine = tables(ctx * rows)

    gain = norm_gain[None, :]
    any_space = pl.BlockSpec(memory_space=pl.ANY)
    vmem = pl.BlockSpec(memory_space=pltpu.VMEM)
    depth = q_weight.shape[0]
    partial, tail = pl.pallas_call(
        functools.partial(early_kernel, rows, cols),
        out_shape=[
            jax.ShapeDtypeStruct((ctx * rows, 3 * cols), jnp.float32),
            jax.ShapeDtypeStruct((ctx * rows, 2 * depth), jnp.bfloat16),
        ],
        in_specs=[any_space] * 14 + [vmem],
        out_specs=[vmem] * 2,
        scratch_shapes=[
            pltpu.VMEM((ctx * rows, features), jnp.bfloat16),
            pltpu.VMEM((ctx * rows, features), jnp.bfloat16),
            pltpu.VMEM((6 * depth, 3 * cols), jnp.bfloat16),
            pltpu.SemaphoreType.DMA((4,)),
            pltpu.SemaphoreType.DMA((6,)),
        ],
        compiler_params=pltpu.CompilerParams(vmem_limit_bytes=VMEM_LIMIT),
        cost_estimate=pl.CostEstimate(
            flops=2 * ctx * rows * 6 * depth * 3 * cols, bytes_accessed=10_000_000, transcendentals=0
        ),
        name="project_early",
    )(*kept, *sent, *[w[k] for k in (0, 1, 2, 5, 6, 7)], gain)
    pieces = pl.pallas_call(
        functools.partial(late_kernel, rows, cols, ctx),
        out_shape=[jax.ShapeDtypeStruct((rows, cols), jnp.bfloat16)] * ctx,
        in_specs=[any_space] * 2 + [vmem] * 4,
        out_specs=[any_space] * ctx,
        scratch_shapes=[
            pltpu.VMEM((2 * depth, 3 * cols), jnp.bfloat16),
            pltpu.VMEM((ctx * rows, 3 * cols), jnp.bfloat16),
            pltpu.VMEM((ctx, rows, cols), jnp.bfloat16),
            pltpu.SemaphoreType.DMA((2,)),
            pltpu.SemaphoreType.DMA((ctx,)),
        ],
        compiler_params=pltpu.CompilerParams(vmem_limit_bytes=VMEM_LIMIT),
        cost_estimate=pl.CostEstimate(
            flops=8_000_000_000, bytes_accessed=10_000_000, transcendentals=2_000_000
        ),
        name="attend",
    )(w[3], w[4], partial, tail, cosine, sine)

    def back(k):
        def to(d, c):
            base = c if c // 2 == d % 2 else c ^ 2
            target = ((d & 6) | (c // 2), base ^ k)
            return None if target == (d, c) else target

        return to

    arrived = [send(f"back_{k}", pieces[k], back(k)) for k in range(ctx)]
    return pl.pallas_call(
        functools.partial(join_kernel, cols, ctx),
        out_shape=jax.ShapeDtypeStruct((1, rows, ctx * cols), jnp.bfloat16),
        in_specs=[vmem] * (ctx + 1),
        out_specs=vmem,
        compiler_params=pltpu.CompilerParams(vmem_limit_bytes=8 * 1024 * 1024),
        name="join",
    )(pieces[0], *arrived)


def rotate(values, positions):
    heads = values.shape[1] // HEAD_DIM
    shaped = values.reshape(values.shape[0], heads, HEAD_DIM)
    freqs = 10000.0 ** (-(jnp.arange(HALF).astype(jnp.float32) * 2.0) / HEAD_DIM)
    angles = positions[:, None] * freqs[None, :]
    cosine = jnp.cos(angles)[:, None, :]
    sine = jnp.sin(angles)[:, None, :]
    first = shaped[:, :, :HALF]
    second = shaped[:, :, HALF:]
    return jnp.concatenate(
        [first * cosine - second * sine, second * cosine + first * sine], axis=2
    )


def general(dp, ctx, tokens, norm_gain, q_weight, k_weight, v_weight):
    rows = tokens.shape[1]
    heads = HEADS // ctx
    cols = heads * HEAD_DIM
    me = lax.axis_index("ctx")
    part = jnp.concatenate(
        [lax.dynamic_slice_in_dim(w, me * cols, cols, 1) for w in (q_weight, k_weight, v_weight)], axis=1
    )
    weights = lax.all_gather(part, "dp", axis=0, tiled=True)
    whole = lax.all_gather(tokens[0], "ctx", axis=0, tiled=True)
    normed = normalize(whole, norm_gain[None, :])
    linear = jnp.dot(normed, weights, preferred_element_type=jnp.float32)
    length = ctx * rows
    positions = jnp.arange(length).astype(jnp.float32)
    q = rotate(linear[:, :cols], positions).astype(jnp.bfloat16)
    k = rotate(linear[:, cols : 2 * cols], positions).astype(jnp.bfloat16)
    v = linear[:, 2 * cols :].astype(jnp.bfloat16).reshape(length, heads, HEAD_DIM)
    allowed = jnp.arange(length)[None, :] <= jnp.arange(length)[:, None]
    scores = jnp.einsum("qhd,khd->hqk", q, k, preferred_element_type=jnp.float32) * HEAD_DIM ** (-0.5)
    scores = jnp.where(allowed[None], scores, -1e30)
    top = jnp.max(scores, axis=2, keepdims=True)
    expo = jnp.where(allowed[None], jnp.exp(scores - top), 0.0)
    numer = jnp.einsum("hqk,khd->hqd", expo.astype(jnp.bfloat16), v, preferred_element_type=jnp.float32)
    result = (numer / jnp.sum(expo, axis=2, keepdims=True)).astype(jnp.bfloat16)
    result = result.reshape(heads, ctx, rows, HEAD_DIM).transpose(1, 2, 0, 3).reshape(ctx, rows, cols)
    back = lax.all_to_all(result, "ctx", 0, 0)
    return back.transpose(1, 0, 2).reshape(1, rows, ctx * cols)


def solution(mesh):
    dp, ctx = mesh.shape["dp"], mesh.shape["ctx"]
    body = fast if (dp, ctx) == (8, 4) else general
    placed = (P("dp", "ctx", None), P(), P("dp", None), P("dp", None), P("dp", None))
    return jax.shard_map(
        functools.partial(body, dp, ctx),
        mesh=mesh,
        in_specs=placed,
        out_specs=P("dp", "ctx", None),
        check_vma=False,
    )
```

time: 102 us -> 99.2 us (0.973)
  the two profiles are of different devices: /device:TPU:0 before, /device:TPU:1 now
where the time goes in v4:
time: 99.2 us; the launch traced here: 98.9 us
  waiting for transfers between devices  39.6 us (40%)
  starting transfers between devices  37.6 us (38%)
  Pallas kernels  16.9 us (17%)
  local copies, waits for them, and re-layouts  2.45 us (2%)
  other arithmetic  2.09 us (2%)
    ppermute x18, waiting for transfers between devices, send(): return lax.ppermute(value, ('dp', 'ctx'), perm)  39.6 us
    ppermute x18, starting transfers between devices, send(): return lax.ppermute(value, ('dp', 'ctx'), perm)  37.6 us
    pallas_call x1, Pallas kernels, fast(): pl.pallas_call(functools.partial(late_kernel, rows, cols, ctx), out_shape...  8.13 us
    pallas_call x1, Pallas kernels, fast(): pl.pallas_call(functools.partial(early_kernel, rows, cols), out_shape=[ja...  7.79 us
    dynamic_slice x2, local copies, waits for them, and re-layouts, columns(): lax.dynamic_slice_in_dim(w, heads * cols, cols, 1)  2.43 us
  transfers between devices with their start and end apart: 18, of which 9 were waited for; matrix products, arithmetic and copies ran while one was open for 2% of the time, Pallas kernels for 8%

profile of v4, /device:TPU:1, one launch (start us, length us, event | category | flops | bytes accessed | tf_op | source)
XLA Modules:
  0.0 98.9 jit_solution(9374930898589524357)
XLA Ops:
  0.0 1.1 %constant_dynamic-slice_fusion.2 = (bf16[256,512]{1,0:T(8,128)(2,1)S(1)}, bf16[256,512]{1,0:T(8,128)(2,1)S(1)}) fusion(bf16[256,2048]{1,0:T(8,128)(2,1)} %param.7, s32[]{:T(128)S(6)} %select_n.24, s32[]{:T(128)S(6)} %select_n.23), kind=kLoop, calls=%fused_computation.10 | loop fusion | bytes 1048584 | tf_op jit(solution)/shard_map/dynamic_slice | solution.py:197
  1.1 0.0 copy-start
  1.1 1.4 %constant_dynamic-slice_fusion = (bf16[256,512]{1,0:T(8,128)(2,1)S(1)}, bf16[256,512]{1,0:T(8,128)(2,1)S(1)}, bf16[256,512]{1,0:T(8,128)(2,1)S(1)}, bf16[256,512]{1,0:T(8,128)(2,1)S(1)}) fusion(bf16[256,2048]{1,0:T(8,128)(2,1)} %param.9, s32[]{:T(128)S(6)} %select_n.24, s32[]{:T(128)S(6)} %select_n.23, bf16[256,2048]{1,0:T(8,128)(2,1)} %param.8), kind=kLoop, calls=%fused_computation.8 | loop fusion | bytes 2097160 | tf_op jit(solution)/shard_map/dynamic_slice | solution.py:197
  2.5 0.0 copy-start.1
  2.5 0.1 pad_maximum_fusion.1
  2.5 0.1 collective-permute-start.1
  2.7 0.0 copy-done
  2.7 0.7 collective-permute-start.3
  3.4 1.3 %collective-permute-start.4 = (bf16[224,2048]{1,0:T(8,128)(2,1)S(1)}, bf16[224,2048]{1,0:T(8,128)(2,1)S(1)}, u32[]{:S(2)}, u32[]{:S(2)}) collective-permute-start(bf16[224,2048]{1,0:T(8,128)(2,1)S(1)} %bitcast.2), channel_id=1, source_target_pairs={{0,4},{1,5},{6,2},{7,3},{8,12},{9,13},{14,10},{15,11},{16,20},{17,... | collective-permute-start | bytes 2752520 | tf_op jit(solution)/shard_map/tokens_core_0/ppermute | solution.py:185
  4.7 8.3 %collective-permute-start.6 = (bf16[224,2048]{1,0:T(8,128)(2,1)S(1)}, bf16[224,2048]{1,0:T(8,128)(2,1)S(1)}, u32[]{:S(2)}, u32[]{:S(2)}) collective-permute-start(bf16[224,2048]{1,0:T(8,128)(2,1)S(1)} %bitcast.3), channel_id=1, source_target_pairs={{2,0},{3,1},{4,6},{5,7},{10,8},{11,9},{12,14},{13,15},{18,16},{19,... | collective-permute-start | bytes 2752520 | tf_op jit(solution)/shard_map/tokens_2/ppermute | solution.py:185
  12.9 0.1 pad_maximum_fusion.refs_8_
  13.0 1.3 %collective-permute-start = (bf16[256,1536]{1,0:T(8,128)(2,1)S(1)}, bf16[256,1536]{1,0:T(8,128)(2,1)S(1)}, u32[]{:S(2)}, u32[]{:S(2)}) collective-permute-start(bf16[256,1536]{1,0:T(8,128)(2,1)S(1)} %pad_maximum_fusion.refs_8_), channel_id=1, source_target_pairs={{0,8},{1,9},{2,10},{3,11},{4,12},{5,13},{6,14},{7,15},{8,0},{9,1},... | collective-permute-start | bytes 2359304 | tf_op jit(solution)/shard_map/weights_x/ppermute | solution.py:185
  14.3 0.0 collective-permute-done.1.refs_9_
  14.3 1.2 %collective-permute-start.2 = (bf16[256,1536]{1,0:T(8,128)(2,1)S(1)}, bf16[256,1536]{1,0:T(8,128)(2,1)S(1)}, u32[]{:S(2)}, u32[]{:S(2)}) collective-permute-start(bf16[256,1536]{1,0:T(8,128)(2,1)S(1)} %collective-permute-done.1.refs_9_), channel_id=1, source_target_pairs={{0,16},{1,17},{2,18},{3,19},{4,20},{5,21},{6,22},{7,23},{8,24},{9,... | collective-permute-start | bytes 2359304 | tf_op jit(solution)/shard_map/weights_core_y/ppermute | solution.py:185
  15.5 14.9 %collective-permute-done.refs_10_ = bf16[256,1536]{1,0:T(8,128)(2,1)S(1)} collective-permute-done((bf16[256,1536]{1,0:T(8,128)(2,1)S(1)}, bf16[256,1536]{1,0:T(8,128)(2,1)S(1)}, u32[]{:S(2)}, u32[]{:S(2)}) %collective-permute-start) | collective-permute-done | bytes 786464 | tf_op jit(solution)/shard_map/weights_x/ppermute | solution.py:185
  30.4 0.0 collective-permute-done.3.refs_1_
  30.4 0.0 collective-permute-done.4.refs_4_
  30.4 1.5 %collective-permute-done.2.refs_11_ = bf16[256,1536]{1,0:T(8,128)(2,1)S(1)} collective-permute-done((bf16[256,1536]{1,0:T(8,128)(2,1)S(1)}, bf16[256,1536]{1,0:T(8,128)(2,1)S(1)}, u32[]{:S(2)}, u32[]{:S(2)}) %collective-permute-start.2) | collective-permute-done | bytes 786464 | tf_op jit(solution)/shard_map/weights_core_y/ppermute | solution.py:185
  31.9 0.0 collective-permute-done.6.refs_2_
  31.9 0.7 collective-permute-start.10
  32.6 1.3 %collective-permute-start.7 = (bf16[224,2048]{1,0:T(8,128)(2,1)S(1)}, bf16[224,2048]{1,0:T(8,128)(2,1)S(1)}, u32[]{:S(2)}, u32[]{:S(2)}) collective-permute-start(bf16[224,2048]{1,0:T(8,128)(2,1)S(1)} %collective-permute-done.6.refs_2_), channel_id=1, source_target_pairs={{0,4},{1,5},{6,2},{7,3},{8,12},{9,13},{14,10},{15,11},{16,20},{17,... | collective-permute-start | bytes 2752520 | tf_op jit(solution)/shard_map/tokens_core_2/ppermute | solution.py:185
  33.9 1.3 %collective-permute-start.5 = (bf16[224,2048]{1,0:T(8,128)(2,1)S(1)}, bf16[224,2048]{1,0:T(8,128)(2,1)S(1)}, u32[]{:S(2)}, u32[]{:S(2)}) collective-permute-start(bf16[224,2048]{1,0:T(8,128)(2,1)S(1)} %collective-permute-done.3.refs_1_), channel_id=1, source_target_pairs={{0,4},{1,5},{6,2},{7,3},{8,12},{9,13},{14,10},{15,11},{16,20},{17,... | collective-permute-start | bytes 2752520 | tf_op jit(solution)/shard_map/tokens_core_1/ppermute | solution.py:185
  35.2 0.0 collective-permute-done.10.refs_3_
  35.2 1.3 %collective-permute-start.11 = (bf16[224,2048]{1,0:T(8,128)(2,1)S(1)}, bf16[224,2048]{1,0:T(8,128)(2,1)S(1)}, u32[]{:S(2)}, u32[]{:S(2)}) collective-permute-start(bf16[224,2048]{1,0:T(8,128)(2,1)S(1)} %collective-permute-done.10.refs_3_), channel_id=1, source_target_pairs={{0,4},{1,5},{6,2},{7,3},{8,12},{9,13},{14,10},{15,11},{16,20},{17,... | collective-permute-start | bytes 2752520 | tf_op jit(solution)/shard_map/tokens_core_3/ppermute | solution.py:185
  36.5 1.3 %collective-permute-start.12 = (bf16[256,1536]{1,0:T(8,128)(2,1)S(1)}, bf16[256,1536]{1,0:T(8,128)(2,1)S(1)}, u32[]{:S(2)}, u32[]{:S(2)}) collective-permute-start(bf16[256,1536]{1,0:T(8,128)(2,1)S(1)} %collective-permute-done.refs_10_), channel_id=1, source_target_pairs={{0,16},{1,17},{2,18},{3,19},{4,20},{5,21},{6,22},{7,23},{8,24},{9,... | collective-permute-start | bytes 2359304 | tf_op jit(solution)/shard_map/weights_xy/ppermute | solution.py:185
  37.9 0.3 collective-permute-start.13
  38.1 1.8 %collective-permute-done.7.refs_6_ = bf16[224,2048]{1,0:T(8,128)(2,1)S(1)} collective-permute-done((bf16[224,2048]{1,0:T(8,128)(2,1)S(1)}, bf16[224,2048]{1,0:T(8,128)(2,1)S(1)}, u32[]{:S(2)}, u32[]{:S(2)}) %collective-permute-start.7) | collective-permute-done | bytes 917536 | tf_op jit(solution)/shard_map/tokens_core_2/ppermute | solution.py:185
  39.9 1.4 %collective-permute-done.5.refs_5_ = bf16[224,2048]{1,0:T(8,128)(2,1)S(1)} collective-permute-done((bf16[224,2048]{1,0:T(8,128)(2,1)S(1)}, bf16[224,2048]{1,0:T(8,128)(2,1)S(1)}, u32[]{:S(2)}, u32[]{:S(2)}) %collective-permute-start.5) | collective-permute-done | bytes 917536 | tf_op jit(solution)/shard_map/tokens_core_1/ppermute | solution.py:185
  41.3 1.4 %collective-permute-start.8 = (bf16[256,1536]{1,0:T(8,128)(2,1)S(1)}, bf16[256,1536]{1,0:T(8,128)(2,1)S(1)}, u32[]{:S(2)}, u32[]{:S(2)}) collective-permute-start(bf16[256,1536]{1,0:T(8,128)(2,1)S(1)} %collective-permute-done.1.refs_9_), channel_id=1, source_target_pairs={{0,8},{1,9},{2,10},{3,11},{4,12},{5,13},{6,14},{7,15},{8,0},{9,1},... | collective-permute-start | bytes 2359304 | tf_op jit(solution)/shard_map/weights_core_x/ppermute | solution.py:185
  42.7 1.2 %collective-permute-start.9 = (bf16[256,1536]{1,0:T(8,128)(2,1)S(1)}, bf16[256,1536]{1,0:T(8,128)(2,1)S(1)}, u32[]{:S(2)}, u32[]{:S(2)}) collective-permute-start(bf16[256,1536]{1,0:T(8,128)(2,1)S(1)} %pad_maximum_fusion.refs_8_), channel_id=1, source_target_pairs={{0,16},{1,17},{2,18},{3,19},{4,20},{5,21},{6,22},{7,23},{8,24},{9,... | collective-permute-start | bytes 2359304 | tf_op jit(solution)/shard_map/weights_y/ppermute | solution.py:185
  43.9 1.7 %fusion = (f32[896,64]{1,0:T(8,128)S(1)}, f32[896,64]{1,0:T(8,128)S(1)}, f32[896,64]{1,0:T(8,128)S(1)}) fusion(f32[64]{0:T(128)S(1)} %multiply_power_fusion, f32[896]{0:T(1024)S(1)} %iota_convert_fusion), kind=kLoop, calls=%fused_computation.6 | loop fusion | flops 114688 | bytes 691968 | tf_op jit(solution)/shard_map/neg | solution.py:25
  45.6 0.3 pad_maximum_fusion.2
  45.9 1.8 %collective-permute-done.12.refs_12_ = bf16[256,1536]{1,0:T(8,128)(2,1)S(1)} collective-permute-done((bf16[256,1536]{1,0:T(8,128)(2,1)S(1)}, bf16[256,1536]{1,0:T(8,128)(2,1)S(1)}, u32[]{:S(2)}, u32[]{:S(2)}) %collective-permute-start.12) | collective-permute-done | bytes 786464 | tf_op jit(solution)/shard_map/weights_xy/ppermute | solution.py:185
  47.7 1.2 %collective-permute-done.13.refs_13_ = bf16[256,1536]{1,0:T(8,128)(2,1)S(1)} collective-permute-done((bf16[256,1536]{1,0:T(8,128)(2,1)S(1)}, bf16[256,1536]{1,0:T(8,128)(2,1)S(1)}, u32[]{:S(2)}, u32[]{:S(2)}) %collective-permute-start.13) | collective-permute-done | bytes 786464 | tf_op jit(solution)/shard_map/weights_core_yx/ppermute | solution.py:185
  49.0 4.3 %collective-permute-done.11.refs_7_ = bf16[224,2048]{1,0:T(8,128)(2,1)S(1)} collective-permute-done((bf16[224,2048]{1,0:T(8,128)(2,1)S(1)}, bf16[224,2048]{1,0:T(8,128)(2,1)S(1)}, u32[]{:S(2)}, u32[]{:S(2)}) %collective-permute-start.11) | collective-permute-done | bytes 917536 | tf_op jit(solution)/shard_map/tokens_core_3/ppermute | solution.py:185
  53.3 7.8 %project_early.1 = (f32[896,1536]{1,0:T(8,128)S(1)}, bf16[896,512]{1,0:T(8,128)(2,1)S(1)}) custom-call(bf16[224,2048]{1,0:T(8,128)(2,1)S(1)} %bitcast.4, bf16[224,2048]{1,0:T(8,128)(2,1)S(1)} %collective-permute-done.3.refs_1_, bf16[224,2048]{1,0:T(8,128)(2,1)S(1)} %collective-permute-done.6.refs_2_, bf16[224,2048]{1,0:T(8,128)(2,1)S(1)} %collective-permute-done.10.refs_3_, ...), custom_call_target="tpu_custom_call" | custom-call | flops 4227858432 | bytes 10000000 | tf_op jit(solution)/shard_map/project_early/pallas_call | solution.py:233
  61.1 0.0 collective-permute-done.8.refs_0_
  61.1 0.0 collective-permute-done.9.refs_1_
  61.1 8.1 %attend.1 = (bf16[224,512]{1,0:T(8,128)(2,1)S(1)}, bf16[224,512]{1,0:T(8,128)(2,1)S(1)}, bf16[224,512]{1,0:T(8,128)(2,1)S(1)}, bf16[224,512]{1,0:T(8,128)(2,1)S(1)}) custom-call(bf16[256,1536]{1,0:T(8,128)(2,1)S(1)} %collective-permute-done.8.refs_0_, bf16[256,1536]{1,0:T(8,128)(2,1)S(1)} %collective-permute-done.9.refs_1_, ...), custom_call_target="tpu_custom_call" | custom-call | flops 8000000000 | bytes 10000000 | tf_op jit(solution)/shard_map/attend/pallas_call | solution.py:254
  69.2 7.6 %collective-permute-start.14 = (bf16[224,512]{1,0:T(8,128)(2,1)S(1)}, bf16[224,512]{1,0:T(8,128)(2,1)S(1)}, u32[]{:S(2)}, u32[]{:S(2)}) collective-permute-start(bf16[224,512]{1,0:T(8,128)(2,1)S(1)} %get-tuple-element.33.own), channel_id=1, source_target_pairs={{2,4},{3,5},{4,2},{5,3},{10,12},{11,13},{12,10},{13,11},{18,20},{1... | collective-permute-start | bytes 688136 | tf_op jit(solution)/shard_map/back_0/ppermute | solution.py:185
  76.8 0.1 collective-permute-start.15
  76.9 8.3 %collective-permute-start.16 = (bf16[224,512]{1,0:T(8,128)(2,1)S(1)}, bf16[224,512]{1,0:T(8,128)(2,1)S(1)}, u32[]{:S(2)}, u32[]{:S(2)}) collective-permute-start(bf16[224,512]{1,0:T(8,128)(2,1)S(1)} %get-tuple-element.35), channel_id=1, source_target_pairs={{0,2},{1,3},{2,6},{3,7},{4,0},{5,1},{6,4},{7,5},{8,10},{9,11},{10,... | collective-permute-start | bytes 688136 | tf_op jit(solution)/shard_map/back_2/ppermute | solution.py:185
  85.1 0.0 collective-permute-start.17
  85.2 0.0 collective-permute-done.14.refs_0_
  85.2 0.0 collective-permute-done.15.refs_1_
  85.2 4.3 %collective-permute-done.16.refs_2_ = bf16[224,512]{1,0:T(8,128)(2,1)S(1)} collective-permute-done((bf16[224,512]{1,0:T(8,128)(2,1)S(1)}, bf16[224,512]{1,0:T(8,128)(2,1)S(1)}, u32[]{:S(2)}, u32[]{:S(2)}) %collective-permute-start.16) | collective-permute-done | bytes 229408 | tf_op jit(solution)/shard_map/back_2/ppermute | solution.py:185
  89.5 8.4 %collective-permute-done.17.refs_3_ = bf16[224,512]{1,0:T(8,128)(2,1)S(1)} collective-permute-done((bf16[224,512]{1,0:T(8,128)(2,1)S(1)}, bf16[224,512]{1,0:T(8,128)(2,1)S(1)}, u32[]{:S(2)}, u32[]{:S(2)}) %collective-permute-start.17) | collective-permute-done | bytes 229408 | tf_op jit(solution)/shard_map/back_3/ppermute | solution.py:185
  97.9 1.0 %join.1 = bf16[1,224,2048]{2,1,0:T(8,128)(2,1)} custom-call(bf16[224,512]{1,0:T(8,128)(2,1)S(1)} %get-tuple-element.33.own, bf16[224,512]{1,0:T(8,128)(2,1)S(1)} %collective-permute-done.14.refs_0_, bf16[224,512]{1,0:T(8,128)(2,1)S(1)} %collective-permute-done.15.refs_1_, bf16[224,512]{1,0:T(8,128)(2,1)S(1)} %collective-permute-done.16.refs_2_, ...), custom_call_target="tpu_custom_call" | custom-call | tf_op jit(solution)/shard_map/join/pallas_call | solution.py:282
  (4 shorter events, 0.0 us)
Async XLA Ops:
  1.1 1.6 %copy-start = (bf16[1,224,2048]{2,1,0:T(8,128)(2,1)S(1)}, bf16[1,224,2048]{2,1,0:T(8,128)(2,1)}, u32[]{:S(2)}) copy-start(bf16[1,224,2048]{2,1,0:T(8,128)(2,1)} %param.5) | copy-start | bytes 2752516
  2.5 35.7 %copy-start.1 = (bf16[2048]{0:T(1024)(128)(2,1)S(1)}, bf16[2048]{0:T(1024)(128)(2,1)}, u32[]{:S(2)}) copy-start(bf16[2048]{0:T(1024)(128)(2,1)} %param.6) | copy-start | bytes 12292
  2.5 11.7 %collective-permute-start.1 = (bf16[256,1536]{1,0:T(8,128)(2,1)S(1)}, bf16[256,1536]{1,0:T(8,128)(2,1)S(1)}, u32[]{:S(2)}, u32[]{:S(2)}) collective-permute-start(bf16[256,1536]{1,0:T(8,128)(2,1)S(1)} %pad_maximum_fusion.1), channel_id=1, source_target_pairs={{0,4},{1,5},{2,6},{3,7},{4,0},{5,1},{6,2},{7,3},{8,12},{9,13},{10,... | collective-permute-start | bytes 2359304 | tf_op jit(solution)/shard_map/weights_core/ppermute | solution.py:185
  2.7 27.8 %collective-permute-start.3 = (bf16[224,2048]{1,0:T(8,128)(2,1)S(1)}, bf16[224,2048]{1,0:T(8,128)(2,1)S(1)}, u32[]{:S(2)}, u32[]{:S(2)}) collective-permute-start(bf16[224,2048]{1,0:T(8,128)(2,1)S(1)} %bitcast.1), channel_id=1, source_target_pairs={{0,1},{1,0},{6,7},{7,6},{8,9},{9,8},{14,15},{15,14},{16,17},{17,16... | collective-permute-start | bytes 2752520 | tf_op jit(solution)/shard_map/tokens_1/ppermute | solution.py:185
  3.4 27.1 %collective-permute-start.4 = (bf16[224,2048]{1,0:T(8,128)(2,1)S(1)}, bf16[224,2048]{1,0:T(8,128)(2,1)S(1)}, u32[]{:S(2)}, u32[]{:S(2)}) collective-permute-start(bf16[224,2048]{1,0:T(8,128)(2,1)S(1)} %bitcast.2), channel_id=1, source_target_pairs={{0,4},{1,5},{6,2},{7,3},{8,12},{9,13},{14,10},{15,11},{16,20},{17,... | collective-permute-start | bytes 2752520 | tf_op jit(solution)/shard_map/tokens_core_0/ppermute | solution.py:185
  4.7 27.2 %collective-permute-start.6 = (bf16[224,2048]{1,0:T(8,128)(2,1)S(1)}, bf16[224,2048]{1,0:T(8,128)(2,1)S(1)}, u32[]{:S(2)}, u32[]{:S(2)}) collective-permute-start(bf16[224,2048]{1,0:T(8,128)(2,1)S(1)} %bitcast.3), channel_id=1, source_target_pairs={{2,0},{3,1},{4,6},{5,7},{10,8},{11,9},{12,14},{13,15},{18,16},{19,... | collective-permute-start | bytes 2752520 | tf_op jit(solution)/shard_map/tokens_2/ppermute | solution.py:185
  13.0 17.4 %collective-permute-start = (bf16[256,1536]{1,0:T(8,128)(2,1)S(1)}, bf16[256,1536]{1,0:T(8,128)(2,1)S(1)}, u32[]{:S(2)}, u32[]{:S(2)}) collective-permute-start(bf16[256,1536]{1,0:T(8,128)(2,1)S(1)} %pad_maximum_fusion.refs_8_), channel_id=1, source_target_pairs={{0,8},{1,9},{2,10},{3,11},{4,12},{5,13},{6,14},{7,15},{8,0},{9,1},... | collective-permute-start | bytes 2359304 | tf_op jit(solution)/shard_map/weights_x/ppermute | solution.py:185
  14.3 17.6 %collective-permute-start.2 = (bf16[256,1536]{1,0:T(8,128)(2,1)S(1)}, bf16[256,1536]{1,0:T(8,128)(2,1)S(1)}, u32[]{:S(2)}, u32[]{:S(2)}) collective-permute-start(bf16[256,1536]{1,0:T(8,128)(2,1)S(1)} %collective-permute-done.1.refs_9_), channel_id=1, source_target_pairs={{0,16},{1,17},{2,18},{3,19},{4,20},{5,21},{6,22},{7,23},{8,24},{9,... | collective-permute-start | bytes 2359304 | tf_op jit(solution)/shard_map/weights_core_y/ppermute | solution.py:185
  31.9 3.3 %collective-permute-start.10 = (bf16[224,2048]{1,0:T(8,128)(2,1)S(1)}, bf16[224,2048]{1,0:T(8,128)(2,1)S(1)}, u32[]{:S(2)}, u32[]{:S(2)}) collective-permute-start(bf16[224,2048]{1,0:T(8,128)(2,1)S(1)} %collective-permute-done.6.refs_2_), channel_id=1, source_target_pairs={{0,1},{1,0},{6,7},{7,6},{8,9},{9,8},{14,15},{15,14},{16,17},{17,16... | collective-permute-start | bytes 2752520 | tf_op jit(solution)/shard_map/tokens_3/ppermute | solution.py:185
  32.6 7.3 %collective-permute-start.7 = (bf16[224,2048]{1,0:T(8,128)(2,1)S(1)}, bf16[224,2048]{1,0:T(8,128)(2,1)S(1)}, u32[]{:S(2)}, u32[]{:S(2)}) collective-permute-start(bf16[224,2048]{1,0:T(8,128)(2,1)S(1)} %collective-permute-done.6.refs_2_), channel_id=1, source_target_pairs={{0,4},{1,5},{6,2},{7,3},{8,12},{9,13},{14,10},{15,11},{16,20},{17,... | collective-permute-start | bytes 2752520 | tf_op jit(solution)/shard_map/tokens_core_2/ppermute | solution.py:185
  33.9 7.3 %collective-permute-start.5 = (bf16[224,2048]{1,0:T(8,128)(2,1)S(1)}, bf16[224,2048]{1,0:T(8,128)(2,1)S(1)}, u32[]{:S(2)}, u32[]{:S(2)}) collective-permute-start(bf16[224,2048]{1,0:T(8,128)(2,1)S(1)} %collective-permute-done.3.refs_1_), channel_id=1, source_target_pairs={{0,4},{1,5},{6,2},{7,3},{8,12},{9,13},{14,10},{15,11},{16,20},{17,... | collective-permute-start | bytes 2752520 | tf_op jit(solution)/shard_map/tokens_core_1/ppermute | solution.py:185
  35.2 18.0 %collective-permute-start.11 = (bf16[224,2048]{1,0:T(8,128)(2,1)S(1)}, bf16[224,2048]{1,0:T(8,128)(2,1)S(1)}, u32[]{:S(2)}, u32[]{:S(2)}) collective-permute-start(bf16[224,2048]{1,0:T(8,128)(2,1)S(1)} %collective-permute-done.10.refs_3_), channel_id=1, source_target_pairs={{0,4},{1,5},{6,2},{7,3},{8,12},{9,13},{14,10},{15,11},{16,20},{17,... | collective-permute-start | bytes 2752520 | tf_op jit(solution)/shard_map/tokens_core_3/ppermute | solution.py:185
  36.5 11.2 %collective-permute-start.12 = (bf16[256,1536]{1,0:T(8,128)(2,1)S(1)}, bf16[256,1536]{1,0:T(8,128)(2,1)S(1)}, u32[]{:S(2)}, u32[]{:S(2)}) collective-permute-start(bf16[256,1536]{1,0:T(8,128)(2,1)S(1)} %collective-permute-done.refs_10_), channel_id=1, source_target_pairs={{0,16},{1,17},{2,18},{3,19},{4,20},{5,21},{6,22},{7,23},{8,24},{9,... | collective-permute-start | bytes 2359304 | tf_op jit(solution)/shard_map/weights_xy/ppermute | solution.py:185
  37.9 11.1 %collective-permute-start.13 = (bf16[256,1536]{1,0:T(8,128)(2,1)S(1)}, bf16[256,1536]{1,0:T(8,128)(2,1)S(1)}, u32[]{:S(2)}, u32[]{:S(2)}) collective-permute-start(bf16[256,1536]{1,0:T(8,128)(2,1)S(1)} %collective-permute-done.2.refs_11_), channel_id=1, source_target_pairs={{0,8},{1,9},{2,10},{3,11},{4,12},{5,13},{6,14},{7,15},{8,0},{9,1},... | collective-permute-start | bytes 2359304 | tf_op jit(solution)/shard_map/weights_core_yx/ppermute | solution.py:185
  41.3 19.8 %collective-permute-start.8 = (bf16[256,1536]{1,0:T(8,128)(2,1)S(1)}, bf16[256,1536]{1,0:T(8,128)(2,1)S(1)}, u32[]{:S(2)}, u32[]{:S(2)}) collective-permute-start(bf16[256,1536]{1,0:T(8,128)(2,1)S(1)} %collective-permute-done.1.refs_9_), channel_id=1, source_target_pairs={{0,8},{1,9},{2,10},{3,11},{4,12},{5,13},{6,14},{7,15},{8,0},{9,1},... | collective-permute-start | bytes 2359304 | tf_op jit(solution)/shard_map/weights_core_x/ppermute | solution.py:185
  42.7 18.4 %collective-permute-start.9 = (bf16[256,1536]{1,0:T(8,128)(2,1)S(1)}, bf16[256,1536]{1,0:T(8,128)(2,1)S(1)}, u32[]{:S(2)}, u32[]{:S(2)}) collective-permute-start(bf16[256,1536]{1,0:T(8,128)(2,1)S(1)} %pad_maximum_fusion.refs_8_), channel_id=1, source_target_pairs={{0,16},{1,17},{2,18},{3,19},{4,20},{5,21},{6,22},{7,23},{8,24},{9,... | collective-permute-start | bytes 2359304 | tf_op jit(solution)/shard_map/weights_y/ppermute | solution.py:185
  69.2 15.9 %collective-permute-start.14 = (bf16[224,512]{1,0:T(8,128)(2,1)S(1)}, bf16[224,512]{1,0:T(8,128)(2,1)S(1)}, u32[]{:S(2)}, u32[]{:S(2)}) collective-permute-start(bf16[224,512]{1,0:T(8,128)(2,1)S(1)} %get-tuple-element.33.own), channel_id=1, source_target_pairs={{2,4},{3,5},{4,2},{5,3},{10,12},{11,13},{12,10},{13,11},{18,20},{1... | collective-permute-start | bytes 688136 | tf_op jit(solution)/shard_map/back_0/ppermute | solution.py:185
  76.8 8.4 %collective-permute-start.15 = (bf16[224,512]{1,0:T(8,128)(2,1)S(1)}, bf16[224,512]{1,0:T(8,128)(2,1)S(1)}, u32[]{:S(2)}, u32[]{:S(2)}) collective-permute-start(bf16[224,512]{1,0:T(8,128)(2,1)S(1)} %get-tuple-element.34), channel_id=1, source_target_pairs={{0,1},{1,0},{2,5},{3,4},{4,3},{5,2},{6,7},{7,6},{8,9},{9,8},{10,13... | collective-permute-start | bytes 688136 | tf_op jit(solution)/shard_map/back_1/ppermute | solution.py:185
  76.9 12.6 %collective-permute-start.16 = (bf16[224,512]{1,0:T(8,128)(2,1)S(1)}, bf16[224,512]{1,0:T(8,128)(2,1)S(1)}, u32[]{:S(2)}, u32[]{:S(2)}) collective-permute-start(bf16[224,512]{1,0:T(8,128)(2,1)S(1)} %get-tuple-element.35), channel_id=1, source_target_pairs={{0,2},{1,3},{2,6},{3,7},{4,0},{5,1},{6,4},{7,5},{8,10},{9,11},{10,... | collective-permute-start | bytes 688136 | tf_op jit(solution)/shard_map/back_2/ppermute | solution.py:185
  85.1 12.7 %collective-permute-start.17 = (bf16[224,512]{1,0:T(8,128)(2,1)S(1)}, bf16[224,512]{1,0:T(8,128)(2,1)S(1)}, u32[]{:S(2)}, u32[]{:S(2)}) collective-permute-start(bf16[224,512]{1,0:T(8,128)(2,1)S(1)} %get-tuple-element.36), channel_id=1, source_target_pairs={{0,3},{1,2},{2,7},{3,6},{4,1},{5,0},{6,5},{7,4},{8,11},{9,10},{10,... | collective-permute-start | bytes 688136 | tf_op jit(solution)/shard_map/back_3/ppermute | solution.py:185

commit v5 on v4

v5 whole, which is shorter than its diff:
```python
import functools
import math

import jax
import jax.numpy as jnp
from jax import lax
from jax.experimental import pallas as pl
from jax.experimental.pallas import tpu as pltpu
from jax.sharding import PartitionSpec as P

HEADS = 16
HEAD_DIM = 128
HALF = HEAD_DIM // 2
EPS = 1e-05
VMEM_LIMIT = 28 * 1024 * 1024

PLAN = {
    "order": ["t1", "t2", "w1", "w2", "w5", "u0", "w6", "w7", "u1", "t3", "u2", "w4", "w3", "u3"],
    "waits": [["w6", ["t1", "u0"]], ["w7", ["w2"]], ["t3", ["w2"]], ["w4", ["u1", "u2"]]],
    "early": [0, 1, 2, 5, 6, 7],
    "splits": [[0, 4]],
    "hold": [1, 2],
    "back": [0, 1, 2, 3],
    "direct3": False,
    "cross3": False,
    "cross5": False,
    "early_flops": 4000000000,
    "late_flops": 8000000000,
}


def tables(length):
    freqs = 10000.0 ** (-(jnp.arange(HALF).astype(jnp.float32) * 2.0) / HEAD_DIM)
    angles = jnp.arange(length).astype(jnp.float32)[:, None] * freqs[None, :]
    cosine = jnp.cos(angles)
    sine = jnp.sin(angles)
    return (
        jnp.concatenate([cosine, cosine], axis=1),
        jnp.concatenate([-sine, sine], axis=1),
    )


def normalize(block, gain):
    rows = block.astype(jnp.float32)
    scale = lax.rsqrt(jnp.mean(rows * rows, axis=1, keepdims=True) + EPS)
    return (rows * scale * gain.astype(jnp.float32)).astype(jnp.bfloat16)


def role(rows):
    d, c = lax.axis_index("dp"), lax.axis_index("ctx")
    home = c // 2 == d % 2
    return {
        "home": home,
        "starts": [pl.multiple_of((c ^ i) * rows, rows) for i in range(4)],
        "base": jnp.where(home, c, c ^ 2),
        "owner": d,
    }


def early_kernel(rows, order, early, groups, *refs):
    n = len(groups)
    kept, sent, shards = refs[:n], refs[n : 2 * n], refs[2 * n : 2 * n + early]
    gain, out, tail, held, normed, weights, token_sems, weight_sems = refs[2 * n + early :]
    me = role(rows)
    depth = shards[0].shape[0]
    loads = []
    row = 0
    for i in range(n):
        slot = held.at[pl.ds(row, kept[i].shape[0])]
        row += kept[i].shape[0]
        for condition, source in ((me["home"], kept[i]), (jnp.logical_not(me["home"]), sent[i])):

            @pl.when(condition)
            def _(source=source, slot=slot, i=i):
                pltpu.make_async_copy(source, slot, token_sems.at[i]).start()

        loads.append(pltpu.make_async_copy(kept[i], slot, token_sems.at[i]))
    weight_loads = []
    for i, shard in enumerate(shards):
        load = pltpu.make_async_copy(shard, weights.at[pl.ds(i * depth, depth)], weight_sems.at[i])
        load.start()
        weight_loads.append(load)
    lanes = []
    for owner in range(8):
        offset = me["owner"] ^ owner
        place = sum(jnp.where(offset == k, at, 0) for at, k in enumerate(order))
        lanes.append(pl.ds(pl.multiple_of(place * depth, depth), depth))
    at = 0
    for load, group in zip(loads, groups):
        load.wait()
        for _ in group:
            part = pl.ds(at * rows, rows)
            at += 1
            value = normalize(held[part, :], gain[...])
            for owner, lane in enumerate(lanes):
                normed[part, lane] = value[:, owner * depth : (owner + 1) * depth]
    for load in weight_loads:
        load.wait()
    first = early * depth
    tail[...] = normed[:, first:]
    step = 2 * HEAD_DIM
    for lane in range(0, out.shape[1], step):
        out[:, lane : lane + step] = jnp.dot(
            normed[:, :first], weights[:, lane : lane + step], preferred_element_type=jnp.float32
        )


def late_kernel(rows, cols, total, blocks, count, first_head, heads, *refs):
    shards = refs[:count]
    partial, tail, cos_ref, sin_ref = refs[count : count + 4]
    outs = refs[count + 4 : count + 4 + total]
    weights, qkv, result, weight_sems, out_sems = refs[count + 4 + total :]
    me = role(rows)
    depth = shards[0].shape[0]
    width = heads * HEAD_DIM
    start_lane = first_head * HEAD_DIM
    loads = []
    for i, shard in enumerate(shards):
        for j in range(3):
            load = pltpu.make_async_copy(
                shard.at[:, pl.ds(j * cols + start_lane, width)],
                weights.at[pl.ds(i * depth, depth), pl.ds(j * width, width)],
                weight_sems.at[3 * i + j],
            )
            load.start()
            loads.append(load)
    for load in loads:
        load.wait()
    step = HEAD_DIM if width % (2 * HEAD_DIM) else 2 * HEAD_DIM
    for j in range(3):
        for lane in range(0, width, step):
            first = j * cols + start_lane + lane
            linear = partial[:, first : first + step] + jnp.dot(
                tail[...],
                weights[:, j * width + lane : j * width + lane + step],
                preferred_element_type=jnp.float32,
            )
            for i, block in enumerate(blocks):
                start = me["starts"][block]
                value = linear[i * rows : (i + 1) * rows]
                if j < 2:
                    cosine = cos_ref[pl.ds(start, rows), :]
                    sine = sin_ref[pl.ds(start, rows), :]
                    parts = [value[:, h * HEAD_DIM : (h + 1) * HEAD_DIM] for h in range(step // HEAD_DIM)]
                    value = jnp.concatenate(
                        [x * cosine + pltpu.roll(x, HALF, 1) * sine for x in parts], axis=1
                    )
                lanes = slice(j * width + lane, j * width + lane + step)
                qkv[pl.ds(start, rows), lanes] = value.astype(jnp.bfloat16)
    attend(qkv, result, me["base"], total, rows, width)
    copies = []
    for k in range(total):
        copy = pltpu.make_async_copy(result.at[k], outs[k], out_sems.at[k])
        copy.start()
        copies.append(copy)
    for copy in copies:
        copy.wait()


def attend(qkv, result, me, total, rows, cols):
    factor = HEAD_DIM ** (-0.5) * math.log2(math.e)
    below = lax.broadcasted_iota(jnp.int32, (rows, rows), 0) >= lax.broadcasted_iota(
        jnp.int32, (rows, rows), 1
    )

    def scored(q, k):
        return lax.dot_general(q, k, (((1,), (1,)), ((), ())), preferred_element_type=jnp.float32)

    for block in range(total):
        own, past = slice(block * rows, (block + 1) * rows), slice(0, block * rows)
        for head in range(cols // HEAD_DIM):
            lane = slice(head * HEAD_DIM, (head + 1) * HEAD_DIM)
            k_lane = slice(cols + lane.start, cols + lane.stop)
            v_lane = slice(2 * cols + lane.start, 2 * cols + lane.stop)
            q = qkv[own, lane]
            near = jnp.where(below, scored(q, qkv[own, k_lane]), -1e30)
            top = jnp.max(near, axis=1, keepdims=True)
            if block:
                far = scored(q, qkv[past, k_lane])
                top = jnp.maximum(top, jnp.max(far, axis=1, keepdims=True))
            top = top * factor
            expo = jnp.exp2(near * factor - top)
            bottom = jnp.sum(expo, axis=1, keepdims=True)
            numer = jnp.dot(expo.astype(jnp.bfloat16), qkv[own, v_lane], preferred_element_type=jnp.float32)
            if block:
                expo = jnp.exp2(far * factor - top)
                bottom += jnp.sum(expo, axis=1, keepdims=True)
                numer += jnp.dot(
                    expo.astype(jnp.bfloat16), qkv[past, v_lane], preferred_element_type=jnp.float32
                )
            result[block ^ me, :, lane] = (numer / bottom).astype(jnp.bfloat16)


def join_kernel(cols, total, splits, *refs):
    out = refs[-1]
    d, c = lax.axis_index("dp"), lax.axis_index("ctx")
    group = d % 2
    for part, (first_head, heads) in enumerate(splits):
        own, *pieces = refs[part * (total + 1) : (part + 1) * (total + 1)]
        for k in range(total):
            base = c ^ k
            same = base // 2 == group
            plane = jnp.where(same, base, base ^ 2)
            core = jnp.where(same, group, 1 - group)
            first = (2 * (plane % 2) + core) * cols + first_head * HEAD_DIM
            lane = pl.ds(pl.multiple_of(first, HEAD_DIM), heads * HEAD_DIM)
            if k:
                out[0, :, lane] = pieces[k][...]
            else:
                out[0, :, lane] = jnp.where(c // 2 == group, own[...], pieces[k][...])


def fast(dp, ctx, tokens, norm_gain, q_weight, k_weight, v_weight):
    rows, features = tokens.shape[1], tokens.shape[2]
    cols = HEADS // ctx * HEAD_DIM
    depth = q_weight.shape[0]
    every = [(d, c) for d in range(dp) for c in range(ctx)]
    plan = PLAN

    def home(to):
        return lambda d, c: to(d, c) if c // 2 == d % 2 else None

    def away(to):
        return lambda d, c: to(d, c) if c // 2 != d % 2 else None

    shift = lambda k: lambda d, c: (d ^ k, c)
    plane = lambda k: lambda d, c: (d, c ^ k)
    routes = {
        "w1": ("o", shift(1)),
        "w2": ("m", shift(2)),
        "w4": ("m", shift(4)),
        "w6": ("w2", shift(4)),
        "w7": ("w5", shift(2)),
        "t1": ("own", home(plane(1))),
        "t2": ("own", away(plane(2))),
        "u0": ("own", home(shift(1))),
        "u1": ("t1", home(shift(1))),
        "u2": ("t2", home(shift(1))),
        "u3": ("t3", home(shift(1))),
    }
    routes["t3"] = ("own", away(plane(3))) if plan["direct3"] else ("t2", home(plane(1)))
    routes["w3"] = ("o", shift(3)) if plan["cross3"] else ("w1", shift(2))
    routes["w5"] = ("o", shift(5)) if plan["cross5"] else ("w1", shift(4))

    d, c = lax.axis_index("dp"), lax.axis_index("ctx")

    def columns(heads):
        return jnp.concatenate(
            [lax.dynamic_slice_in_dim(w, heads * cols, cols, 1) for w in (q_weight, k_weight, v_weight)],
            axis=1,
        )

    heads = 2 * (c % 2) + d % 2
    values = {"own": tokens[0], "o": columns(heads ^ 1), "m": columns(heads)}
    inputs = {}
    waits = {name: list(earlier) for name, earlier in plan["waits"]}

    for name in plan["order"]:
        source, to = routes[name]
        operand = values[source]
        earlier = waits.get(name, [])
        if earlier:
            operand, *late = lax.optimization_barrier((operand, *[values[e] for e in earlier]))
            values.update(zip(earlier, late))
        perm = [
            (dd * ctx + cc, to(dd, cc)[0] * ctx + to(dd, cc)[1])
            for dd, cc in every
            if to(dd, cc) is not None
        ]
        with jax.named_scope(name):
            values[name] = lax.ppermute(operand, ("dp", "ctx"), perm)
    cosine, sine = tables(ctx * rows)
    names = {0: "m", 1: "w1", 2: "w2", 3: "w3", 4: "w4", 5: "w5", 6: "w6", 7: "w7"}
    early = plan["early"]
    shard_order = early + [k for k in range(8) if k not in early]
    blocks = [0, 1, 2, 3]
    kept = [values[n] for n in ("own", "t1", "t2", "t3")]
    sent = [values[n] for n in ("u0", "u1", "u2", "u3")]

    gain = norm_gain[None, :]
    any_space = pl.BlockSpec(memory_space=pl.ANY)
    vmem = pl.BlockSpec(memory_space=pltpu.VMEM)
    n, late = len(early), 8 - len(early)
    partial, tail = pl.pallas_call(
        functools.partial(early_kernel, rows, shard_order, n, [[b] for b in blocks]),
        out_shape=[
            jax.ShapeDtypeStruct((ctx * rows, 3 * cols), jnp.float32),
            jax.ShapeDtypeStruct((ctx * rows, late * depth), jnp.bfloat16),
        ],
        in_specs=[any_space] * (8 + n) + [vmem],
        out_specs=[vmem] * 2,
        scratch_shapes=[
            pltpu.VMEM((ctx * rows, features), jnp.bfloat16),
            pltpu.VMEM((ctx * rows, features), jnp.bfloat16),
            pltpu.VMEM((n * depth, 3 * cols), jnp.bfloat16),
            pltpu.SemaphoreType.DMA((4,)),
            pltpu.SemaphoreType.DMA((n,)),
        ],
        compiler_params=pltpu.CompilerParams(vmem_limit_bytes=VMEM_LIMIT),
        cost_estimate=pl.CostEstimate(
            flops=plan["early_flops"], bytes_accessed=1_000_000, transcendentals=0
        ),
        name="project_early",
    )(*kept, *sent, *[values[names[k]] for k in early], gain)

    def back(k):
        def to(d, c):
            base = c if c // 2 == d % 2 else c ^ 2
            target = ((d & 6) | (c // 2), base ^ k)
            return None if target == (d, c) else target

        return to

    arrived = []
    last = [values[names[k]] for k in shard_order[n:]]
    for part, (first_head, count) in enumerate(plan["splits"]):
        width = count * HEAD_DIM
        pieces = pl.pallas_call(
            functools.partial(late_kernel, rows, cols, ctx, blocks, late, first_head, count),
            out_shape=[jax.ShapeDtypeStruct((rows, width), jnp.bfloat16)] * ctx,
            in_specs=[any_space] * late + [vmem] * 4,
            out_specs=[any_space] * ctx,
            scratch_shapes=[
                pltpu.VMEM((late * depth, 3 * width), jnp.bfloat16),
                pltpu.VMEM((ctx * rows, 3 * width), jnp.bfloat16),
                pltpu.VMEM((ctx, rows, width), jnp.bfloat16),
                pltpu.SemaphoreType.DMA((3 * late,)),
                pltpu.SemaphoreType.DMA((ctx,)),
            ],
            compiler_params=pltpu.CompilerParams(vmem_limit_bytes=VMEM_LIMIT),
            cost_estimate=pl.CostEstimate(
                flops=plan["late_flops"], bytes_accessed=1_000_000, transcendentals=0
            ),
            name=f"attend_{part}",
        )(*last, partial, tail, cosine, sine)
        if arrived:
            hold = plan["hold"]
            both = lax.optimization_barrier((*[arrived[-ctx + k] for k in hold], *pieces))
            for k, value in zip(hold, both):
                arrived[-ctx + k] = value
            pieces = both[len(hold) :]
        elif len(plan["splits"]) > 1:
            pieces = list(pieces)
            pieces[0], last[0] = lax.optimization_barrier((pieces[0], last[0]))
        moved = {}
        for k in plan["back"]:
            with jax.named_scope(f"back_{part}_{k}"):
                to = back(k)
                perm = [
                    (dd * ctx + cc, to(dd, cc)[0] * ctx + to(dd, cc)[1])
                    for dd, cc in every
                    if to(dd, cc) is not None
                ]
                moved[k] = lax.ppermute(pieces[k], ("dp", "ctx"), perm)
        arrived += [pieces[0]] + [moved[k] for k in range(ctx)]
    return pl.pallas_call(
        functools.partial(join_kernel, cols, ctx, plan["splits"]),
        out_shape=jax.ShapeDtypeStruct((1, rows, ctx * cols), jnp.bfloat16),
        in_specs=[vmem] * len(arrived),
        out_specs=vmem,
        compiler_params=pltpu.CompilerParams(vmem_limit_bytes=8 * 1024 * 1024),
        name="join",
    )(*arrived)


def rotate(values, positions):
    heads = values.shape[1] // HEAD_DIM
    shaped = values.reshape(values.shape[0], heads, HEAD_DIM)
    freqs = 10000.0 ** (-(jnp.arange(HALF).astype(jnp.float32) * 2.0) / HEAD_DIM)
    angles = positions[:, None] * freqs[None, :]
    cosine = jnp.cos(angles)[:, None, :]
    sine = jnp.sin(angles)[:, None, :]
    first = shaped[:, :, :HALF]
    second = shaped[:, :, HALF:]
    return jnp.concatenate(
        [first * cosine - second * sine, second * cosine + first * sine], axis=2
    )


def general(dp, ctx, tokens, norm_gain, q_weight, k_weight, v_weight):
    rows = tokens.shape[1]
    heads = HEADS // ctx
    cols = heads * HEAD_DIM
    me = lax.axis_index("ctx")
    part = jnp.concatenate(
        [lax.dynamic_slice_in_dim(w, me * cols, cols, 1) for w in (q_weight, k_weight, v_weight)], axis=1
    )
    weights = lax.all_gather(part, "dp", axis=0, tiled=True)
    whole = lax.all_gather(tokens[0], "ctx", axis=0, tiled=True)
    normed = normalize(whole, norm_gain[None, :])
    linear = jnp.dot(normed, weights, preferred_element_type=jnp.float32)
    length = ctx * rows
    positions = jnp.arange(length).astype(jnp.float32)
    q = rotate(linear[:, :cols], positions).astype(jnp.bfloat16)
    k = rotate(linear[:, cols : 2 * cols], positions).astype(jnp.bfloat16)
    v = linear[:, 2 * cols :].astype(jnp.bfloat16).reshape(length, heads, HEAD_DIM)
    allowed = jnp.arange(length)[None, :] <= jnp.arange(length)[:, None]
    scores = jnp.einsum("qhd,khd->hqk", q, k, preferred_element_type=jnp.float32) * HEAD_DIM ** (-0.5)
    scores = jnp.where(allowed[None], scores, -1e30)
    top = jnp.max(scores, axis=2, keepdims=True)
    expo = jnp.where(allowed[None], jnp.exp(scores - top), 0.0)
    numer = jnp.einsum("hqk,khd->hqd", expo.astype(jnp.bfloat16), v, preferred_element_type=jnp.float32)
    result = (numer / jnp.sum(expo, axis=2, keepdims=True)).astype(jnp.bfloat16)
    result = result.reshape(heads, ctx, rows, HEAD_DIM).transpose(1, 2, 0, 3).reshape(ctx, rows, cols)
    back = lax.all_to_all(result, "ctx", 0, 0)
    return back.transpose(1, 0, 2).reshape(1, rows, ctx * cols)


def solution(mesh):
    dp, ctx = mesh.shape["dp"], mesh.shape["ctx"]
    body = fast if (dp, ctx) == (8, 4) else general
    placed = (P("dp", "ctx", None), P(), P("dp", None), P("dp", None), P("dp", None))
    return jax.shard_map(
        functools.partial(body, dp, ctx),
        mesh=mesh,
        in_specs=placed,
        out_specs=P("dp", "ctx", None),
        check_vma=False,
    )
```

time: 99.2 us -> 94.5 us (0.953)
  the two profiles are of different devices: /device:TPU:1 before, /device:TPU:0 now
where the time goes in v5:
time: 94.5 us; the launch traced here: 93.4 us
  waiting for transfers between devices  44.4 us (47%)
  starting transfers between devices  27.2 us (29%)
  Pallas kernels  17 us (18%)
  local copies, waits for them, and re-layouts  2.45 us (3%)
  other arithmetic  2.1 us (2%)
    ppermute x14, waiting for transfers between devices, fast(): values[name] = lax.ppermute(operand, ('dp', 'ctx'), perm)  35.2 us
    ppermute x14, starting transfers between devices, fast(): values[name] = lax.ppermute(operand, ('dp', 'ctx'), perm)  22 us
    ppermute x4, waiting for transfers between devices, fast(): moved[k] = lax.ppermute(pieces[k], ('dp', 'ctx'), perm)  9.24 us
    pallas_call x1, Pallas kernels, fast(): pl.pallas_call(functools.partial(late_kernel, rows, cols, ctx, blocks, la...  8.15 us
    pallas_call x1, Pallas kernels, fast(): pl.pallas_call(functools.partial(early_kernel, rows, shard_order, n, [[b]...  7.88 us
    ppermute x4, starting transfers between devices, fast(): moved[k] = lax.ppermute(pieces[k], ('dp', 'ctx'), perm)  5.14 us
    dynamic_slice x2, local copies, waits for them, and re-layouts, columns(): lax.dynamic_slice_in_dim(w, heads * cols, cols, 1)  2.43 us
  transfers between devices with their start and end apart: 18, of which 10 were waited for; matrix products, arithmetic and copies ran while one was open for 2% of the time, Pallas kernels for 8%

profile of v5, /device:TPU:0, one launch (start us, length us, event | category | flops | bytes accessed | tf_op | source)
XLA Modules:
  0.0 93.4 jit_solution(16692452734255737499)
XLA Ops:
  0.0 1.1 %constant_dynamic-slice_fusion.2 = (bf16[256,512]{1,0:T(8,128)(2,1)S(1)}, bf16[256,512]{1,0:T(8,128)(2,1)S(1)}) fusion(bf16[256,2048]{1,0:T(8,128)(2,1)} %param.7, s32[]{:T(128)S(6)} %select_n.24, s32[]{:T(128)S(6)} %select_n.23), kind=kLoop, calls=%fused_computation.10 | loop fusion | bytes 1048584 | tf_op jit(solution)/shard_map/dynamic_slice | solution.py:249
  1.1 0.0 copy-start
  1.1 1.4 %constant_dynamic-slice_fusion = (bf16[256,512]{1,0:T(8,128)(2,1)S(1)}, bf16[256,512]{1,0:T(8,128)(2,1)S(1)}, bf16[256,512]{1,0:T(8,128)(2,1)S(1)}, bf16[256,512]{1,0:T(8,128)(2,1)S(1)}) fusion(bf16[256,2048]{1,0:T(8,128)(2,1)} %param.9, s32[]{:T(128)S(6)} %select_n.24, s32[]{:T(128)S(6)} %select_n.23, bf16[256,2048]{1,0:T(8,128)(2,1)} %param.8), kind=kLoop, calls=%fused_computation.8 | loop fusion | bytes 2097160 | tf_op jit(solution)/shard_map/dynamic_slice | solution.py:249
  2.5 0.0 copy-start.1
  2.5 0.1 pad_maximum_fusion
  2.5 0.5 collective-permute-start
  3.0 0.0 copy-done
  3.1 1.3 %collective-permute-start.6 = (bf16[224,2048]{1,0:T(8,128)(2,1)S(1)}, bf16[224,2048]{1,0:T(8,128)(2,1)S(1)}, u32[]{:S(2)}, u32[]{:S(2)}) collective-permute-start(bf16[224,2048]{1,0:T(8,128)(2,1)S(1)} %bitcast.1), channel_id=1, source_target_pairs={{2,0},{3,1},{4,6},{5,7},{10,8},{11,9},{12,14},{13,15},{18,16},{19,... | collective-permute-start | bytes 2752520 | tf_op jit(solution)/shard_map/t2/ppermute | solution.py:271
  4.3 0.1 pad_maximum_fusion.1.refs_8_
  4.4 2.6 %collective-permute-start.2 = (bf16[256,1536]{1,0:T(8,128)(2,1)S(1)}, bf16[256,1536]{1,0:T(8,128)(2,1)S(1)}, u32[]{:S(2)}, u32[]{:S(2)}) collective-permute-start(bf16[256,1536]{1,0:T(8,128)(2,1)S(1)} %pad_maximum_fusion.1.refs_8_), channel_id=1, source_target_pairs={{0,8},{1,9},{2,10},{3,11},{4,12},{5,13},{6,14},{7,15},{8,0},{9,1},... | collective-permute-start | bytes 2359304 | tf_op jit(solution)/shard_map/w2/ppermute | solution.py:271
  7.0 0.0 collective-permute-done.refs_9_
  7.0 1.5 %collective-permute-start.9 = (bf16[256,1536]{1,0:T(8,128)(2,1)S(1)}, bf16[256,1536]{1,0:T(8,128)(2,1)S(1)}, u32[]{:S(2)}, u32[]{:S(2)}) collective-permute-start(bf16[256,1536]{1,0:T(8,128)(2,1)S(1)} %collective-permute-done.refs_9_), channel_id=1, source_target_pairs={{0,16},{1,17},{2,18},{3,19},{4,20},{5,21},{6,22},{7,23},{8,24},{9,... | collective-permute-start | bytes 2359304 | tf_op jit(solution)/shard_map/w5/ppermute | solution.py:271
  8.5 3.5 %collective-permute-start.3 = (bf16[224,2048]{1,0:T(8,128)(2,1)S(1)}, bf16[224,2048]{1,0:T(8,128)(2,1)S(1)}, u32[]{:S(2)}, u32[]{:S(2)}) collective-permute-start(bf16[224,2048]{1,0:T(8,128)(2,1)S(1)} %bitcast.2), channel_id=1, source_target_pairs={{0,1},{1,0},{6,7},{7,6},{8,9},{9,8},{14,15},{15,14},{16,17},{17,16... | collective-permute-start | bytes 2752520 | tf_op jit(solution)/shard_map/t1/ppermute | solution.py:271
  12.0 2.1 %collective-permute-start.4 = (bf16[224,2048]{1,0:T(8,128)(2,1)S(1)}, bf16[224,2048]{1,0:T(8,128)(2,1)S(1)}, u32[]{:S(2)}, u32[]{:S(2)}) collective-permute-start(bf16[224,2048]{1,0:T(8,128)(2,1)S(1)} %bitcast.3), channel_id=1, source_target_pairs={{0,4},{1,5},{6,2},{7,3},{8,12},{9,13},{14,10},{15,11},{16,20},{17,... | collective-permute-start | bytes 2752520 | tf_op jit(solution)/shard_map/u0/ppermute | solution.py:271
  14.1 8.3 %collective-permute-done.2.refs_10_ = bf16[256,1536]{1,0:T(8,128)(2,1)S(1)} collective-permute-done((bf16[256,1536]{1,0:T(8,128)(2,1)S(1)}, bf16[256,1536]{1,0:T(8,128)(2,1)S(1)}, u32[]{:S(2)}, u32[]{:S(2)}) %collective-permute-start.2) | collective-permute-done | bytes 786464 | tf_op jit(solution)/shard_map/w2/ppermute | solution.py:271
  22.4 2.8 %collective-permute-done.9.refs_11_ = bf16[256,1536]{1,0:T(8,128)(2,1)S(1)} collective-permute-done((bf16[256,1536]{1,0:T(8,128)(2,1)S(1)}, bf16[256,1536]{1,0:T(8,128)(2,1)S(1)}, u32[]{:S(2)}, u32[]{:S(2)}) %collective-permute-start.9) | collective-permute-done | bytes 786464 | tf_op jit(solution)/shard_map/w5/ppermute | solution.py:271
  25.1 4.1 %collective-permute-done.6.refs_2_ = bf16[224,2048]{1,0:T(8,128)(2,1)S(1)} collective-permute-done((bf16[224,2048]{1,0:T(8,128)(2,1)S(1)}, bf16[224,2048]{1,0:T(8,128)(2,1)S(1)}, u32[]{:S(2)}, u32[]{:S(2)}) %collective-permute-start.6) | collective-permute-done | bytes 917536 | tf_op jit(solution)/shard_map/t2/ppermute | solution.py:271
  29.2 1.9 %collective-permute-start.10 = (bf16[224,2048]{1,0:T(8,128)(2,1)S(1)}, bf16[224,2048]{1,0:T(8,128)(2,1)S(1)}, u32[]{:S(2)}, u32[]{:S(2)}) collective-permute-start(bf16[224,2048]{1,0:T(8,128)(2,1)S(1)} %collective-permute-done.6.refs_2_), channel_id=1, source_target_pairs={{0,1},{1,0},{6,7},{7,6},{8,9},{9,8},{14,15},{15,14},{16,17},{17,16... | collective-permute-start | bytes 2752520 | tf_op jit(solution)/shard_map/t3/ppermute | solution.py:271
  31.2 0.4 collective-permute-done.3.refs_1_
  31.6 0.0 collective-permute-done.4.refs_4_
  31.6 1.3 %collective-permute-start.5 = (bf16[224,2048]{1,0:T(8,128)(2,1)S(1)}, bf16[224,2048]{1,0:T(8,128)(2,1)S(1)}, u32[]{:S(2)}, u32[]{:S(2)}) collective-permute-start(bf16[224,2048]{1,0:T(8,128)(2,1)S(1)} %collective-permute-done.3.refs_1_), channel_id=1, source_target_pairs={{0,4},{1,5},{6,2},{7,3},{8,12},{9,13},{14,10},{15,11},{16,20},{17,... | collective-permute-start | bytes 2752520 | tf_op jit(solution)/shard_map/u1/ppermute | solution.py:271
  32.9 1.3 %collective-permute-start.7 = (bf16[224,2048]{1,0:T(8,128)(2,1)S(1)}, bf16[224,2048]{1,0:T(8,128)(2,1)S(1)}, u32[]{:S(2)}, u32[]{:S(2)}) collective-permute-start(bf16[224,2048]{1,0:T(8,128)(2,1)S(1)} %collective-permute-done.6.refs_2_), channel_id=1, source_target_pairs={{0,4},{1,5},{6,2},{7,3},{8,12},{9,13},{14,10},{15,11},{16,20},{17,... | collective-permute-start | bytes 2752520 | tf_op jit(solution)/shard_map/u2/ppermute | solution.py:271
  34.3 10.3 %collective-permute-done.10.refs_3_ = bf16[224,2048]{1,0:T(8,128)(2,1)S(1)} collective-permute-done((bf16[224,2048]{1,0:T(8,128)(2,1)S(1)}, bf16[224,2048]{1,0:T(8,128)(2,1)S(1)}, u32[]{:S(2)}, u32[]{:S(2)}) %collective-permute-start.10) | collective-permute-done | bytes 917536 | tf_op jit(solution)/shard_map/t3/ppermute | solution.py:271
  44.5 1.3 %collective-permute-start.11 = (bf16[224,2048]{1,0:T(8,128)(2,1)S(1)}, bf16[224,2048]{1,0:T(8,128)(2,1)S(1)}, u32[]{:S(2)}, u32[]{:S(2)}) collective-permute-start(bf16[224,2048]{1,0:T(8,128)(2,1)S(1)} %collective-permute-done.10.refs_3_), channel_id=1, source_target_pairs={{0,4},{1,5},{6,2},{7,3},{8,12},{9,13},{14,10},{15,11},{16,20},{17,... | collective-permute-start | bytes 2752520 | tf_op jit(solution)/shard_map/u3/ppermute | solution.py:271
  45.9 2.5 %collective-permute-start.12 = (bf16[256,1536]{1,0:T(8,128)(2,1)S(1)}, bf16[256,1536]{1,0:T(8,128)(2,1)S(1)}, u32[]{:S(2)}, u32[]{:S(2)}) collective-permute-start(bf16[256,1536]{1,0:T(8,128)(2,1)S(1)} %collective-permute-done.2.refs_10_), channel_id=1, source_target_pairs={{0,16},{1,17},{2,18},{3,19},{4,20},{5,21},{6,22},{7,23},{8,24},{9,... | collective-permute-start | bytes 2359304 | tf_op jit(solution)/shard_map/w6/ppermute | solution.py:271
  48.4 1.5 %collective-permute-start.13 = (bf16[256,1536]{1,0:T(8,128)(2,1)S(1)}, bf16[256,1536]{1,0:T(8,128)(2,1)S(1)}, u32[]{:S(2)}, u32[]{:S(2)}) collective-permute-start(bf16[256,1536]{1,0:T(8,128)(2,1)S(1)} %collective-permute-done.9.refs_11_), channel_id=1, source_target_pairs={{0,8},{1,9},{2,10},{3,11},{4,12},{5,13},{6,14},{7,15},{8,0},{9,1},... | collective-permute-start | bytes 2359304 | tf_op jit(solution)/shard_map/w7/ppermute | solution.py:271
  49.9 0.0 collective-permute-done.5.refs_5_
  49.9 0.5 collective-permute-start.1
  50.4 0.0 collective-permute-done.7.refs_6_
  50.4 0.1 collective-permute-start.8
  50.5 1.7 %fusion = (f32[896,64]{1,0:T(8,128)S(1)}, f32[896,64]{1,0:T(8,128)S(1)}, f32[896,64]{1,0:T(8,128)S(1)}) fusion(f32[64]{0:T(128)S(1)} %multiply_power_fusion, f32[896]{0:T(1024)S(1)} %iota_convert_fusion), kind=kLoop, calls=%fused_computation.6 | loop fusion | flops 114688 | bytes 691968 | tf_op jit(solution)/shard_map/neg | solution.py:39
  52.2 0.3 pad_maximum_fusion.2
  52.5 7.6 %collective-permute-done.12.refs_12_ = bf16[256,1536]{1,0:T(8,128)(2,1)S(1)} collective-permute-done((bf16[256,1536]{1,0:T(8,128)(2,1)S(1)}, bf16[256,1536]{1,0:T(8,128)(2,1)S(1)}, u32[]{:S(2)}, u32[]{:S(2)}) %collective-permute-start.12) | collective-permute-done | bytes 786464 | tf_op jit(solution)/shard_map/w6/ppermute | solution.py:271
  60.1 1.2 %collective-permute-done.13.refs_13_ = bf16[256,1536]{1,0:T(8,128)(2,1)S(1)} collective-permute-done((bf16[256,1536]{1,0:T(8,128)(2,1)S(1)}, bf16[256,1536]{1,0:T(8,128)(2,1)S(1)}, u32[]{:S(2)}, u32[]{:S(2)}) %collective-permute-start.13) | collective-permute-done | bytes 786464 | tf_op jit(solution)/shard_map/w7/ppermute | solution.py:271
  61.4 0.0 collective-permute-done.11.refs_7_
  61.4 7.9 %project_early.1 = (f32[896,1536]{1,0:T(8,128)S(1)}, bf16[896,512]{1,0:T(8,128)(2,1)S(1)}) custom-call(bf16[224,2048]{1,0:T(8,128)(2,1)S(1)} %bitcast.4, bf16[224,2048]{1,0:T(8,128)(2,1)S(1)} %collective-permute-done.3.refs_1_, bf16[224,2048]{1,0:T(8,128)(2,1)S(1)} %collective-permute-done.6.refs_2_, bf16[224,2048]{1,0:T(8,128)(2,1)S(1)} %collective-permute-done.10.refs_3_, ...), custom_call_target="tpu_custom_call" | custom-call | flops 4000000000 | bytes 1000000 | tf_op jit(solution)/shard_map/project_early/pallas_call | solution.py:284
  69.2 0.5 collective-permute-done.1.refs_0_
  69.8 0.0 collective-permute-done.8.refs_1_
  69.8 8.2 %attend_0.1 = (bf16[224,512]{1,0:T(8,128)(2,1)S(1)}, bf16[224,512]{1,0:T(8,128)(2,1)S(1)}, bf16[224,512]{1,0:T(8,128)(2,1)S(1)}, bf16[224,512]{1,0:T(8,128)(2,1)S(1)}) custom-call(bf16[256,1536]{1,0:T(8,128)(2,1)S(1)} %collective-permute-done.1.refs_0_, bf16[256,1536]{1,0:T(8,128)(2,1)S(1)} %collective-permute-done.8.refs_1_, ...), custom_call_target="tpu_custom_call" | custom-call | flops 8000000000 | bytes 1000000 | tf_op jit(solution)/shard_map/attend_0/pallas_call | solution.py:318
  77.9 0.7 collective-permute-start.14
  78.6 3.0 %collective-permute-start.15 = (bf16[224,512]{1,0:T(8,128)(2,1)S(1)}, bf16[224,512]{1,0:T(8,128)(2,1)S(1)}, u32[]{:S(2)}, u32[]{:S(2)}) collective-permute-start(bf16[224,512]{1,0:T(8,128)(2,1)S(1)} %get-tuple-element.34), channel_id=1, source_target_pairs={{0,1},{1,0},{2,5},{3,4},{4,3},{5,2},{6,7},{7,6},{8,9},{9,8},{10,13... | collective-permute-start | bytes 688136 | tf_op jit(solution)/shard_map/back_0_1/ppermute | solution.py:354
  81.6 0.0 collective-permute-start.16
  81.6 1.5 %collective-permute-start.17 = (bf16[224,512]{1,0:T(8,128)(2,1)S(1)}, bf16[224,512]{1,0:T(8,128)(2,1)S(1)}, u32[]{:S(2)}, u32[]{:S(2)}) collective-permute-start(bf16[224,512]{1,0:T(8,128)(2,1)S(1)} %get-tuple-element.36), channel_id=1, source_target_pairs={{0,3},{1,2},{2,7},{3,6},{4,1},{5,0},{6,5},{7,4},{8,11},{9,10},{10,... | collective-permute-start | bytes 688136 | tf_op jit(solution)/shard_map/back_0_3/ppermute | solution.py:354
  83.1 0.0 collective-permute-done.14.refs_1_
  83.1 6.8 %collective-permute-done.15.refs_2_ = bf16[224,512]{1,0:T(8,128)(2,1)S(1)} collective-permute-done((bf16[224,512]{1,0:T(8,128)(2,1)S(1)}, bf16[224,512]{1,0:T(8,128)(2,1)S(1)}, u32[]{:S(2)}, u32[]{:S(2)}) %collective-permute-start.15) | collective-permute-done | bytes 229408 | tf_op jit(solution)/shard_map/back_0_1/ppermute | solution.py:354
  89.9 0.0 collective-permute-done.16.refs_3_
  89.9 2.4 %collective-permute-done.17.refs_4_ = bf16[224,512]{1,0:T(8,128)(2,1)S(1)} collective-permute-done((bf16[224,512]{1,0:T(8,128)(2,1)S(1)}, bf16[224,512]{1,0:T(8,128)(2,1)S(1)}, u32[]{:S(2)}, u32[]{:S(2)}) %collective-permute-start.17) | collective-permute-done | bytes 229408 | tf_op jit(solution)/shard_map/back_0_3/ppermute | solution.py:354
  92.3 1.0 %join.1 = bf16[1,224,2048]{2,1,0:T(8,128)(2,1)} custom-call(bf16[224,512]{1,0:T(8,128)(2,1)S(1)} %get-tuple-element.33.refs_0_, bf16[224,512]{1,0:T(8,128)(2,1)S(1)} %collective-permute-done.14.refs_1_, bf16[224,512]{1,0:T(8,128)(2,1)S(1)} %collective-permute-done.15.refs_2_, bf16[224,512]{1,0:T(8,128)(2,1)S(1)} %collective-permute-done.16.refs_3_, ...), custom_call_target="tpu_custom_call" | custom-call | tf_op jit(solution)/shard_map/join/pallas_call | solution.py:356
  (4 shorter events, 0.0 us)
Async XLA Ops:
  1.1 2.0 %copy-start = (bf16[1,224,2048]{2,1,0:T(8,128)(2,1)S(1)}, bf16[1,224,2048]{2,1,0:T(8,128)(2,1)}, u32[]{:S(2)}) copy-start(bf16[1,224,2048]{2,1,0:T(8,128)(2,1)} %param.5) | copy-start | bytes 2752516
  2.5 48.1 %copy-start.1 = (bf16[2048]{0:T(1024)(128)(2,1)S(1)}, bf16[2048]{0:T(1024)(128)(2,1)}, u32[]{:S(2)}) copy-start(bf16[2048]{0:T(1024)(128)(2,1)} %param.6) | copy-start | bytes 12292
  2.5 4.5 %collective-permute-start = (bf16[256,1536]{1,0:T(8,128)(2,1)S(1)}, bf16[256,1536]{1,0:T(8,128)(2,1)S(1)}, u32[]{:S(2)}, u32[]{:S(2)}) collective-permute-start(bf16[256,1536]{1,0:T(8,128)(2,1)S(1)} %pad_maximum_fusion), channel_id=1, source_target_pairs={{0,4},{1,5},{2,6},{3,7},{4,0},{5,1},{6,2},{7,3},{8,12},{9,13},{10,... | collective-permute-start | bytes 2359304 | tf_op jit(solution)/shard_map/w1/ppermute | solution.py:271
  3.1 26.2 %collective-permute-start.6 = (bf16[224,2048]{1,0:T(8,128)(2,1)S(1)}, bf16[224,2048]{1,0:T(8,128)(2,1)S(1)}, u32[]{:S(2)}, u32[]{:S(2)}) collective-permute-start(bf16[224,2048]{1,0:T(8,128)(2,1)S(1)} %bitcast.1), channel_id=1, source_target_pairs={{2,0},{3,1},{4,6},{5,7},{10,8},{11,9},{12,14},{13,15},{18,16},{19,... | collective-permute-start | bytes 2752520 | tf_op jit(solution)/shard_map/t2/ppermute | solution.py:271
  4.4 18.0 %collective-permute-start.2 = (bf16[256,1536]{1,0:T(8,128)(2,1)S(1)}, bf16[256,1536]{1,0:T(8,128)(2,1)S(1)}, u32[]{:S(2)}, u32[]{:S(2)}) collective-permute-start(bf16[256,1536]{1,0:T(8,128)(2,1)S(1)} %pad_maximum_fusion.1.refs_8_), channel_id=1, source_target_pairs={{0,8},{1,9},{2,10},{3,11},{4,12},{5,13},{6,14},{7,15},{8,0},{9,1},... | collective-permute-start | bytes 2359304 | tf_op jit(solution)/shard_map/w2/ppermute | solution.py:271
  7.0 18.1 %collective-permute-start.9 = (bf16[256,1536]{1,0:T(8,128)(2,1)S(1)}, bf16[256,1536]{1,0:T(8,128)(2,1)S(1)}, u32[]{:S(2)}, u32[]{:S(2)}) collective-permute-start(bf16[256,1536]{1,0:T(8,128)(2,1)S(1)} %collective-permute-done.refs_9_), channel_id=1, source_target_pairs={{0,16},{1,17},{2,18},{3,19},{4,20},{5,21},{6,22},{7,23},{8,24},{9,... | collective-permute-start | bytes 2359304 | tf_op jit(solution)/shard_map/w5/ppermute | solution.py:271
  8.5 23.0 %collective-permute-start.3 = (bf16[224,2048]{1,0:T(8,128)(2,1)S(1)}, bf16[224,2048]{1,0:T(8,128)(2,1)S(1)}, u32[]{:S(2)}, u32[]{:S(2)}) collective-permute-start(bf16[224,2048]{1,0:T(8,128)(2,1)S(1)} %bitcast.2), channel_id=1, source_target_pairs={{0,1},{1,0},{6,7},{7,6},{8,9},{9,8},{14,15},{15,14},{16,17},{17,16... | collective-permute-start | bytes 2752520 | tf_op jit(solution)/shard_map/t1/ppermute | solution.py:271
  12.0 19.6 %collective-permute-start.4 = (bf16[224,2048]{1,0:T(8,128)(2,1)S(1)}, bf16[224,2048]{1,0:T(8,128)(2,1)S(1)}, u32[]{:S(2)}, u32[]{:S(2)}) collective-permute-start(bf16[224,2048]{1,0:T(8,128)(2,1)S(1)} %bitcast.3), channel_id=1, source_target_pairs={{0,4},{1,5},{6,2},{7,3},{8,12},{9,13},{14,10},{15,11},{16,20},{17,... | collective-permute-start | bytes 2752520 | tf_op jit(solution)/shard_map/u0/ppermute | solution.py:271
  29.2 15.3 %collective-permute-start.10 = (bf16[224,2048]{1,0:T(8,128)(2,1)S(1)}, bf16[224,2048]{1,0:T(8,128)(2,1)S(1)}, u32[]{:S(2)}, u32[]{:S(2)}) collective-permute-start(bf16[224,2048]{1,0:T(8,128)(2,1)S(1)} %collective-permute-done.6.refs_2_), channel_id=1, source_target_pairs={{0,1},{1,0},{6,7},{7,6},{8,9},{9,8},{14,15},{15,14},{16,17},{17,16... | collective-permute-start | bytes 2752520 | tf_op jit(solution)/shard_map/t3/ppermute | solution.py:271
  31.6 18.3 %collective-permute-start.5 = (bf16[224,2048]{1,0:T(8,128)(2,1)S(1)}, bf16[224,2048]{1,0:T(8,128)(2,1)S(1)}, u32[]{:S(2)}, u32[]{:S(2)}) collective-permute-start(bf16[224,2048]{1,0:T(8,128)(2,1)S(1)} %collective-permute-done.3.refs_1_), channel_id=1, source_target_pairs={{0,4},{1,5},{6,2},{7,3},{8,12},{9,13},{14,10},{15,11},{16,20},{17,... | collective-permute-start | bytes 2752520 | tf_op jit(solution)/shard_map/u1/ppermute | solution.py:271
  32.9 17.5 %collective-permute-start.7 = (bf16[224,2048]{1,0:T(8,128)(2,1)S(1)}, bf16[224,2048]{1,0:T(8,128)(2,1)S(1)}, u32[]{:S(2)}, u32[]{:S(2)}) collective-permute-start(bf16[224,2048]{1,0:T(8,128)(2,1)S(1)} %collective-permute-done.6.refs_2_), channel_id=1, source_target_pairs={{0,4},{1,5},{6,2},{7,3},{8,12},{9,13},{14,10},{15,11},{16,20},{17,... | collective-permute-start | bytes 2752520 | tf_op jit(solution)/shard_map/u2/ppermute | solution.py:271
  44.5 16.8 %collective-permute-start.11 = (bf16[224,2048]{1,0:T(8,128)(2,1)S(1)}, bf16[224,2048]{1,0:T(8,128)(2,1)S(1)}, u32[]{:S(2)}, u32[]{:S(2)}) collective-permute-start(bf16[224,2048]{1,0:T(8,128)(2,1)S(1)} %collective-permute-done.10.refs_3_), channel_id=1, source_target_pairs={{0,4},{1,5},{6,2},{7,3},{8,12},{9,13},{14,10},{15,11},{16,20},{17,... | collective-permute-start | bytes 2752520 | tf_op jit(solution)/shard_map/u3/ppermute | solution.py:271
  45.9 14.2 %collective-permute-start.12 = (bf16[256,1536]{1,0:T(8,128)(2,1)S(1)}, bf16[256,1536]{1,0:T(8,128)(2,1)S(1)}, u32[]{:S(2)}, u32[]{:S(2)}) collective-permute-start(bf16[256,1536]{1,0:T(8,128)(2,1)S(1)} %collective-permute-done.2.refs_10_), channel_id=1, source_target_pairs={{0,16},{1,17},{2,18},{3,19},{4,20},{5,21},{6,22},{7,23},{8,24},{9,... | collective-permute-start | bytes 2359304 | tf_op jit(solution)/shard_map/w6/ppermute | solution.py:271
  48.4 12.9 %collective-permute-start.13 = (bf16[256,1536]{1,0:T(8,128)(2,1)S(1)}, bf16[256,1536]{1,0:T(8,128)(2,1)S(1)}, u32[]{:S(2)}, u32[]{:S(2)}) collective-permute-start(bf16[256,1536]{1,0:T(8,128)(2,1)S(1)} %collective-permute-done.9.refs_11_), channel_id=1, source_target_pairs={{0,8},{1,9},{2,10},{3,11},{4,12},{5,13},{6,14},{7,15},{8,0},{9,1},... | collective-permute-start | bytes 2359304 | tf_op jit(solution)/shard_map/w7/ppermute | solution.py:271
  49.9 19.9 %collective-permute-start.1 = (bf16[256,1536]{1,0:T(8,128)(2,1)S(1)}, bf16[256,1536]{1,0:T(8,128)(2,1)S(1)}, u32[]{:S(2)}, u32[]{:S(2)}) collective-permute-start(bf16[256,1536]{1,0:T(8,128)(2,1)S(1)} %collective-permute-done.refs_9_), channel_id=1, source_target_pairs={{0,8},{1,9},{2,10},{3,11},{4,12},{5,13},{6,14},{7,15},{8,0},{9,1},... | collective-permute-start | bytes 2359304 | tf_op jit(solution)/shard_map/w3/ppermute | solution.py:271
  50.4 19.3 %collective-permute-start.8 = (bf16[256,1536]{1,0:T(8,128)(2,1)S(1)}, bf16[256,1536]{1,0:T(8,128)(2,1)S(1)}, u32[]{:S(2)}, u32[]{:S(2)}) collective-permute-start(bf16[256,1536]{1,0:T(8,128)(2,1)S(1)} %pad_maximum_fusion.1.refs_8_), channel_id=1, source_target_pairs={{0,16},{1,17},{2,18},{3,19},{4,20},{5,21},{6,22},{7,23},{8,24},{9,... | collective-permute-start | bytes 2359304 | tf_op jit(solution)/shard_map/w4/ppermute | solution.py:271
  77.9 5.2 %collective-permute-start.14 = (bf16[224,512]{1,0:T(8,128)(2,1)S(1)}, bf16[224,512]{1,0:T(8,128)(2,1)S(1)}, u32[]{:S(2)}, u32[]{:S(2)}) collective-permute-start(bf16[224,512]{1,0:T(8,128)(2,1)S(1)} %get-tuple-element.33.refs_0_), channel_id=1, source_target_pairs={{2,4},{3,5},{4,2},{5,3},{10,12},{11,13},{12,10},{13,11},{18,20},{1... | collective-permute-start | bytes 688136 | tf_op jit(solution)/shard_map/back_0_0/ppermute | solution.py:354
  78.6 11.3 %collective-permute-start.15 = (bf16[224,512]{1,0:T(8,128)(2,1)S(1)}, bf16[224,512]{1,0:T(8,128)(2,1)S(1)}, u32[]{:S(2)}, u32[]{:S(2)}) collective-permute-start(bf16[224,512]{1,0:T(8,128)(2,1)S(1)} %get-tuple-element.34), channel_id=1, source_target_pairs={{0,1},{1,0},{2,5},{3,4},{4,3},{5,2},{6,7},{7,6},{8,9},{9,8},{10,13... | collective-permute-start | bytes 688136 | tf_op jit(solution)/shard_map/back_0_1/ppermute | solution.py:354
  81.6 8.3 %collective-permute-start.16 = (bf16[224,512]{1,0:T(8,128)(2,1)S(1)}, bf16[224,512]{1,0:T(8,128)(2,1)S(1)}, u32[]{:S(2)}, u32[]{:S(2)}) collective-permute-start(bf16[224,512]{1,0:T(8,128)(2,1)S(1)} %get-tuple-element.35), channel_id=1, source_target_pairs={{0,2},{1,3},{2,6},{3,7},{4,0},{5,1},{6,4},{7,5},{8,10},{9,11},{10,... | collective-permute-start | bytes 688136 | tf_op jit(solution)/shard_map/back_0_2/ppermute | solution.py:354
  81.6 10.7 %collective-permute-start.17 = (bf16[224,512]{1,0:T(8,128)(2,1)S(1)}, bf16[224,512]{1,0:T(8,128)(2,1)S(1)}, u32[]{:S(2)}, u32[]{:S(2)}) collective-permute-start(bf16[224,512]{1,0:T(8,128)(2,1)S(1)} %get-tuple-element.36), channel_id=1, source_target_pairs={{0,3},{1,2},{2,7},{3,6},{4,1},{5,0},{6,5},{7,4},{8,11},{9,10},{10,... | collective-permute-start | bytes 688136 | tf_op jit(solution)/shard_map/back_0_3/ppermute | solution.py:354

commit v6 on v5

--- a/solution.py
+++ b/solution.py
@@ -15,17 +15,19 @@
 VMEM_LIMIT = 28 * 1024 * 1024
 
 PLAN = {
-    "order": ["t1", "t2", "w1", "w2", "w5", "u0", "w6", "w7", "u1", "t3", "u2", "w4", "w3", "u3"],
-    "waits": [["w6", ["t1", "u0"]], ["w7", ["w2"]], ["t3", ["w2"]], ["w4", ["u1", "u2"]]],
+    "order": ["t2", "w1", "u0", "w2", "w5", "w7", "t3", "u2", "w3", "u3", "t1", "w6", "u1", "w4"],
+    "waits": [["w6", ["t1", "u0"]], ["w7", ["w2"]], ["t3", ["w2"]], ["w4", ["u1", "u2"]], ["t1", ["cos", "sin"]]],
     "early": [0, 1, 2, 5, 6, 7],
     "splits": [[0, 4]],
-    "hold": [1, 2],
-    "back": [0, 1, 2, 3],
+    "hold": [0, 1, 2, 3],
+    "back": [1, 0, 3, 2],
     "direct3": False,
     "cross3": False,
     "cross5": False,
     "early_flops": 4000000000,
-    "late_flops": 8000000000,
+    "late_flops": 1000000,
+    "norm_flops": 4000000000,
+    "join": [1, 0, 3, 2],
 }
 
 
@@ -57,17 +59,14 @@
     }
 
 
-def early_kernel(rows, order, early, groups, *refs):
-    n = len(groups)
-    kept, sent, shards = refs[:n], refs[n : 2 * n], refs[2 * n : 2 * n + early]
-    gain, out, tail, held, normed, weights, token_sems, weight_sems = refs[2 * n + early :]
+def norm_kernel(rows, order, *refs):
+    kept, sent, shards = refs[:4], refs[4:8], refs[8:12]
+    gain, out, weights, held, token_sems, weight_sems = refs[12:]
     me = role(rows)
     depth = shards[0].shape[0]
     loads = []
-    row = 0
-    for i in range(n):
-        slot = held.at[pl.ds(row, kept[i].shape[0])]
-        row += kept[i].shape[0]
+    for i in range(4):
+        slot = held.at[pl.ds(i * rows, rows)]
         for condition, source in ((me["home"], kept[i]), (jnp.logical_not(me["home"]), sent[i])):
 
             @pl.when(condition)
@@ -85,58 +84,70 @@
         offset = me["owner"] ^ owner
         place = sum(jnp.where(offset == k, at, 0) for at, k in enumerate(order))
         lanes.append(pl.ds(pl.multiple_of(place * depth, depth), depth))
-    at = 0
-    for load, group in zip(loads, groups):
-        load.wait()
-        for _ in group:
-            part = pl.ds(at * rows, rows)
-            at += 1
-            value = normalize(held[part, :], gain[...])
-            for owner, lane in enumerate(lanes):
-                normed[part, lane] = value[:, owner * depth : (owner + 1) * depth]
+    for i in range(4):
+        loads[i].wait()
+        part = pl.ds(i * rows, rows)
+        value = normalize(held[part, :], gain[...])
+        for owner, lane in enumerate(lanes):
+            out[part, lane] = value[:, owner * depth : (owner + 1) * depth]
     for load in weight_loads:
         load.wait()
-    first = early * depth
-    tail[...] = normed[:, first:]
+
+
+def load_shards(shards, weights, sems, lanes):
+    depth = shards[0].shape[0]
+    loads = []
+    for i, shard in enumerate(shards):
+        for j, (source, target, width) in enumerate(lanes):
+            load = pltpu.make_async_copy(
+                shard.at[:, pl.ds(source, width)],
+                weights.at[pl.ds(i * depth, depth), pl.ds(target, width)],
+                sems.at[len(lanes) * i + j],
+            )
+            load.start()
+            loads.append(load)
+    return loads
+
+
+def early_kernel(*refs):
+    normed, first, shards, out, weights, sems = refs[0], refs[1], refs[2:-3], *refs[-3:]
+    columns = out.shape[1]
+    loads = load_shards(shards, weights, sems, [(0, 0, columns)])
+    for load in loads:
+        load.wait()
+    middle, end = first.shape[0], first.shape[0] + weights.shape[0]
     step = 2 * HEAD_DIM
-    for lane in range(0, out.shape[1], step):
-        out[:, lane : lane + step] = jnp.dot(
-            normed[:, :first], weights[:, lane : lane + step], preferred_element_type=jnp.float32
-        )
-
-
-def late_kernel(rows, cols, total, blocks, count, first_head, heads, *refs):
+    for lane in range(0, columns, step):
+        lanes = slice(lane, lane + step)
+        out[:, lanes] = jnp.dot(
+            normed[:, :middle], first[:, lanes], preferred_element_type=jnp.float32
+        ) + jnp.dot(normed[:, middle:end], weights[:, lanes], preferred_element_type=jnp.float32)
+
+
+def late_kernel(rows, cols, total, count, first_head, heads, *refs):
     shards = refs[:count]
-    partial, tail, cos_ref, sin_ref = refs[count : count + 4]
+    partial, normed, cos_ref, sin_ref = refs[count : count + 4]
     outs = refs[count + 4 : count + 4 + total]
     weights, qkv, result, weight_sems, out_sems = refs[count + 4 + total :]
     me = role(rows)
-    depth = shards[0].shape[0]
     width = heads * HEAD_DIM
     start_lane = first_head * HEAD_DIM
-    loads = []
-    for i, shard in enumerate(shards):
-        for j in range(3):
-            load = pltpu.make_async_copy(
-                shard.at[:, pl.ds(j * cols + start_lane, width)],
-                weights.at[pl.ds(i * depth, depth), pl.ds(j * width, width)],
-                weight_sems.at[3 * i + j],
-            )
-            load.start()
-            loads.append(load)
+    loads = load_shards(
+        shards, weights, weight_sems, [(j * cols + start_lane, j * width, width) for j in range(3)]
+    )
     for load in loads:
         load.wait()
+    tail = normed.shape[1] - weights.shape[0]
     step = HEAD_DIM if width % (2 * HEAD_DIM) else 2 * HEAD_DIM
     for j in range(3):
         for lane in range(0, width, step):
             first = j * cols + start_lane + lane
             linear = partial[:, first : first + step] + jnp.dot(
-                tail[...],
+                normed[:, tail:],
                 weights[:, j * width + lane : j * width + lane + step],
                 preferred_element_type=jnp.float32,
             )
-            for i, block in enumerate(blocks):
-                start = me["starts"][block]
+            for i, start in enumerate(me["starts"]):
                 value = linear[i * rows : (i + 1) * rows]
                 if j < 2:
                     cosine = cos_ref[pl.ds(start, rows), :]
@@ -191,13 +202,13 @@
             result[block ^ me, :, lane] = (numer / bottom).astype(jnp.bfloat16)
 
 
-def join_kernel(cols, total, splits, *refs):
+def join_kernel(cols, total, splits, order, *refs):
     out = refs[-1]
     d, c = lax.axis_index("dp"), lax.axis_index("ctx")
     group = d % 2
     for part, (first_head, heads) in enumerate(splits):
         own, *pieces = refs[part * (total + 1) : (part + 1) * (total + 1)]
-        for k in range(total):
+        for piece, k in zip(pieces, order):
             base = c ^ k
             same = base // 2 == group
             plane = jnp.where(same, base, base ^ 2)
@@ -205,9 +216,9 @@
             first = (2 * (plane % 2) + core) * cols + first_head * HEAD_DIM
             lane = pl.ds(pl.multiple_of(first, HEAD_DIM), heads * HEAD_DIM)
             if k:
-                out[0, :, lane] = pieces[k][...]
+                out[0, :, lane] = piece[...]
             else:
-                out[0, :, lane] = jnp.where(c // 2 == group, own[...], pieces[k][...])
+                out[0, :, lane] = jnp.where(c // 2 == group, own[...], piece[...])
 
 
 def fast(dp, ctx, tokens, norm_gain, q_weight, k_weight, v_weight):
@@ -252,7 +263,7 @@
 
     heads = 2 * (c % 2) + d % 2
     values = {"own": tokens[0], "o": columns(heads ^ 1), "m": columns(heads)}
-    inputs = {}
+    values["cos"], values["sin"] = tables(ctx * rows)
     waits = {name: list(earlier) for name, earlier in plan["waits"]}
 
     for name in plan["order"]:
@@ -269,11 +280,10 @@
         ]
         with jax.named_scope(name):
             values[name] = lax.ppermute(operand, ("dp", "ctx"), perm)
-    cosine, sine = tables(ctx * rows)
+    cosine, sine = values["cos"], values["sin"]
     names = {0: "m", 1: "w1", 2: "w2", 3: "w3", 4: "w4", 5: "w5", 6: "w6", 7: "w7"}
     early = plan["early"]
     shard_order = early + [k for k in range(8) if k not in early]
-    blocks = [0, 1, 2, 3]
     kept = [values[n] for n in ("own", "t1", "t2", "t3")]
     sent = [values[n] for n in ("u0", "u1", "u2", "u3")]
 
@@ -281,27 +291,41 @@
     any_space = pl.BlockSpec(memory_space=pl.ANY)
     vmem = pl.BlockSpec(memory_space=pltpu.VMEM)
     n, late = len(early), 8 - len(early)
-    partial, tail = pl.pallas_call(
-        functools.partial(early_kernel, rows, shard_order, n, [[b] for b in blocks]),
+    length = ctx * rows
+    normed, first = pl.pallas_call(
+        functools.partial(norm_kernel, rows, shard_order),
         out_shape=[
-            jax.ShapeDtypeStruct((ctx * rows, 3 * cols), jnp.float32),
-            jax.ShapeDtypeStruct((ctx * rows, late * depth), jnp.bfloat16),
+            jax.ShapeDtypeStruct((length, features), jnp.bfloat16),
+            jax.ShapeDtypeStruct((4 * depth, 3 * cols), jnp.bfloat16),
         ],
-        in_specs=[any_space] * (8 + n) + [vmem],
+        in_specs=[any_space] * 12 + [vmem],
         out_specs=[vmem] * 2,
         scratch_shapes=[
-            pltpu.VMEM((ctx * rows, features), jnp.bfloat16),
-            pltpu.VMEM((ctx * rows, features), jnp.bfloat16),
-            pltpu.VMEM((n * depth, 3 * cols), jnp.bfloat16),
+            pltpu.VMEM((length, features), jnp.bfloat16),
             pltpu.SemaphoreType.DMA((4,)),
-            pltpu.SemaphoreType.DMA((n,)),
+            pltpu.SemaphoreType.DMA((4,)),
+        ],
+        compiler_params=pltpu.CompilerParams(vmem_limit_bytes=VMEM_LIMIT),
+        cost_estimate=pl.CostEstimate(
+            flops=plan["norm_flops"], bytes_accessed=1_000_000, transcendentals=0
+        ),
+        name="normalize",
+    )(*kept, *sent, *[values[names[k]] for k in early[:4]], gain)
+    partial = pl.pallas_call(
+        early_kernel,
+        out_shape=jax.ShapeDtypeStruct((length, 3 * cols), jnp.float32),
+        in_specs=[vmem] * 2 + [any_space] * (n - 4),
+        out_specs=vmem,
+        scratch_shapes=[
+            pltpu.VMEM(((n - 4) * depth, 3 * cols), jnp.bfloat16),
+            pltpu.SemaphoreType.DMA((n - 4,)),
         ],
         compiler_params=pltpu.CompilerParams(vmem_limit_bytes=VMEM_LIMIT),
         cost_estimate=pl.CostEstimate(
             flops=plan["early_flops"], bytes_accessed=1_000_000, transcendentals=0
         ),
         name="project_early",
-    )(*kept, *sent, *[values[names[k]] for k in early], gain)
+    )(normed, first, *[values[names[k]] for k in early[4:]])
 
     def back(k):
         def to(d, c):
@@ -316,7 +340,7 @@
     for part, (first_head, count) in enumerate(plan["splits"]):
         width = count * HEAD_DIM
         pieces = pl.pallas_call(
-            functools.partial(late_kernel, rows, cols, ctx, blocks, late, first_head, count),
+            functools.partial(late_kernel, rows, cols, ctx, late, first_head, count),
             out_shape=[jax.ShapeDtypeStruct((rows, width), jnp.bfloat16)] * ctx,
             in_specs=[any_space] * late + [vmem] * 4,
             out_specs=[any_space] * ctx,
@@ -332,7 +356,7 @@
                 flops=plan["late_flops"], bytes_accessed=1_000_000, transcendentals=0
             ),
             name=f"attend_{part}",
-        )(*last, partial, tail, cosine, sine)
+        )(*last, partial, normed, cosine, sine)
         if arrived:
             hold = plan["hold"]
             both = lax.optimization_barrier((*[arrived[-ctx + k] for k in hold], *pieces))
@@ -352,9 +376,9 @@
                     if to(dd, cc) is not None
                 ]
                 moved[k] = lax.ppermute(pieces[k], ("dp", "ctx"), perm)
-        arrived += [pieces[0]] + [moved[k] for k in range(ctx)]
+        arrived += [pieces[0]] + [moved[k] for k in plan["join"]]
     return pl.pallas_call(
-        functools.partial(join_kernel, cols, ctx, plan["splits"]),
+        functools.partial(join_kernel, cols, ctx, plan["splits"], plan["join"]),
         out_shape=jax.ShapeDtypeStruct((1, rows, ctx * cols), jnp.bfloat16),
         in_specs=[vmem] * len(arrived),
         out_specs=vmem,

time: 94.5 us -> 94.1 us (level)
    pallas_call x3 -> x4, Pallas kernels: 17 us -> 16.8 us  [the longest x1 7.99 us: fast(): pl.pallas_call(functools.partial(late_kernel, rows, cols, ctx, late, firs...]
where the time goes in v6:
time: 94.1 us; the launch traced here: 93 us
  waiting for transfers between devices  43.7 us (46%)
  starting transfers between devices  27.7 us (29%)
  Pallas kernels  16.8 us (18%)
  local copies, waits for them, and re-layouts  2.45 us (3%)
  other arithmetic  2.1 us (2%)
    ppermute x14, waiting for transfers between devices, fast(): values[name] = lax.ppermute(operand, ('dp', 'ctx'), perm)  35.2 us
    ppermute x14, starting transfers between devices, fast(): values[name] = lax.ppermute(operand, ('dp', 'ctx'), perm)  22 us
    ppermute x4, waiting for transfers between devices, fast(): moved[k] = lax.ppermute(pieces[k], ('dp', 'ctx'), perm)  8.52 us
    pallas_call x1, Pallas kernels, fast(): pl.pallas_call(functools.partial(late_kernel, rows, cols, ctx, late, firs...  7.99 us
    ppermute x4, starting transfers between devices, fast(): moved[k] = lax.ppermute(pieces[k], ('dp', 'ctx'), perm)  5.65 us
    pallas_call x1, Pallas kernels, fast(): pl.pallas_call(early_kernel, out_shape=jax.ShapeDtypeStruct((length, 3 *...  4.54 us
    pallas_call x1, Pallas kernels, fast(): pl.pallas_call(functools.partial(norm_kernel, rows, shard_order), out_sha...  3.26 us
    dynamic_slice x2, local copies, waits for them, and re-layouts, columns(): lax.dynamic_slice_in_dim(w, heads * cols, cols, 1)  2.43 us
  transfers between devices with their start and end apart: 18, of which 10 were waited for; matrix products, arithmetic and copies ran while one was open for 2% of the time, Pallas kernels for 8%

profile of v6, /device:TPU:0, one launch (start us, length us, event | category | flops | bytes accessed | tf_op | source)
XLA Modules:
  0.0 93.0 jit_solution(16336126169663950237)
XLA Ops:
  0.0 1.1 %constant_dynamic-slice_fusion.2 = (bf16[256,512]{1,0:T(8,128)(2,1)S(1)}, bf16[256,512]{1,0:T(8,128)(2,1)S(1)}) fusion(bf16[256,2048]{1,0:T(8,128)(2,1)} %param.7, s32[]{:T(128)S(6)} %select_n.24, s32[]{:T(128)S(6)} %select_n.23), kind=kLoop, calls=%fused_computation.10 | loop fusion | bytes 1048584 | tf_op jit(solution)/shard_map/dynamic_slice | solution.py:260
  1.1 0.0 copy-start
  1.1 1.4 %constant_dynamic-slice_fusion = (bf16[256,512]{1,0:T(8,128)(2,1)S(1)}, bf16[256,512]{1,0:T(8,128)(2,1)S(1)}, bf16[256,512]{1,0:T(8,128)(2,1)S(1)}, bf16[256,512]{1,0:T(8,128)(2,1)S(1)}) fusion(bf16[256,2048]{1,0:T(8,128)(2,1)} %param.9, s32[]{:T(128)S(6)} %select_n.24, s32[]{:T(128)S(6)} %select_n.23, bf16[256,2048]{1,0:T(8,128)(2,1)} %param.8), kind=kLoop, calls=%fused_computation.8 | loop fusion | bytes 2097160 | tf_op jit(solution)/shard_map/dynamic_slice | solution.py:260
  2.5 0.1 pad_maximum_fusion
  2.5 0.5 collective-permute-start
  3.0 1.3 %collective-permute-start.2 = (bf16[224,2048]{1,0:T(8,128)(2,1)S(1)}, bf16[224,2048]{1,0:T(8,128)(2,1)S(1)}, u32[]{:S(2)}, u32[]{:S(2)}) collective-permute-start(bf16[224,2048]{1,0:T(8,128)(2,1)S(1)} %bitcast.1), channel_id=1, source_target_pairs={{2,0},{3,1},{4,6},{5,7},{10,8},{11,9},{12,14},{13,15},{18,16},{19,... | collective-permute-start | bytes 2752520 | tf_op jit(solution)/shard_map/t2/ppermute | solution.py:282
  4.3 0.1 pad_maximum_fusion.1.refs_8_
  4.4 2.6 %collective-permute-start.4 = (bf16[256,1536]{1,0:T(8,128)(2,1)S(1)}, bf16[256,1536]{1,0:T(8,128)(2,1)S(1)}, u32[]{:S(2)}, u32[]{:S(2)}) collective-permute-start(bf16[256,1536]{1,0:T(8,128)(2,1)S(1)} %pad_maximum_fusion.1.refs_8_), channel_id=1, source_target_pairs={{0,8},{1,9},{2,10},{3,11},{4,12},{5,13},{6,14},{7,15},{8,0},{9,1},... | collective-permute-start | bytes 2359304 | tf_op jit(solution)/shard_map/w2/ppermute | solution.py:282
  7.0 0.0 collective-permute-done.refs_9_
  7.0 1.5 %collective-permute-start.3 = (bf16[256,1536]{1,0:T(8,128)(2,1)S(1)}, bf16[256,1536]{1,0:T(8,128)(2,1)S(1)}, u32[]{:S(2)}, u32[]{:S(2)}) collective-permute-start(bf16[256,1536]{1,0:T(8,128)(2,1)S(1)} %collective-permute-done.refs_9_), channel_id=1, source_target_pairs={{0,16},{1,17},{2,18},{3,19},{4,20},{5,21},{6,22},{7,23},{8,24},{9,... | collective-permute-start | bytes 2359304 | tf_op jit(solution)/shard_map/w5/ppermute | solution.py:282
  8.5 0.0 copy-start.1
  8.5 1.7 %fusion = (f32[896,64]{1,0:T(8,128)S(1)}, f32[896,64]{1,0:T(8,128)S(1)}, f32[896,64]{1,0:T(8,128)S(1)}) fusion(f32[64]{0:T(128)S(1)} %multiply_power_fusion, f32[896]{0:T(1024)S(1)} %iota_convert_fusion), kind=kLoop, calls=%fused_computation.6 | loop fusion | flops 114688 | bytes 691968 | tf_op jit(solution)/shard_map/neg | solution.py:41
  10.2 0.3 pad_maximum_fusion.2
  10.5 3.5 %collective-permute-start.5 = (bf16[224,2048]{1,0:T(8,128)(2,1)S(1)}, bf16[224,2048]{1,0:T(8,128)(2,1)S(1)}, u32[]{:S(2)}, u32[]{:S(2)}) collective-permute-start(bf16[224,2048]{1,0:T(8,128)(2,1)S(1)} %bitcast.2), channel_id=1, source_target_pairs={{0,1},{1,0},{6,7},{7,6},{8,9},{9,8},{14,15},{15,14},{16,17},{17,16... | collective-permute-start | bytes 2752520 | tf_op jit(solution)/shard_map/t1/ppermute | solution.py:282
  14.0 2.1 %collective-permute-start.6 = (bf16[224,2048]{1,0:T(8,128)(2,1)S(1)}, bf16[224,2048]{1,0:T(8,128)(2,1)S(1)}, u32[]{:S(2)}, u32[]{:S(2)}) collective-permute-start(bf16[224,2048]{1,0:T(8,128)(2,1)S(1)} %bitcast.3), channel_id=1, source_target_pairs={{0,4},{1,5},{6,2},{7,3},{8,12},{9,13},{14,10},{15,11},{16,20},{17,... | collective-permute-start | bytes 2752520 | tf_op jit(solution)/shard_map/u0/ppermute | solution.py:282
  16.1 6.2 %collective-permute-done.4.refs_10_ = bf16[256,1536]{1,0:T(8,128)(2,1)S(1)} collective-permute-done((bf16[256,1536]{1,0:T(8,128)(2,1)S(1)}, bf16[256,1536]{1,0:T(8,128)(2,1)S(1)}, u32[]{:S(2)}, u32[]{:S(2)}) %collective-permute-start.4) | collective-permute-done | bytes 786464 | tf_op jit(solution)/shard_map/w2/ppermute | solution.py:282
  22.4 2.8 %collective-permute-done.3.refs_11_ = bf16[256,1536]{1,0:T(8,128)(2,1)S(1)} collective-permute-done((bf16[256,1536]{1,0:T(8,128)(2,1)S(1)}, bf16[256,1536]{1,0:T(8,128)(2,1)S(1)}, u32[]{:S(2)}, u32[]{:S(2)}) %collective-permute-start.3) | collective-permute-done | bytes 786464 | tf_op jit(solution)/shard_map/w5/ppermute | solution.py:282
  25.1 4.1 %collective-permute-done.2.refs_2_ = bf16[224,2048]{1,0:T(8,128)(2,1)S(1)} collective-permute-done((bf16[224,2048]{1,0:T(8,128)(2,1)S(1)}, bf16[224,2048]{1,0:T(8,128)(2,1)S(1)}, u32[]{:S(2)}, u32[]{:S(2)}) %collective-permute-start.2) | collective-permute-done | bytes 917536 | tf_op jit(solution)/shard_map/t2/ppermute | solution.py:282
  29.2 1.9 %collective-permute-start.10 = (bf16[224,2048]{1,0:T(8,128)(2,1)S(1)}, bf16[224,2048]{1,0:T(8,128)(2,1)S(1)}, u32[]{:S(2)}, u32[]{:S(2)}) collective-permute-start(bf16[224,2048]{1,0:T(8,128)(2,1)S(1)} %collective-permute-done.2.refs_2_), channel_id=1, source_target_pairs={{0,1},{1,0},{6,7},{7,6},{8,9},{9,8},{14,15},{15,14},{16,17},{17,16... | collective-permute-start | bytes 2752520 | tf_op jit(solution)/shard_map/t3/ppermute | solution.py:282
  31.1 1.3 %collective-permute-start.8 = (bf16[224,2048]{1,0:T(8,128)(2,1)S(1)}, bf16[224,2048]{1,0:T(8,128)(2,1)S(1)}, u32[]{:S(2)}, u32[]{:S(2)}) collective-permute-start(bf16[224,2048]{1,0:T(8,128)(2,1)S(1)} %collective-permute-done.2.refs_2_), channel_id=1, source_target_pairs={{0,4},{1,5},{6,2},{7,3},{8,12},{9,13},{14,10},{15,11},{16,20},{17,... | collective-permute-start | bytes 2752520 | tf_op jit(solution)/shard_map/u2/ppermute | solution.py:282
  32.5 1.1 %collective-permute-done.5.refs_1_ = bf16[224,2048]{1,0:T(8,128)(2,1)S(1)} collective-permute-done((bf16[224,2048]{1,0:T(8,128)(2,1)S(1)}, bf16[224,2048]{1,0:T(8,128)(2,1)S(1)}, u32[]{:S(2)}, u32[]{:S(2)}) %collective-permute-start.5) | collective-permute-done | bytes 917536 | tf_op jit(solution)/shard_map/t1/ppermute | solution.py:282
  33.6 0.0 collective-permute-done.6.refs_4_
  33.6 1.3 %collective-permute-start.7 = (bf16[224,2048]{1,0:T(8,128)(2,1)S(1)}, bf16[224,2048]{1,0:T(8,128)(2,1)S(1)}, u32[]{:S(2)}, u32[]{:S(2)}) collective-permute-start(bf16[224,2048]{1,0:T(8,128)(2,1)S(1)} %collective-permute-done.5.refs_1_), channel_id=1, source_target_pairs={{0,4},{1,5},{6,2},{7,3},{8,12},{9,13},{14,10},{15,11},{16,20},{17,... | collective-permute-start | bytes 2752520 | tf_op jit(solution)/shard_map/u1/ppermute | solution.py:282
  34.9 9.6 %collective-permute-done.10.refs_3_ = bf16[224,2048]{1,0:T(8,128)(2,1)S(1)} collective-permute-done((bf16[224,2048]{1,0:T(8,128)(2,1)S(1)}, bf16[224,2048]{1,0:T(8,128)(2,1)S(1)}, u32[]{:S(2)}, u32[]{:S(2)}) %collective-permute-start.10) | collective-permute-done | bytes 917536 | tf_op jit(solution)/shard_map/t3/ppermute | solution.py:282
  44.5 1.3 %collective-permute-start.11 = (bf16[224,2048]{1,0:T(8,128)(2,1)S(1)}, bf16[224,2048]{1,0:T(8,128)(2,1)S(1)}, u32[]{:S(2)}, u32[]{:S(2)}) collective-permute-start(bf16[224,2048]{1,0:T(8,128)(2,1)S(1)} %collective-permute-done.10.refs_3_), channel_id=1, source_target_pairs={{0,4},{1,5},{6,2},{7,3},{8,12},{9,13},{14,10},{15,11},{16,20},{17,... | collective-permute-start | bytes 2752520 | tf_op jit(solution)/shard_map/u3/ppermute | solution.py:282
  45.9 2.5 %collective-permute-start.12 = (bf16[256,1536]{1,0:T(8,128)(2,1)S(1)}, bf16[256,1536]{1,0:T(8,128)(2,1)S(1)}, u32[]{:S(2)}, u32[]{:S(2)}) collective-permute-start(bf16[256,1536]{1,0:T(8,128)(2,1)S(1)} %collective-permute-done.4.refs_10_), channel_id=1, source_target_pairs={{0,16},{1,17},{2,18},{3,19},{4,20},{5,21},{6,22},{7,23},{8,24},{9,... | collective-permute-start | bytes 2359304 | tf_op jit(solution)/shard_map/w6/ppermute | solution.py:282
  48.4 1.5 %collective-permute-start.13 = (bf16[256,1536]{1,0:T(8,128)(2,1)S(1)}, bf16[256,1536]{1,0:T(8,128)(2,1)S(1)}, u32[]{:S(2)}, u32[]{:S(2)}) collective-permute-start(bf16[256,1536]{1,0:T(8,128)(2,1)S(1)} %collective-permute-done.3.refs_11_), channel_id=1, source_target_pairs={{0,8},{1,9},{2,10},{3,11},{4,12},{5,13},{6,14},{7,15},{8,0},{9,1},... | collective-permute-start | bytes 2359304 | tf_op jit(solution)/shard_map/w7/ppermute | solution.py:282
  49.9 0.0 collective-permute-done.8.refs_6_
  49.9 0.5 collective-permute-start.1
  50.4 0.0 collective-permute-done.7.refs_5_
  50.4 0.1 collective-permute-start.9
  50.5 0.0 collective-permute-done.11.refs_7_
  50.5 3.3 %normalize.1 = (bf16[896,2048]{1,0:T(8,128)(2,1)S(1)}, bf16[1024,1536]{1,0:T(8,128)(2,1)S(1)}) custom-call(bf16[224,2048]{1,0:T(8,128)(2,1)S(1)} %bitcast.4, bf16[224,2048]{1,0:T(8,128)(2,1)S(1)} %collective-permute-done.5.refs_1_, bf16[224,2048]{1,0:T(8,128)(2,1)S(1)} %collective-permute-done.2.refs_2_, ...), custom_call_target="tpu_custom_call" | custom-call | flops 4000000000 | bytes 1000000 | tf_op jit(solution)/shard_map/normalize/pallas_call | solution.py:295
  53.8 6.3 %collective-permute-done.12.refs_2_ = bf16[256,1536]{1,0:T(8,128)(2,1)S(1)} collective-permute-done((bf16[256,1536]{1,0:T(8,128)(2,1)S(1)}, bf16[256,1536]{1,0:T(8,128)(2,1)S(1)}, u32[]{:S(2)}, u32[]{:S(2)}) %collective-permute-start.12) | collective-permute-done | bytes 786464 | tf_op jit(solution)/shard_map/w6/ppermute | solution.py:282
  60.1 1.2 %collective-permute-done.13.refs_3_ = bf16[256,1536]{1,0:T(8,128)(2,1)S(1)} collective-permute-done((bf16[256,1536]{1,0:T(8,128)(2,1)S(1)}, bf16[256,1536]{1,0:T(8,128)(2,1)S(1)}, u32[]{:S(2)}, u32[]{:S(2)}) %collective-permute-start.13) | collective-permute-done | bytes 786464 | tf_op jit(solution)/shard_map/w7/ppermute | solution.py:282
  61.3 4.5 %project_early.1.refs_2_ = f32[896,1536]{1,0:T(8,128)S(1)} custom-call(bf16[896,2048]{1,0:T(8,128)(2,1)S(1)} %get-tuple-element.33.refs_0_.refs_3_, bf16[1024,1536]{1,0:T(8,128)(2,1)S(1)} %get-tuple-element.34.refs_1_, bf16[256,1536]{1,0:T(8,128)(2,1)S(1)} %collective-permute-done.12.refs_2_, bf16[256,1536]{1,0:T(8,128)(2,1)S(1)} %collective-permute-done.13.refs_3_), custom_call_target="tpu_custom_call" | custom-call | flops 4000000000 | bytes 1000000 | tf_op jit(solution)/shard_map/project_early/pallas_call | solution.py:314
  65.9 3.9 %collective-permute-done.1.refs_0_ = bf16[256,1536]{1,0:T(8,128)(2,1)S(1)} collective-permute-done((bf16[256,1536]{1,0:T(8,128)(2,1)S(1)}, bf16[256,1536]{1,0:T(8,128)(2,1)S(1)}, u32[]{:S(2)}, u32[]{:S(2)}) %collective-permute-start.1) | collective-permute-done | bytes 786464 | tf_op jit(solution)/shard_map/w3/ppermute | solution.py:282
  69.8 0.0 collective-permute-done.9.refs_1_
  69.8 8.0 %attend_0.1 = (bf16[224,512]{1,0:T(8,128)(2,1)S(1)}, bf16[224,512]{1,0:T(8,128)(2,1)S(1)}, bf16[224,512]{1,0:T(8,128)(2,1)S(1)}, bf16[224,512]{1,0:T(8,128)(2,1)S(1)}) custom-call(bf16[256,1536]{1,0:T(8,128)(2,1)S(1)} %collective-permute-done.1.refs_0_, bf16[256,1536]{1,0:T(8,128)(2,1)S(1)} %collective-permute-done.9.refs_1_, ...), custom_call_target="tpu_custom_call" | custom-call | flops 1000000 | bytes 1000000 | tf_op jit(solution)/shard_map/attend_0/pallas_call | solution.py:342
  77.8 3.0 %collective-permute-start.14 = (bf16[224,512]{1,0:T(8,128)(2,1)S(1)}, bf16[224,512]{1,0:T(8,128)(2,1)S(1)}, u32[]{:S(2)}, u32[]{:S(2)}) collective-permute-start(bf16[224,512]{1,0:T(8,128)(2,1)S(1)} %get-tuple-element.40), channel_id=1, source_target_pairs={{0,1},{1,0},{2,5},{3,4},{4,3},{5,2},{6,7},{7,6},{8,9},{9,8},{10,13... | collective-permute-start | bytes 688136 | tf_op jit(solution)/shard_map/back_0_1/ppermute | solution.py:378
  80.7 0.7 collective-permute-start.15
  81.4 0.1 collective-permute-start.16
  81.5 2.0 %collective-permute-start.17 = (bf16[224,512]{1,0:T(8,128)(2,1)S(1)}, bf16[224,512]{1,0:T(8,128)(2,1)S(1)}, u32[]{:S(2)}, u32[]{:S(2)}) collective-permute-start(bf16[224,512]{1,0:T(8,128)(2,1)S(1)} %get-tuple-element.42), channel_id=1, source_target_pairs={{0,2},{1,3},{2,6},{3,7},{4,0},{5,1},{6,4},{7,5},{8,10},{9,11},{10,... | collective-permute-start | bytes 688136 | tf_op jit(solution)/shard_map/back_0_2/ppermute | solution.py:378
  83.4 3.1 %collective-permute-done.14.refs_1_ = bf16[224,512]{1,0:T(8,128)(2,1)S(1)} collective-permute-done((bf16[224,512]{1,0:T(8,128)(2,1)S(1)}, bf16[224,512]{1,0:T(8,128)(2,1)S(1)}, u32[]{:S(2)}, u32[]{:S(2)}) %collective-permute-start.14) | collective-permute-done | bytes 229408 | tf_op jit(solution)/shard_map/back_0_1/ppermute | solution.py:378
  86.5 0.0 collective-permute-done.15.refs_2_
  86.5 5.4 %collective-permute-done.16.refs_3_ = bf16[224,512]{1,0:T(8,128)(2,1)S(1)} collective-permute-done((bf16[224,512]{1,0:T(8,128)(2,1)S(1)}, bf16[224,512]{1,0:T(8,128)(2,1)S(1)}, u32[]{:S(2)}, u32[]{:S(2)}) %collective-permute-start.16) | collective-permute-done | bytes 229408 | tf_op jit(solution)/shard_map/back_0_3/ppermute | solution.py:378
  91.9 0.0 collective-permute-done.17.refs_4_
  92.0 1.0 %join.1 = bf16[1,224,2048]{2,1,0:T(8,128)(2,1)} custom-call(bf16[224,512]{1,0:T(8,128)(2,1)S(1)} %get-tuple-element.39.refs_0_, bf16[224,512]{1,0:T(8,128)(2,1)S(1)} %collective-permute-done.14.refs_1_, bf16[224,512]{1,0:T(8,128)(2,1)S(1)} %collective-permute-done.15.refs_2_, bf16[224,512]{1,0:T(8,128)(2,1)S(1)} %collective-permute-done.16.refs_3_, ...), custom_call_target="tpu_custom_call" | custom-call | tf_op jit(solution)/shard_map/join/pallas_call | solution.py:380
  (5 shorter events, 0.0 us)
Async XLA Ops:
  1.1 2.0 %copy-start = (bf16[1,224,2048]{2,1,0:T(8,128)(2,1)S(1)}, bf16[1,224,2048]{2,1,0:T(8,128)(2,1)}, u32[]{:S(2)}) copy-start(bf16[1,224,2048]{2,1,0:T(8,128)(2,1)} %param.5) | copy-start | bytes 2752516
  2.5 4.5 %collective-permute-start = (bf16[256,1536]{1,0:T(8,128)(2,1)S(1)}, bf16[256,1536]{1,0:T(8,128)(2,1)S(1)}, u32[]{:S(2)}, u32[]{:S(2)}) collective-permute-start(bf16[256,1536]{1,0:T(8,128)(2,1)S(1)} %pad_maximum_fusion), channel_id=1, source_target_pairs={{0,4},{1,5},{2,6},{3,7},{4,0},{5,1},{6,2},{7,3},{8,12},{9,13},{10,... | collective-permute-start | bytes 2359304 | tf_op jit(solution)/shard_map/w1/ppermute | solution.py:282
  3.0 26.2 %collective-permute-start.2 = (bf16[224,2048]{1,0:T(8,128)(2,1)S(1)}, bf16[224,2048]{1,0:T(8,128)(2,1)S(1)}, u32[]{:S(2)}, u32[]{:S(2)}) collective-permute-start(bf16[224,2048]{1,0:T(8,128)(2,1)S(1)} %bitcast.1), channel_id=1, source_target_pairs={{2,0},{3,1},{4,6},{5,7},{10,8},{11,9},{12,14},{13,15},{18,16},{19,... | collective-permute-start | bytes 2752520 | tf_op jit(solution)/shard_map/t2/ppermute | solution.py:282
  4.4 18.0 %collective-permute-start.4 = (bf16[256,1536]{1,0:T(8,128)(2,1)S(1)}, bf16[256,1536]{1,0:T(8,128)(2,1)S(1)}, u32[]{:S(2)}, u32[]{:S(2)}) collective-permute-start(bf16[256,1536]{1,0:T(8,128)(2,1)S(1)} %pad_maximum_fusion.1.refs_8_), channel_id=1, source_target_pairs={{0,8},{1,9},{2,10},{3,11},{4,12},{5,13},{6,14},{7,15},{8,0},{9,1},... | collective-permute-start | bytes 2359304 | tf_op jit(solution)/shard_map/w2/ppermute | solution.py:282
  7.0 18.1 %collective-permute-start.3 = (bf16[256,1536]{1,0:T(8,128)(2,1)S(1)}, bf16[256,1536]{1,0:T(8,128)(2,1)S(1)}, u32[]{:S(2)}, u32[]{:S(2)}) collective-permute-start(bf16[256,1536]{1,0:T(8,128)(2,1)S(1)} %collective-permute-done.refs_9_), channel_id=1, source_target_pairs={{0,16},{1,17},{2,18},{3,19},{4,20},{5,21},{6,22},{7,23},{8,24},{9,... | collective-permute-start | bytes 2359304 | tf_op jit(solution)/shard_map/w5/ppermute | solution.py:282
  8.5 42.0 %copy-start.1 = (bf16[2048]{0:T(1024)(128)(2,1)S(1)}, bf16[2048]{0:T(1024)(128)(2,1)}, u32[]{:S(2)}) copy-start(bf16[2048]{0:T(1024)(128)(2,1)} %param.6) | copy-start | bytes 12292
  10.5 23.1 %collective-permute-start.5 = (bf16[224,2048]{1,0:T(8,128)(2,1)S(1)}, bf16[224,2048]{1,0:T(8,128)(2,1)S(1)}, u32[]{:S(2)}, u32[]{:S(2)}) collective-permute-start(bf16[224,2048]{1,0:T(8,128)(2,1)S(1)} %bitcast.2), channel_id=1, source_target_pairs={{0,1},{1,0},{6,7},{7,6},{8,9},{9,8},{14,15},{15,14},{16,17},{17,16... | collective-permute-start | bytes 2752520 | tf_op jit(solution)/shard_map/t1/ppermute | solution.py:282
  14.0 19.6 %collective-permute-start.6 = (bf16[224,2048]{1,0:T(8,128)(2,1)S(1)}, bf16[224,2048]{1,0:T(8,128)(2,1)S(1)}, u32[]{:S(2)}, u32[]{:S(2)}) collective-permute-start(bf16[224,2048]{1,0:T(8,128)(2,1)S(1)} %bitcast.3), channel_id=1, source_target_pairs={{0,4},{1,5},{6,2},{7,3},{8,12},{9,13},{14,10},{15,11},{16,20},{17,... | collective-permute-start | bytes 2752520 | tf_op jit(solution)/shard_map/u0/ppermute | solution.py:282
  29.2 15.3 %collective-permute-start.10 = (bf16[224,2048]{1,0:T(8,128)(2,1)S(1)}, bf16[224,2048]{1,0:T(8,128)(2,1)S(1)}, u32[]{:S(2)}, u32[]{:S(2)}) collective-permute-start(bf16[224,2048]{1,0:T(8,128)(2,1)S(1)} %collective-permute-done.2.refs_2_), channel_id=1, source_target_pairs={{0,1},{1,0},{6,7},{7,6},{8,9},{9,8},{14,15},{15,14},{16,17},{17,16... | collective-permute-start | bytes 2752520 | tf_op jit(solution)/shard_map/t3/ppermute | solution.py:282
  31.1 18.7 %collective-permute-start.8 = (bf16[224,2048]{1,0:T(8,128)(2,1)S(1)}, bf16[224,2048]{1,0:T(8,128)(2,1)S(1)}, u32[]{:S(2)}, u32[]{:S(2)}) collective-permute-start(bf16[224,2048]{1,0:T(8,128)(2,1)S(1)} %collective-permute-done.2.refs_2_), channel_id=1, source_target_pairs={{0,4},{1,5},{6,2},{7,3},{8,12},{9,13},{14,10},{15,11},{16,20},{17,... | collective-permute-start | bytes 2752520 | tf_op jit(solution)/shard_map/u2/ppermute | solution.py:282
  33.6 16.8 %collective-permute-start.7 = (bf16[224,2048]{1,0:T(8,128)(2,1)S(1)}, bf16[224,2048]{1,0:T(8,128)(2,1)S(1)}, u32[]{:S(2)}, u32[]{:S(2)}) collective-permute-start(bf16[224,2048]{1,0:T(8,128)(2,1)S(1)} %collective-permute-done.5.refs_1_), channel_id=1, source_target_pairs={{0,4},{1,5},{6,2},{7,3},{8,12},{9,13},{14,10},{15,11},{16,20},{17,... | collective-permute-start | bytes 2752520 | tf_op jit(solution)/shard_map/u1/ppermute | solution.py:282
  44.5 6.0 %collective-permute-start.11 = (bf16[224,2048]{1,0:T(8,128)(2,1)S(1)}, bf16[224,2048]{1,0:T(8,128)(2,1)S(1)}, u32[]{:S(2)}, u32[]{:S(2)}) collective-permute-start(bf16[224,2048]{1,0:T(8,128)(2,1)S(1)} %collective-permute-done.10.refs_3_), channel_id=1, source_target_pairs={{0,4},{1,5},{6,2},{7,3},{8,12},{9,13},{14,10},{15,11},{16,20},{17,... | collective-permute-start | bytes 2752520 | tf_op jit(solution)/shard_map/u3/ppermute | solution.py:282
  45.9 14.2 %collective-permute-start.12 = (bf16[256,1536]{1,0:T(8,128)(2,1)S(1)}, bf16[256,1536]{1,0:T(8,128)(2,1)S(1)}, u32[]{:S(2)}, u32[]{:S(2)}) collective-permute-start(bf16[256,1536]{1,0:T(8,128)(2,1)S(1)} %collective-permute-done.4.refs_10_), channel_id=1, source_target_pairs={{0,16},{1,17},{2,18},{3,19},{4,20},{5,21},{6,22},{7,23},{8,24},{9,... | collective-permute-start | bytes 2359304 | tf_op jit(solution)/shard_map/w6/ppermute | solution.py:282
  48.4 13.0 %collective-permute-start.13 = (bf16[256,1536]{1,0:T(8,128)(2,1)S(1)}, bf16[256,1536]{1,0:T(8,128)(2,1)S(1)}, u32[]{:S(2)}, u32[]{:S(2)}) collective-permute-start(bf16[256,1536]{1,0:T(8,128)(2,1)S(1)} %collective-permute-done.3.refs_11_), channel_id=1, source_target_pairs={{0,8},{1,9},{2,10},{3,11},{4,12},{5,13},{6,14},{7,15},{8,0},{9,1},... | collective-permute-start | bytes 2359304 | tf_op jit(solution)/shard_map/w7/ppermute | solution.py:282
  49.9 19.9 %collective-permute-start.1 = (bf16[256,1536]{1,0:T(8,128)(2,1)S(1)}, bf16[256,1536]{1,0:T(8,128)(2,1)S(1)}, u32[]{:S(2)}, u32[]{:S(2)}) collective-permute-start(bf16[256,1536]{1,0:T(8,128)(2,1)S(1)} %collective-permute-done.refs_9_), channel_id=1, source_target_pairs={{0,8},{1,9},{2,10},{3,11},{4,12},{5,13},{6,14},{7,15},{8,0},{9,1},... | collective-permute-start | bytes 2359304 | tf_op jit(solution)/shard_map/w3/ppermute | solution.py:282
  50.4 19.4 %collective-permute-start.9 = (bf16[256,1536]{1,0:T(8,128)(2,1)S(1)}, bf16[256,1536]{1,0:T(8,128)(2,1)S(1)}, u32[]{:S(2)}, u32[]{:S(2)}) collective-permute-start(bf16[256,1536]{1,0:T(8,128)(2,1)S(1)} %pad_maximum_fusion.1.refs_8_), channel_id=1, source_target_pairs={{0,16},{1,17},{2,18},{3,19},{4,20},{5,21},{6,22},{7,23},{8,24},{9,... | collective-permute-start | bytes 2359304 | tf_op jit(solution)/shard_map/w4/ppermute | solution.py:282
  77.8 8.8 %collective-permute-start.14 = (bf16[224,512]{1,0:T(8,128)(2,1)S(1)}, bf16[224,512]{1,0:T(8,128)(2,1)S(1)}, u32[]{:S(2)}, u32[]{:S(2)}) collective-permute-start(bf16[224,512]{1,0:T(8,128)(2,1)S(1)} %get-tuple-element.40), channel_id=1, source_target_pairs={{0,1},{1,0},{2,5},{3,4},{4,3},{5,2},{6,7},{7,6},{8,9},{9,8},{10,13... | collective-permute-start | bytes 688136 | tf_op jit(solution)/shard_map/back_0_1/ppermute | solution.py:378
  80.7 5.8 %collective-permute-start.15 = (bf16[224,512]{1,0:T(8,128)(2,1)S(1)}, bf16[224,512]{1,0:T(8,128)(2,1)S(1)}, u32[]{:S(2)}, u32[]{:S(2)}) collective-permute-start(bf16[224,512]{1,0:T(8,128)(2,1)S(1)} %get-tuple-element.39.refs_0_), channel_id=1, source_target_pairs={{2,4},{3,5},{4,2},{5,3},{10,12},{11,13},{12,10},{13,11},{18,20},{1... | collective-permute-start | bytes 688136 | tf_op jit(solution)/shard_map/back_0_0/ppermute | solution.py:378
  81.4 10.5 %collective-permute-start.16 = (bf16[224,512]{1,0:T(8,128)(2,1)S(1)}, bf16[224,512]{1,0:T(8,128)(2,1)S(1)}, u32[]{:S(2)}, u32[]{:S(2)}) collective-permute-start(bf16[224,512]{1,0:T(8,128)(2,1)S(1)} %get-tuple-element.41), channel_id=1, source_target_pairs={{0,3},{1,2},{2,7},{3,6},{4,1},{5,0},{6,5},{7,4},{8,11},{9,10},{10,... | collective-permute-start | bytes 688136 | tf_op jit(solution)/shard_map/back_0_3/ppermute | solution.py:378
  81.5 10.5 %collective-permute-start.17 = (bf16[224,512]{1,0:T(8,128)(2,1)S(1)}, bf16[224,512]{1,0:T(8,128)(2,1)S(1)}, u32[]{:S(2)}, u32[]{:S(2)}) collective-permute-start(bf16[224,512]{1,0:T(8,128)(2,1)S(1)} %get-tuple-element.42), channel_id=1, source_target_pairs={{0,2},{1,3},{2,6},{3,7},{4,0},{5,1},{6,4},{7,5},{8,10},{9,11},{10,... | collective-permute-start | bytes 688136 | tf_op jit(solution)/shard_map/back_0_2/ppermute | solution.py:378

commit v7 on v6

--- a/solution.py
+++ b/solution.py
@@ -19,7 +19,7 @@
     "waits": [["w6", ["t1", "u0"]], ["w7", ["w2"]], ["t3", ["w2"]], ["w4", ["u1", "u2"]], ["t1", ["cos", "sin"]]],
     "early": [0, 1, 2, 5, 6, 7],
     "splits": [[0, 4]],
-    "hold": [0, 1, 2, 3],
+    "hold": [],
     "back": [1, 0, 3, 2],
     "direct3": False,
     "cross3": False,
@@ -135,11 +135,11 @@
     loads = load_shards(
         shards, weights, weight_sems, [(j * cols + start_lane, j * width, width) for j in range(3)]
     )
-    for load in loads:
-        load.wait()
     tail = normed.shape[1] - weights.shape[0]
     step = HEAD_DIM if width % (2 * HEAD_DIM) else 2 * HEAD_DIM
     for j in range(3):
+        for load in loads[j::3]:
+            load.wait()
         for lane in range(0, width, step):
             first = j * cols + start_lane + lane
             linear = partial[:, first : first + step] + jnp.dot(

time: 94.1 us -> 94.8 us (level)
  no operation moved by 1% of the time
where the time goes in v7:
time: 94.8 us; the launch traced here: 93.8 us
  waiting for transfers between devices  43.8 us (46%)
  starting transfers between devices  27.7 us (29%)
  Pallas kernels  17.6 us (19%)
  local copies, waits for them, and re-layouts  2.45 us (3%)
  other arithmetic  2.1 us (2%)
    ppermute x14, waiting for transfers between devices, fast(): values[name] = lax.ppermute(operand, ('dp', 'ctx'), perm)  35.2 us
    ppermute x14, starting transfers between devices, fast(): values[name] = lax.ppermute(operand, ('dp', 'ctx'), perm)  22 us
    pallas_call x1, Pallas kernels, fast(): pl.pallas_call(functools.partial(late_kernel, rows, cols, ctx, late, firs...  8.77 us
    ppermute x4, waiting for transfers between devices, fast(): moved[k] = lax.ppermute(pieces[k], ('dp', 'ctx'), perm)  8.54 us
    ppermute x4, starting transfers between devices, fast(): moved[k] = lax.ppermute(pieces[k], ('dp', 'ctx'), perm)  5.63 us
    pallas_call x1, Pallas kernels, fast(): pl.pallas_call(early_kernel, out_shape=jax.ShapeDtypeStruct((length, 3 *...  4.54 us
    pallas_call x1, Pallas kernels, fast(): pl.pallas_call(functools.partial(norm_kernel, rows, shard_order), out_sha...  3.26 us
    dynamic_slice x2, local copies, waits for them, and re-layouts, columns(): lax.dynamic_slice_in_dim(w, heads * cols, cols, 1)  2.43 us
  transfers between devices with their start and end apart: 18, of which 10 were waited for; matrix products, arithmetic and copies ran while one was open for 2% of the time, Pallas kernels for 8%

profile of v7, /device:TPU:0, one launch (start us, length us, event | category | flops | bytes accessed | tf_op | source)
XLA Modules:
  0.0 93.8 jit_solution(12388996601168905654)
XLA Ops:
  0.0 1.1 %constant_dynamic-slice_fusion.2 = (bf16[256,512]{1,0:T(8,128)(2,1)S(1)}, bf16[256,512]{1,0:T(8,128)(2,1)S(1)}) fusion(bf16[256,2048]{1,0:T(8,128)(2,1)} %param.7, s32[]{:T(128)S(6)} %select_n.24, s32[]{:T(128)S(6)} %select_n.23), kind=kLoop, calls=%fused_computation.10 | loop fusion | bytes 1048584 | tf_op jit(solution)/shard_map/dynamic_slice | solution.py:260
  1.1 0.0 copy-start
  1.1 1.4 %constant_dynamic-slice_fusion = (bf16[256,512]{1,0:T(8,128)(2,1)S(1)}, bf16[256,512]{1,0:T(8,128)(2,1)S(1)}, bf16[256,512]{1,0:T(8,128)(2,1)S(1)}, bf16[256,512]{1,0:T(8,128)(2,1)S(1)}) fusion(bf16[256,2048]{1,0:T(8,128)(2,1)} %param.9, s32[]{:T(128)S(6)} %select_n.24, s32[]{:T(128)S(6)} %select_n.23, bf16[256,2048]{1,0:T(8,128)(2,1)} %param.8), kind=kLoop, calls=%fused_computation.8 | loop fusion | bytes 2097160 | tf_op jit(solution)/shard_map/dynamic_slice | solution.py:260
  2.5 0.1 pad_maximum_fusion
  2.5 0.5 collective-permute-start
  3.0 1.3 %collective-permute-start.2 = (bf16[224,2048]{1,0:T(8,128)(2,1)S(1)}, bf16[224,2048]{1,0:T(8,128)(2,1)S(1)}, u32[]{:S(2)}, u32[]{:S(2)}) collective-permute-start(bf16[224,2048]{1,0:T(8,128)(2,1)S(1)} %bitcast.1), channel_id=1, source_target_pairs={{2,0},{3,1},{4,6},{5,7},{10,8},{11,9},{12,14},{13,15},{18,16},{19,... | collective-permute-start | bytes 2752520 | tf_op jit(solution)/shard_map/t2/ppermute | solution.py:282
  4.3 0.1 pad_maximum_fusion.1.refs_8_
  4.4 2.6 %collective-permute-start.4 = (bf16[256,1536]{1,0:T(8,128)(2,1)S(1)}, bf16[256,1536]{1,0:T(8,128)(2,1)S(1)}, u32[]{:S(2)}, u32[]{:S(2)}) collective-permute-start(bf16[256,1536]{1,0:T(8,128)(2,1)S(1)} %pad_maximum_fusion.1.refs_8_), channel_id=1, source_target_pairs={{0,8},{1,9},{2,10},{3,11},{4,12},{5,13},{6,14},{7,15},{8,0},{9,1},... | collective-permute-start | bytes 2359304 | tf_op jit(solution)/shard_map/w2/ppermute | solution.py:282
  7.0 0.0 collective-permute-done.refs_9_
  7.0 1.5 %collective-permute-start.3 = (bf16[256,1536]{1,0:T(8,128)(2,1)S(1)}, bf16[256,1536]{1,0:T(8,128)(2,1)S(1)}, u32[]{:S(2)}, u32[]{:S(2)}) collective-permute-start(bf16[256,1536]{1,0:T(8,128)(2,1)S(1)} %collective-permute-done.refs_9_), channel_id=1, source_target_pairs={{0,16},{1,17},{2,18},{3,19},{4,20},{5,21},{6,22},{7,23},{8,24},{9,... | collective-permute-start | bytes 2359304 | tf_op jit(solution)/shard_map/w5/ppermute | solution.py:282
  8.5 0.0 copy-start.1
  8.5 1.7 %fusion = (f32[896,64]{1,0:T(8,128)S(1)}, f32[896,64]{1,0:T(8,128)S(1)}, f32[896,64]{1,0:T(8,128)S(1)}) fusion(f32[64]{0:T(128)S(1)} %multiply_power_fusion, f32[896]{0:T(1024)S(1)} %iota_convert_fusion), kind=kLoop, calls=%fused_computation.6 | loop fusion | flops 114688 | bytes 691968 | tf_op jit(solution)/shard_map/neg | solution.py:41
  10.2 0.3 pad_maximum_fusion.2
  10.5 3.5 %collective-permute-start.5 = (bf16[224,2048]{1,0:T(8,128)(2,1)S(1)}, bf16[224,2048]{1,0:T(8,128)(2,1)S(1)}, u32[]{:S(2)}, u32[]{:S(2)}) collective-permute-start(bf16[224,2048]{1,0:T(8,128)(2,1)S(1)} %bitcast.2), channel_id=1, source_target_pairs={{0,1},{1,0},{6,7},{7,6},{8,9},{9,8},{14,15},{15,14},{16,17},{17,16... | collective-permute-start | bytes 2752520 | tf_op jit(solution)/shard_map/t1/ppermute | solution.py:282
  14.0 2.1 %collective-permute-start.6 = (bf16[224,2048]{1,0:T(8,128)(2,1)S(1)}, bf16[224,2048]{1,0:T(8,128)(2,1)S(1)}, u32[]{:S(2)}, u32[]{:S(2)}) collective-permute-start(bf16[224,2048]{1,0:T(8,128)(2,1)S(1)} %bitcast.3), channel_id=1, source_target_pairs={{0,4},{1,5},{6,2},{7,3},{8,12},{9,13},{14,10},{15,11},{16,20},{17,... | collective-permute-start | bytes 2752520 | tf_op jit(solution)/shard_map/u0/ppermute | solution.py:282
  16.1 6.2 %collective-permute-done.4.refs_10_ = bf16[256,1536]{1,0:T(8,128)(2,1)S(1)} collective-permute-done((bf16[256,1536]{1,0:T(8,128)(2,1)S(1)}, bf16[256,1536]{1,0:T(8,128)(2,1)S(1)}, u32[]{:S(2)}, u32[]{:S(2)}) %collective-permute-start.4) | collective-permute-done | bytes 786464 | tf_op jit(solution)/shard_map/w2/ppermute | solution.py:282
  22.4 2.8 %collective-permute-done.3.refs_11_ = bf16[256,1536]{1,0:T(8,128)(2,1)S(1)} collective-permute-done((bf16[256,1536]{1,0:T(8,128)(2,1)S(1)}, bf16[256,1536]{1,0:T(8,128)(2,1)S(1)}, u32[]{:S(2)}, u32[]{:S(2)}) %collective-permute-start.3) | collective-permute-done | bytes 786464 | tf_op jit(solution)/shard_map/w5/ppermute | solution.py:282
  25.1 4.1 %collective-permute-done.2.refs_2_ = bf16[224,2048]{1,0:T(8,128)(2,1)S(1)} collective-permute-done((bf16[224,2048]{1,0:T(8,128)(2,1)S(1)}, bf16[224,2048]{1,0:T(8,128)(2,1)S(1)}, u32[]{:S(2)}, u32[]{:S(2)}) %collective-permute-start.2) | collective-permute-done | bytes 917536 | tf_op jit(solution)/shard_map/t2/ppermute | solution.py:282
  29.2 1.9 %collective-permute-start.10 = (bf16[224,2048]{1,0:T(8,128)(2,1)S(1)}, bf16[224,2048]{1,0:T(8,128)(2,1)S(1)}, u32[]{:S(2)}, u32[]{:S(2)}) collective-permute-start(bf16[224,2048]{1,0:T(8,128)(2,1)S(1)} %collective-permute-done.2.refs_2_), channel_id=1, source_target_pairs={{0,1},{1,0},{6,7},{7,6},{8,9},{9,8},{14,15},{15,14},{16,17},{17,16... | collective-permute-start | bytes 2752520 | tf_op jit(solution)/shard_map/t3/ppermute | solution.py:282
  31.1 1.3 %collective-permute-start.8 = (bf16[224,2048]{1,0:T(8,128)(2,1)S(1)}, bf16[224,2048]{1,0:T(8,128)(2,1)S(1)}, u32[]{:S(2)}, u32[]{:S(2)}) collective-permute-start(bf16[224,2048]{1,0:T(8,128)(2,1)S(1)} %collective-permute-done.2.refs_2_), channel_id=1, source_target_pairs={{0,4},{1,5},{6,2},{7,3},{8,12},{9,13},{14,10},{15,11},{16,20},{17,... | collective-permute-start | bytes 2752520 | tf_op jit(solution)/shard_map/u2/ppermute | solution.py:282
  32.5 1.1 %collective-permute-done.5.refs_1_ = bf16[224,2048]{1,0:T(8,128)(2,1)S(1)} collective-permute-done((bf16[224,2048]{1,0:T(8,128)(2,1)S(1)}, bf16[224,2048]{1,0:T(8,128)(2,1)S(1)}, u32[]{:S(2)}, u32[]{:S(2)}) %collective-permute-start.5) | collective-permute-done | bytes 917536 | tf_op jit(solution)/shard_map/t1/ppermute | solution.py:282
  33.6 0.0 collective-permute-done.6.refs_4_
  33.6 1.3 %collective-permute-start.7 = (bf16[224,2048]{1,0:T(8,128)(2,1)S(1)}, bf16[224,2048]{1,0:T(8,128)(2,1)S(1)}, u32[]{:S(2)}, u32[]{:S(2)}) collective-permute-start(bf16[224,2048]{1,0:T(8,128)(2,1)S(1)} %collective-permute-done.5.refs_1_), channel_id=1, source_target_pairs={{0,4},{1,5},{6,2},{7,3},{8,12},{9,13},{14,10},{15,11},{16,20},{17,... | collective-permute-start | bytes 2752520 | tf_op jit(solution)/shard_map/u1/ppermute | solution.py:282
  34.9 9.6 %collective-permute-done.10.refs_3_ = bf16[224,2048]{1,0:T(8,128)(2,1)S(1)} collective-permute-done((bf16[224,2048]{1,0:T(8,128)(2,1)S(1)}, bf16[224,2048]{1,0:T(8,128)(2,1)S(1)}, u32[]{:S(2)}, u32[]{:S(2)}) %collective-permute-start.10) | collective-permute-done | bytes 917536 | tf_op jit(solution)/shard_map/t3/ppermute | solution.py:282
  44.5 1.3 %collective-permute-start.11 = (bf16[224,2048]{1,0:T(8,128)(2,1)S(1)}, bf16[224,2048]{1,0:T(8,128)(2,1)S(1)}, u32[]{:S(2)}, u32[]{:S(2)}) collective-permute-start(bf16[224,2048]{1,0:T(8,128)(2,1)S(1)} %collective-permute-done.10.refs_3_), channel_id=1, source_target_pairs={{0,4},{1,5},{6,2},{7,3},{8,12},{9,13},{14,10},{15,11},{16,20},{17,... | collective-permute-start | bytes 2752520 | tf_op jit(solution)/shard_map/u3/ppermute | solution.py:282
  45.9 2.5 %collective-permute-start.12 = (bf16[256,1536]{1,0:T(8,128)(2,1)S(1)}, bf16[256,1536]{1,0:T(8,128)(2,1)S(1)}, u32[]{:S(2)}, u32[]{:S(2)}) collective-permute-start(bf16[256,1536]{1,0:T(8,128)(2,1)S(1)} %collective-permute-done.4.refs_10_), channel_id=1, source_target_pairs={{0,16},{1,17},{2,18},{3,19},{4,20},{5,21},{6,22},{7,23},{8,24},{9,... | collective-permute-start | bytes 2359304 | tf_op jit(solution)/shard_map/w6/ppermute | solution.py:282
  48.4 1.5 %collective-permute-start.13 = (bf16[256,1536]{1,0:T(8,128)(2,1)S(1)}, bf16[256,1536]{1,0:T(8,128)(2,1)S(1)}, u32[]{:S(2)}, u32[]{:S(2)}) collective-permute-start(bf16[256,1536]{1,0:T(8,128)(2,1)S(1)} %collective-permute-done.3.refs_11_), channel_id=1, source_target_pairs={{0,8},{1,9},{2,10},{3,11},{4,12},{5,13},{6,14},{7,15},{8,0},{9,1},... | collective-permute-start | bytes 2359304 | tf_op jit(solution)/shard_map/w7/ppermute | solution.py:282
  49.9 0.0 collective-permute-done.8.refs_6_
  49.9 0.5 collective-permute-start.1
  50.4 0.0 collective-permute-done.7.refs_5_
  50.4 0.1 collective-permute-start.9
  50.5 0.0 collective-permute-done.11.refs_7_
  50.5 3.3 %normalize.1 = (bf16[896,2048]{1,0:T(8,128)(2,1)S(1)}, bf16[1024,1536]{1,0:T(8,128)(2,1)S(1)}) custom-call(bf16[224,2048]{1,0:T(8,128)(2,1)S(1)} %bitcast.4, bf16[224,2048]{1,0:T(8,128)(2,1)S(1)} %collective-permute-done.5.refs_1_, bf16[224,2048]{1,0:T(8,128)(2,1)S(1)} %collective-permute-done.2.refs_2_, ...), custom_call_target="tpu_custom_call" | custom-call | flops 4000000000 | bytes 1000000 | tf_op jit(solution)/shard_map/normalize/pallas_call | solution.py:295
  53.8 6.3 %collective-permute-done.12.refs_2_ = bf16[256,1536]{1,0:T(8,128)(2,1)S(1)} collective-permute-done((bf16[256,1536]{1,0:T(8,128)(2,1)S(1)}, bf16[256,1536]{1,0:T(8,128)(2,1)S(1)}, u32[]{:S(2)}, u32[]{:S(2)}) %collective-permute-start.12) | collective-permute-done | bytes 786464 | tf_op jit(solution)/shard_map/w6/ppermute | solution.py:282
  60.1 1.2 %collective-permute-done.13.refs_3_ = bf16[256,1536]{1,0:T(8,128)(2,1)S(1)} collective-permute-done((bf16[256,1536]{1,0:T(8,128)(2,1)S(1)}, bf16[256,1536]{1,0:T(8,128)(2,1)S(1)}, u32[]{:S(2)}, u32[]{:S(2)}) %collective-permute-start.13) | collective-permute-done | bytes 786464 | tf_op jit(solution)/shard_map/w7/ppermute | solution.py:282
  61.3 4.5 %project_early.1.refs_2_ = f32[896,1536]{1,0:T(8,128)S(1)} custom-call(bf16[896,2048]{1,0:T(8,128)(2,1)S(1)} %get-tuple-element.33.refs_0_.refs_3_, bf16[1024,1536]{1,0:T(8,128)(2,1)S(1)} %get-tuple-element.34.refs_1_, bf16[256,1536]{1,0:T(8,128)(2,1)S(1)} %collective-permute-done.12.refs_2_, bf16[256,1536]{1,0:T(8,128)(2,1)S(1)} %collective-permute-done.13.refs_3_), custom_call_target="tpu_custom_call" | custom-call | flops 4000000000 | bytes 1000000 | tf_op jit(solution)/shard_map/project_early/pallas_call | solution.py:314
  65.9 3.9 %collective-permute-done.1.refs_0_ = bf16[256,1536]{1,0:T(8,128)(2,1)S(1)} collective-permute-done((bf16[256,1536]{1,0:T(8,128)(2,1)S(1)}, bf16[256,1536]{1,0:T(8,128)(2,1)S(1)}, u32[]{:S(2)}, u32[]{:S(2)}) %collective-permute-start.1) | collective-permute-done | bytes 786464 | tf_op jit(solution)/shard_map/w3/ppermute | solution.py:282
  69.8 0.0 collective-permute-done.9.refs_1_
  69.8 8.8 %attend_0.1 = (bf16[224,512]{1,0:T(8,128)(2,1)S(1)}, bf16[224,512]{1,0:T(8,128)(2,1)S(1)}, bf16[224,512]{1,0:T(8,128)(2,1)S(1)}, bf16[224,512]{1,0:T(8,128)(2,1)S(1)}) custom-call(bf16[256,1536]{1,0:T(8,128)(2,1)S(1)} %collective-permute-done.1.refs_0_, bf16[256,1536]{1,0:T(8,128)(2,1)S(1)} %collective-permute-done.9.refs_1_, ...), custom_call_target="tpu_custom_call" | custom-call | flops 1000000 | bytes 1000000 | tf_op jit(solution)/shard_map/attend_0/pallas_call | solution.py:342
  78.5 3.0 %collective-permute-start.14 = (bf16[224,512]{1,0:T(8,128)(2,1)S(1)}, bf16[224,512]{1,0:T(8,128)(2,1)S(1)}, u32[]{:S(2)}, u32[]{:S(2)}) collective-permute-start(bf16[224,512]{1,0:T(8,128)(2,1)S(1)} %get-tuple-element.40), channel_id=1, source_target_pairs={{0,1},{1,0},{2,5},{3,4},{4,3},{5,2},{6,7},{7,6},{8,9},{9,8},{10,13... | collective-permute-start | bytes 688136 | tf_op jit(solution)/shard_map/back_0_1/ppermute | solution.py:378
  81.5 0.7 collective-permute-start.15
  82.2 0.1 collective-permute-start.16
  82.3 1.9 %collective-permute-start.17 = (bf16[224,512]{1,0:T(8,128)(2,1)S(1)}, bf16[224,512]{1,0:T(8,128)(2,1)S(1)}, u32[]{:S(2)}, u32[]{:S(2)}) collective-permute-start(bf16[224,512]{1,0:T(8,128)(2,1)S(1)} %get-tuple-element.42), channel_id=1, source_target_pairs={{0,2},{1,3},{2,6},{3,7},{4,0},{5,1},{6,4},{7,5},{8,10},{9,11},{10,... | collective-permute-start | bytes 688136 | tf_op jit(solution)/shard_map/back_0_2/ppermute | solution.py:378
  84.2 3.1 %collective-permute-done.14.refs_1_ = bf16[224,512]{1,0:T(8,128)(2,1)S(1)} collective-permute-done((bf16[224,512]{1,0:T(8,128)(2,1)S(1)}, bf16[224,512]{1,0:T(8,128)(2,1)S(1)}, u32[]{:S(2)}, u32[]{:S(2)}) %collective-permute-start.14) | collective-permute-done | bytes 229408 | tf_op jit(solution)/shard_map/back_0_1/ppermute | solution.py:378
  87.3 0.0 collective-permute-done.15.refs_2_
  87.3 5.4 %collective-permute-done.16.refs_3_ = bf16[224,512]{1,0:T(8,128)(2,1)S(1)} collective-permute-done((bf16[224,512]{1,0:T(8,128)(2,1)S(1)}, bf16[224,512]{1,0:T(8,128)(2,1)S(1)}, u32[]{:S(2)}, u32[]{:S(2)}) %collective-permute-start.16) | collective-permute-done | bytes 229408 | tf_op jit(solution)/shard_map/back_0_3/ppermute | solution.py:378
  92.7 0.0 collective-permute-done.17.refs_4_
  92.7 1.0 %join.1 = bf16[1,224,2048]{2,1,0:T(8,128)(2,1)} custom-call(bf16[224,512]{1,0:T(8,128)(2,1)S(1)} %get-tuple-element.39.refs_0_, bf16[224,512]{1,0:T(8,128)(2,1)S(1)} %collective-permute-done.14.refs_1_, bf16[224,512]{1,0:T(8,128)(2,1)S(1)} %collective-permute-done.15.refs_2_, bf16[224,512]{1,0:T(8,128)(2,1)S(1)} %collective-permute-done.16.refs_3_, ...), custom_call_target="tpu_custom_call" | custom-call | tf_op jit(solution)/shard_map/join/pallas_call | solution.py:380
  (5 shorter events, 0.0 us)
Async XLA Ops:
  1.1 2.0 %copy-start = (bf16[1,224,2048]{2,1,0:T(8,128)(2,1)S(1)}, bf16[1,224,2048]{2,1,0:T(8,128)(2,1)}, u32[]{:S(2)}) copy-start(bf16[1,224,2048]{2,1,0:T(8,128)(2,1)} %param.5) | copy-start | bytes 2752516
  2.5 4.5 %collective-permute-start = (bf16[256,1536]{1,0:T(8,128)(2,1)S(1)}, bf16[256,1536]{1,0:T(8,128)(2,1)S(1)}, u32[]{:S(2)}, u32[]{:S(2)}) collective-permute-start(bf16[256,1536]{1,0:T(8,128)(2,1)S(1)} %pad_maximum_fusion), channel_id=1, source_target_pairs={{0,4},{1,5},{2,6},{3,7},{4,0},{5,1},{6,2},{7,3},{8,12},{9,13},{10,... | collective-permute-start | bytes 2359304 | tf_op jit(solution)/shard_map/w1/ppermute | solution.py:282
  3.0 26.2 %collective-permute-start.2 = (bf16[224,2048]{1,0:T(8,128)(2,1)S(1)}, bf16[224,2048]{1,0:T(8,128)(2,1)S(1)}, u32[]{:S(2)}, u32[]{:S(2)}) collective-permute-start(bf16[224,2048]{1,0:T(8,128)(2,1)S(1)} %bitcast.1), channel_id=1, source_target_pairs={{2,0},{3,1},{4,6},{5,7},{10,8},{11,9},{12,14},{13,15},{18,16},{19,... | collective-permute-start | bytes 2752520 | tf_op jit(solution)/shard_map/t2/ppermute | solution.py:282
  4.4 18.0 %collective-permute-start.4 = (bf16[256,1536]{1,0:T(8,128)(2,1)S(1)}, bf16[256,1536]{1,0:T(8,128)(2,1)S(1)}, u32[]{:S(2)}, u32[]{:S(2)}) collective-permute-start(bf16[256,1536]{1,0:T(8,128)(2,1)S(1)} %pad_maximum_fusion.1.refs_8_), channel_id=1, source_target_pairs={{0,8},{1,9},{2,10},{3,11},{4,12},{5,13},{6,14},{7,15},{8,0},{9,1},... | collective-permute-start | bytes 2359304 | tf_op jit(solution)/shard_map/w2/ppermute | solution.py:282
  7.0 18.1 %collective-permute-start.3 = (bf16[256,1536]{1,0:T(8,128)(2,1)S(1)}, bf16[256,1536]{1,0:T(8,128)(2,1)S(1)}, u32[]{:S(2)}, u32[]{:S(2)}) collective-permute-start(bf16[256,1536]{1,0:T(8,128)(2,1)S(1)} %collective-permute-done.refs_9_), channel_id=1, source_target_pairs={{0,16},{1,17},{2,18},{3,19},{4,20},{5,21},{6,22},{7,23},{8,24},{9,... | collective-permute-start | bytes 2359304 | tf_op jit(solution)/shard_map/w5/ppermute | solution.py:282
  8.5 42.0 %copy-start.1 = (bf16[2048]{0:T(1024)(128)(2,1)S(1)}, bf16[2048]{0:T(1024)(128)(2,1)}, u32[]{:S(2)}) copy-start(bf16[2048]{0:T(1024)(128)(2,1)} %param.6) | copy-start | bytes 12292
  10.5 23.1 %collective-permute-start.5 = (bf16[224,2048]{1,0:T(8,128)(2,1)S(1)}, bf16[224,2048]{1,0:T(8,128)(2,1)S(1)}, u32[]{:S(2)}, u32[]{:S(2)}) collective-permute-start(bf16[224,2048]{1,0:T(8,128)(2,1)S(1)} %bitcast.2), channel_id=1, source_target_pairs={{0,1},{1,0},{6,7},{7,6},{8,9},{9,8},{14,15},{15,14},{16,17},{17,16... | collective-permute-start | bytes 2752520 | tf_op jit(solution)/shard_map/t1/ppermute | solution.py:282
  14.0 19.6 %collective-permute-start.6 = (bf16[224,2048]{1,0:T(8,128)(2,1)S(1)}, bf16[224,2048]{1,0:T(8,128)(2,1)S(1)}, u32[]{:S(2)}, u32[]{:S(2)}) collective-permute-start(bf16[224,2048]{1,0:T(8,128)(2,1)S(1)} %bitcast.3), channel_id=1, source_target_pairs={{0,4},{1,5},{6,2},{7,3},{8,12},{9,13},{14,10},{15,11},{16,20},{17,... | collective-permute-start | bytes 2752520 | tf_op jit(solution)/shard_map/u0/ppermute | solution.py:282
  29.2 15.3 %collective-permute-start.10 = (bf16[224,2048]{1,0:T(8,128)(2,1)S(1)}, bf16[224,2048]{1,0:T(8,128)(2,1)S(1)}, u32[]{:S(2)}, u32[]{:S(2)}) collective-permute-start(bf16[224,2048]{1,0:T(8,128)(2,1)S(1)} %collective-permute-done.2.refs_2_), channel_id=1, source_target_pairs={{0,1},{1,0},{6,7},{7,6},{8,9},{9,8},{14,15},{15,14},{16,17},{17,16... | collective-permute-start | bytes 2752520 | tf_op jit(solution)/shard_map/t3/ppermute | solution.py:282
  31.1 18.7 %collective-permute-start.8 = (bf16[224,2048]{1,0:T(8,128)(2,1)S(1)}, bf16[224,2048]{1,0:T(8,128)(2,1)S(1)}, u32[]{:S(2)}, u32[]{:S(2)}) collective-permute-start(bf16[224,2048]{1,0:T(8,128)(2,1)S(1)} %collective-permute-done.2.refs_2_), channel_id=1, source_target_pairs={{0,4},{1,5},{6,2},{7,3},{8,12},{9,13},{14,10},{15,11},{16,20},{17,... | collective-permute-start | bytes 2752520 | tf_op jit(solution)/shard_map/u2/ppermute | solution.py:282
  33.6 16.8 %collective-permute-start.7 = (bf16[224,2048]{1,0:T(8,128)(2,1)S(1)}, bf16[224,2048]{1,0:T(8,128)(2,1)S(1)}, u32[]{:S(2)}, u32[]{:S(2)}) collective-permute-start(bf16[224,2048]{1,0:T(8,128)(2,1)S(1)} %collective-permute-done.5.refs_1_), channel_id=1, source_target_pairs={{0,4},{1,5},{6,2},{7,3},{8,12},{9,13},{14,10},{15,11},{16,20},{17,... | collective-permute-start | bytes 2752520 | tf_op jit(solution)/shard_map/u1/ppermute | solution.py:282
  44.5 6.0 %collective-permute-start.11 = (bf16[224,2048]{1,0:T(8,128)(2,1)S(1)}, bf16[224,2048]{1,0:T(8,128)(2,1)S(1)}, u32[]{:S(2)}, u32[]{:S(2)}) collective-permute-start(bf16[224,2048]{1,0:T(8,128)(2,1)S(1)} %collective-permute-done.10.refs_3_), channel_id=1, source_target_pairs={{0,4},{1,5},{6,2},{7,3},{8,12},{9,13},{14,10},{15,11},{16,20},{17,... | collective-permute-start | bytes 2752520 | tf_op jit(solution)/shard_map/u3/ppermute | solution.py:282
  45.9 14.2 %collective-permute-start.12 = (bf16[256,1536]{1,0:T(8,128)(2,1)S(1)}, bf16[256,1536]{1,0:T(8,128)(2,1)S(1)}, u32[]{:S(2)}, u32[]{:S(2)}) collective-permute-start(bf16[256,1536]{1,0:T(8,128)(2,1)S(1)} %collective-permute-done.4.refs_10_), channel_id=1, source_target_pairs={{0,16},{1,17},{2,18},{3,19},{4,20},{5,21},{6,22},{7,23},{8,24},{9,... | collective-permute-start | bytes 2359304 | tf_op jit(solution)/shard_map/w6/ppermute | solution.py:282
  48.4 13.0 %collective-permute-start.13 = (bf16[256,1536]{1,0:T(8,128)(2,1)S(1)}, bf16[256,1536]{1,0:T(8,128)(2,1)S(1)}, u32[]{:S(2)}, u32[]{:S(2)}) collective-permute-start(bf16[256,1536]{1,0:T(8,128)(2,1)S(1)} %collective-permute-done.3.refs_11_), channel_id=1, source_target_pairs={{0,8},{1,9},{2,10},{3,11},{4,12},{5,13},{6,14},{7,15},{8,0},{9,1},... | collective-permute-start | bytes 2359304 | tf_op jit(solution)/shard_map/w7/ppermute | solution.py:282
  49.9 19.9 %collective-permute-start.1 = (bf16[256,1536]{1,0:T(8,128)(2,1)S(1)}, bf16[256,1536]{1,0:T(8,128)(2,1)S(1)}, u32[]{:S(2)}, u32[]{:S(2)}) collective-permute-start(bf16[256,1536]{1,0:T(8,128)(2,1)S(1)} %collective-permute-done.refs_9_), channel_id=1, source_target_pairs={{0,8},{1,9},{2,10},{3,11},{4,12},{5,13},{6,14},{7,15},{8,0},{9,1},... | collective-permute-start | bytes 2359304 | tf_op jit(solution)/shard_map/w3/ppermute | solution.py:282
  50.4 19.4 %collective-permute-start.9 = (bf16[256,1536]{1,0:T(8,128)(2,1)S(1)}, bf16[256,1536]{1,0:T(8,128)(2,1)S(1)}, u32[]{:S(2)}, u32[]{:S(2)}) collective-permute-start(bf16[256,1536]{1,0:T(8,128)(2,1)S(1)} %pad_maximum_fusion.1.refs_8_), channel_id=1, source_target_pairs={{0,16},{1,17},{2,18},{3,19},{4,20},{5,21},{6,22},{7,23},{8,24},{9,... | collective-permute-start | bytes 2359304 | tf_op jit(solution)/shard_map/w4/ppermute | solution.py:282
  78.5 8.8 %collective-permute-start.14 = (bf16[224,512]{1,0:T(8,128)(2,1)S(1)}, bf16[224,512]{1,0:T(8,128)(2,1)S(1)}, u32[]{:S(2)}, u32[]{:S(2)}) collective-permute-start(bf16[224,512]{1,0:T(8,128)(2,1)S(1)} %get-tuple-element.40), channel_id=1, source_target_pairs={{0,1},{1,0},{2,5},{3,4},{4,3},{5,2},{6,7},{7,6},{8,9},{9,8},{10,13... | collective-permute-start | bytes 688136 | tf_op jit(solution)/shard_map/back_0_1/ppermute | solution.py:378
  81.5 5.8 %collective-permute-start.15 = (bf16[224,512]{1,0:T(8,128)(2,1)S(1)}, bf16[224,512]{1,0:T(8,128)(2,1)S(1)}, u32[]{:S(2)}, u32[]{:S(2)}) collective-permute-start(bf16[224,512]{1,0:T(8,128)(2,1)S(1)} %get-tuple-element.39.refs_0_), channel_id=1, source_target_pairs={{2,4},{3,5},{4,2},{5,3},{10,12},{11,13},{12,10},{13,11},{18,20},{1... | collective-permute-start | bytes 688136 | tf_op jit(solution)/shard_map/back_0_0/ppermute | solution.py:378
  82.2 10.5 %collective-permute-start.16 = (bf16[224,512]{1,0:T(8,128)(2,1)S(1)}, bf16[224,512]{1,0:T(8,128)(2,1)S(1)}, u32[]{:S(2)}, u32[]{:S(2)}) collective-permute-start(bf16[224,512]{1,0:T(8,128)(2,1)S(1)} %get-tuple-element.41), channel_id=1, source_target_pairs={{0,3},{1,2},{2,7},{3,6},{4,1},{5,0},{6,5},{7,4},{8,11},{9,10},{10,... | collective-permute-start | bytes 688136 | tf_op jit(solution)/shard_map/back_0_3/ppermute | solution.py:378
  82.3 10.5 %collective-permute-start.17 = (bf16[224,512]{1,0:T(8,128)(2,1)S(1)}, bf16[224,512]{1,0:T(8,128)(2,1)S(1)}, u32[]{:S(2)}, u32[]{:S(2)}) collective-permute-start(bf16[224,512]{1,0:T(8,128)(2,1)S(1)} %get-tuple-element.42), channel_id=1, source_target_pairs={{0,2},{1,3},{2,6},{3,7},{4,0},{5,1},{6,4},{7,5},{8,10},{9,11},{10,... | collective-permute-start | bytes 688136 | tf_op jit(solution)/shard_map/back_0_2/ppermute | solution.py:378

commit v8 on v6

--- a/solution.py
+++ b/solution.py
@@ -128,25 +128,23 @@
     shards = refs[:count]
     partial, normed, cos_ref, sin_ref = refs[count : count + 4]
     outs = refs[count + 4 : count + 4 + total]
-    weights, qkv, result, weight_sems, out_sems = refs[count + 4 + total :]
+    qkv, result, out_sems = refs[count + 4 + total :]
     me = role(rows)
     width = heads * HEAD_DIM
     start_lane = first_head * HEAD_DIM
-    loads = load_shards(
-        shards, weights, weight_sems, [(j * cols + start_lane, j * width, width) for j in range(3)]
-    )
-    for load in loads:
-        load.wait()
-    tail = normed.shape[1] - weights.shape[0]
+    depth = shards[0].shape[0]
+    tail = normed.shape[1] - count * depth
     step = HEAD_DIM if width % (2 * HEAD_DIM) else 2 * HEAD_DIM
     for j in range(3):
         for lane in range(0, width, step):
             first = j * cols + start_lane + lane
-            linear = partial[:, first : first + step] + jnp.dot(
-                normed[:, tail:],
-                weights[:, j * width + lane : j * width + lane + step],
-                preferred_element_type=jnp.float32,
-            )
+            linear = partial[:, first : first + step]
+            for i, shard in enumerate(shards):
+                linear += jnp.dot(
+                    normed[:, tail + i * depth : tail + (i + 1) * depth],
+                    shard[:, first : first + step],
+                    preferred_element_type=jnp.float32,
+                )
             for i, start in enumerate(me["starts"]):
                 value = linear[i * rows : (i + 1) * rows]
                 if j < 2:
@@ -342,13 +340,11 @@
         pieces = pl.pallas_call(
             functools.partial(late_kernel, rows, cols, ctx, late, first_head, count),
             out_shape=[jax.ShapeDtypeStruct((rows, width), jnp.bfloat16)] * ctx,
-            in_specs=[any_space] * late + [vmem] * 4,
+            in_specs=[vmem] * (late + 4),
             out_specs=[any_space] * ctx,
             scratch_shapes=[
-                pltpu.VMEM((late * depth, 3 * width), jnp.bfloat16),
                 pltpu.VMEM((ctx * rows, 3 * width), jnp.bfloat16),
                 pltpu.VMEM((ctx, rows, width), jnp.bfloat16),
-                pltpu.SemaphoreType.DMA((3 * late,)),
                 pltpu.SemaphoreType.DMA((ctx,)),
             ],
             compiler_params=pltpu.CompilerParams(vmem_limit_bytes=VMEM_LIMIT),

time: 94.1 us -> 94 us (level)
  no operation moved by 1% of the time
where the time goes in v8:
time: 94 us; the launch traced here: 92.9 us
  waiting for transfers between devices  43.8 us (47%)
  starting transfers between devices  27.7 us (29%)
  Pallas kernels  16.7 us (18%)
  local copies, waits for them, and re-layouts  2.45 us (3%)
  other arithmetic  2.1 us (2%)
    ppermute x14, waiting for transfers between devices, fast(): values[name] = lax.ppermute(operand, ('dp', 'ctx'), perm)  35.2 us
    ppermute x14, starting transfers between devices, fast(): values[name] = lax.ppermute(operand, ('dp', 'ctx'), perm)  22 us
    ppermute x4, waiting for transfers between devices, fast(): moved[k] = lax.ppermute(pieces[k], ('dp', 'ctx'), perm)  8.53 us
    pallas_call x1, Pallas kernels, fast(): pl.pallas_call(functools.partial(late_kernel, rows, cols, ctx, late, firs...  7.89 us
    ppermute x4, starting transfers between devices, fast(): moved[k] = lax.ppermute(pieces[k], ('dp', 'ctx'), perm)  5.65 us
    pallas_call x1, Pallas kernels, fast(): pl.pallas_call(early_kernel, out_shape=jax.ShapeDtypeStruct((length, 3 *...  4.54 us
    pallas_call x1, Pallas kernels, fast(): pl.pallas_call(functools.partial(norm_kernel, rows, shard_order), out_sha...  3.26 us
    dynamic_slice x2, local copies, waits for them, and re-layouts, columns(): lax.dynamic_slice_in_dim(w, heads * cols, cols, 1)  2.43 us
  transfers between devices with their start and end apart: 18, of which 10 were waited for; matrix products, arithmetic and copies ran while one was open for 2% of the time, Pallas kernels for 8%

profile of v8, /device:TPU:0, one launch (start us, length us, event | category | flops | bytes accessed | tf_op | source)
XLA Modules:
  0.0 92.9 jit_solution(8511882647320487094)
XLA Ops:
  0.0 1.1 %constant_dynamic-slice_fusion.2 = (bf16[256,512]{1,0:T(8,128)(2,1)S(1)}, bf16[256,512]{1,0:T(8,128)(2,1)S(1)}) fusion(bf16[256,2048]{1,0:T(8,128)(2,1)} %param.7, s32[]{:T(128)S(6)} %select_n.24, s32[]{:T(128)S(6)} %select_n.23), kind=kLoop, calls=%fused_computation.10 | loop fusion | bytes 1048584 | tf_op jit(solution)/shard_map/dynamic_slice | solution.py:258
  1.1 0.0 copy-start
  1.1 1.4 %constant_dynamic-slice_fusion = (bf16[256,512]{1,0:T(8,128)(2,1)S(1)}, bf16[256,512]{1,0:T(8,128)(2,1)S(1)}, bf16[256,512]{1,0:T(8,128)(2,1)S(1)}, bf16[256,512]{1,0:T(8,128)(2,1)S(1)}) fusion(bf16[256,2048]{1,0:T(8,128)(2,1)} %param.9, s32[]{:T(128)S(6)} %select_n.24, s32[]{:T(128)S(6)} %select_n.23, bf16[256,2048]{1,0:T(8,128)(2,1)} %param.8), kind=kLoop, calls=%fused_computation.8 | loop fusion | bytes 2097160 | tf_op jit(solution)/shard_map/dynamic_slice | solution.py:258
  2.5 0.1 pad_maximum_fusion
  2.5 0.5 collective-permute-start
  3.0 1.3 %collective-permute-start.2 = (bf16[224,2048]{1,0:T(8,128)(2,1)S(1)}, bf16[224,2048]{1,0:T(8,128)(2,1)S(1)}, u32[]{:S(2)}, u32[]{:S(2)}) collective-permute-start(bf16[224,2048]{1,0:T(8,128)(2,1)S(1)} %bitcast.1), channel_id=1, source_target_pairs={{2,0},{3,1},{4,6},{5,7},{10,8},{11,9},{12,14},{13,15},{18,16},{19,... | collective-permute-start | bytes 2752520 | tf_op jit(solution)/shard_map/t2/ppermute | solution.py:280
  4.3 0.1 pad_maximum_fusion.1.refs_8_
  4.4 2.6 %collective-permute-start.4 = (bf16[256,1536]{1,0:T(8,128)(2,1)S(1)}, bf16[256,1536]{1,0:T(8,128)(2,1)S(1)}, u32[]{:S(2)}, u32[]{:S(2)}) collective-permute-start(bf16[256,1536]{1,0:T(8,128)(2,1)S(1)} %pad_maximum_fusion.1.refs_8_), channel_id=1, source_target_pairs={{0,8},{1,9},{2,10},{3,11},{4,12},{5,13},{6,14},{7,15},{8,0},{9,1},... | collective-permute-start | bytes 2359304 | tf_op jit(solution)/shard_map/w2/ppermute | solution.py:280
  7.0 0.0 collective-permute-done.refs_9_
  7.0 1.5 %collective-permute-start.3 = (bf16[256,1536]{1,0:T(8,128)(2,1)S(1)}, bf16[256,1536]{1,0:T(8,128)(2,1)S(1)}, u32[]{:S(2)}, u32[]{:S(2)}) collective-permute-start(bf16[256,1536]{1,0:T(8,128)(2,1)S(1)} %collective-permute-done.refs_9_), channel_id=1, source_target_pairs={{0,16},{1,17},{2,18},{3,19},{4,20},{5,21},{6,22},{7,23},{8,24},{9,... | collective-permute-start | bytes 2359304 | tf_op jit(solution)/shard_map/w5/ppermute | solution.py:280
  8.5 0.0 copy-start.1
  8.5 1.7 %fusion = (f32[896,64]{1,0:T(8,128)S(1)}, f32[896,64]{1,0:T(8,128)S(1)}, f32[896,64]{1,0:T(8,128)S(1)}) fusion(f32[64]{0:T(128)S(1)} %multiply_power_fusion, f32[896]{0:T(1024)S(1)} %iota_convert_fusion), kind=kLoop, calls=%fused_computation.6 | loop fusion | flops 114688 | bytes 691968 | tf_op jit(solution)/shard_map/neg | solution.py:41
  10.2 0.3 pad_maximum_fusion.2
  10.5 3.5 %collective-permute-start.5 = (bf16[224,2048]{1,0:T(8,128)(2,1)S(1)}, bf16[224,2048]{1,0:T(8,128)(2,1)S(1)}, u32[]{:S(2)}, u32[]{:S(2)}) collective-permute-start(bf16[224,2048]{1,0:T(8,128)(2,1)S(1)} %bitcast.2), channel_id=1, source_target_pairs={{0,1},{1,0},{6,7},{7,6},{8,9},{9,8},{14,15},{15,14},{16,17},{17,16... | collective-permute-start | bytes 2752520 | tf_op jit(solution)/shard_map/t1/ppermute | solution.py:280
  14.0 2.1 %collective-permute-start.6 = (bf16[224,2048]{1,0:T(8,128)(2,1)S(1)}, bf16[224,2048]{1,0:T(8,128)(2,1)S(1)}, u32[]{:S(2)}, u32[]{:S(2)}) collective-permute-start(bf16[224,2048]{1,0:T(8,128)(2,1)S(1)} %bitcast.3), channel_id=1, source_target_pairs={{0,4},{1,5},{6,2},{7,3},{8,12},{9,13},{14,10},{15,11},{16,20},{17,... | collective-permute-start | bytes 2752520 | tf_op jit(solution)/shard_map/u0/ppermute | solution.py:280
  16.1 6.2 %collective-permute-done.4.refs_10_ = bf16[256,1536]{1,0:T(8,128)(2,1)S(1)} collective-permute-done((bf16[256,1536]{1,0:T(8,128)(2,1)S(1)}, bf16[256,1536]{1,0:T(8,128)(2,1)S(1)}, u32[]{:S(2)}, u32[]{:S(2)}) %collective-permute-start.4) | collective-permute-done | bytes 786464 | tf_op jit(solution)/shard_map/w2/ppermute | solution.py:280
  22.4 2.8 %collective-permute-done.3.refs_11_ = bf16[256,1536]{1,0:T(8,128)(2,1)S(1)} collective-permute-done((bf16[256,1536]{1,0:T(8,128)(2,1)S(1)}, bf16[256,1536]{1,0:T(8,128)(2,1)S(1)}, u32[]{:S(2)}, u32[]{:S(2)}) %collective-permute-start.3) | collective-permute-done | bytes 786464 | tf_op jit(solution)/shard_map/w5/ppermute | solution.py:280
  25.1 4.1 %collective-permute-done.2.refs_2_ = bf16[224,2048]{1,0:T(8,128)(2,1)S(1)} collective-permute-done((bf16[224,2048]{1,0:T(8,128)(2,1)S(1)}, bf16[224,2048]{1,0:T(8,128)(2,1)S(1)}, u32[]{:S(2)}, u32[]{:S(2)}) %collective-permute-start.2) | collective-permute-done | bytes 917536 | tf_op jit(solution)/shard_map/t2/ppermute | solution.py:280
  29.2 1.9 %collective-permute-start.10 = (bf16[224,2048]{1,0:T(8,128)(2,1)S(1)}, bf16[224,2048]{1,0:T(8,128)(2,1)S(1)}, u32[]{:S(2)}, u32[]{:S(2)}) collective-permute-start(bf16[224,2048]{1,0:T(8,128)(2,1)S(1)} %collective-permute-done.2.refs_2_), channel_id=1, source_target_pairs={{0,1},{1,0},{6,7},{7,6},{8,9},{9,8},{14,15},{15,14},{16,17},{17,16... | collective-permute-start | bytes 2752520 | tf_op jit(solution)/shard_map/t3/ppermute | solution.py:280
  31.1 1.3 %collective-permute-start.8 = (bf16[224,2048]{1,0:T(8,128)(2,1)S(1)}, bf16[224,2048]{1,0:T(8,128)(2,1)S(1)}, u32[]{:S(2)}, u32[]{:S(2)}) collective-permute-start(bf16[224,2048]{1,0:T(8,128)(2,1)S(1)} %collective-permute-done.2.refs_2_), channel_id=1, source_target_pairs={{0,4},{1,5},{6,2},{7,3},{8,12},{9,13},{14,10},{15,11},{16,20},{17,... | collective-permute-start | bytes 2752520 | tf_op jit(solution)/shard_map/u2/ppermute | solution.py:280
  32.5 1.1 %collective-permute-done.5.refs_1_ = bf16[224,2048]{1,0:T(8,128)(2,1)S(1)} collective-permute-done((bf16[224,2048]{1,0:T(8,128)(2,1)S(1)}, bf16[224,2048]{1,0:T(8,128)(2,1)S(1)}, u32[]{:S(2)}, u32[]{:S(2)}) %collective-permute-start.5) | collective-permute-done | bytes 917536 | tf_op jit(solution)/shard_map/t1/ppermute | solution.py:280
  33.6 0.0 collective-permute-done.6.refs_4_
  33.6 1.3 %collective-permute-start.7 = (bf16[224,2048]{1,0:T(8,128)(2,1)S(1)}, bf16[224,2048]{1,0:T(8,128)(2,1)S(1)}, u32[]{:S(2)}, u32[]{:S(2)}) collective-permute-start(bf16[224,2048]{1,0:T(8,128)(2,1)S(1)} %collective-permute-done.5.refs_1_), channel_id=1, source_target_pairs={{0,4},{1,5},{6,2},{7,3},{8,12},{9,13},{14,10},{15,11},{16,20},{17,... | collective-permute-start | bytes 2752520 | tf_op jit(solution)/shard_map/u1/ppermute | solution.py:280
  34.9 9.6 %collective-permute-done.10.refs_3_ = bf16[224,2048]{1,0:T(8,128)(2,1)S(1)} collective-permute-done((bf16[224,2048]{1,0:T(8,128)(2,1)S(1)}, bf16[224,2048]{1,0:T(8,128)(2,1)S(1)}, u32[]{:S(2)}, u32[]{:S(2)}) %collective-permute-start.10) | collective-permute-done | bytes 917536 | tf_op jit(solution)/shard_map/t3/ppermute | solution.py:280
  44.5 1.3 %collective-permute-start.11 = (bf16[224,2048]{1,0:T(8,128)(2,1)S(1)}, bf16[224,2048]{1,0:T(8,128)(2,1)S(1)}, u32[]{:S(2)}, u32[]{:S(2)}) collective-permute-start(bf16[224,2048]{1,0:T(8,128)(2,1)S(1)} %collective-permute-done.10.refs_3_), channel_id=1, source_target_pairs={{0,4},{1,5},{6,2},{7,3},{8,12},{9,13},{14,10},{15,11},{16,20},{17,... | collective-permute-start | bytes 2752520 | tf_op jit(solution)/shard_map/u3/ppermute | solution.py:280
  45.9 2.5 %collective-permute-start.12 = (bf16[256,1536]{1,0:T(8,128)(2,1)S(1)}, bf16[256,1536]{1,0:T(8,128)(2,1)S(1)}, u32[]{:S(2)}, u32[]{:S(2)}) collective-permute-start(bf16[256,1536]{1,0:T(8,128)(2,1)S(1)} %collective-permute-done.4.refs_10_), channel_id=1, source_target_pairs={{0,16},{1,17},{2,18},{3,19},{4,20},{5,21},{6,22},{7,23},{8,24},{9,... | collective-permute-start | bytes 2359304 | tf_op jit(solution)/shard_map/w6/ppermute | solution.py:280
  48.4 1.5 %collective-permute-start.13 = (bf16[256,1536]{1,0:T(8,128)(2,1)S(1)}, bf16[256,1536]{1,0:T(8,128)(2,1)S(1)}, u32[]{:S(2)}, u32[]{:S(2)}) collective-permute-start(bf16[256,1536]{1,0:T(8,128)(2,1)S(1)} %collective-permute-done.3.refs_11_), channel_id=1, source_target_pairs={{0,8},{1,9},{2,10},{3,11},{4,12},{5,13},{6,14},{7,15},{8,0},{9,1},... | collective-permute-start | bytes 2359304 | tf_op jit(solution)/shard_map/w7/ppermute | solution.py:280
  49.9 0.0 collective-permute-done.8.refs_6_
  49.9 0.5 collective-permute-start.1
  50.4 0.0 collective-permute-done.7.refs_5_
  50.4 0.1 collective-permute-start.9
  50.5 0.0 collective-permute-done.11.refs_7_
  50.5 3.3 %normalize.1 = (bf16[896,2048]{1,0:T(8,128)(2,1)S(1)}, bf16[1024,1536]{1,0:T(8,128)(2,1)S(1)}) custom-call(bf16[224,2048]{1,0:T(8,128)(2,1)S(1)} %bitcast.4, bf16[224,2048]{1,0:T(8,128)(2,1)S(1)} %collective-permute-done.5.refs_1_, bf16[224,2048]{1,0:T(8,128)(2,1)S(1)} %collective-permute-done.2.refs_2_, ...), custom_call_target="tpu_custom_call" | custom-call | flops 4000000000 | bytes 1000000 | tf_op jit(solution)/shard_map/normalize/pallas_call | solution.py:293
  53.8 6.3 %collective-permute-done.12.refs_2_ = bf16[256,1536]{1,0:T(8,128)(2,1)S(1)} collective-permute-done((bf16[256,1536]{1,0:T(8,128)(2,1)S(1)}, bf16[256,1536]{1,0:T(8,128)(2,1)S(1)}, u32[]{:S(2)}, u32[]{:S(2)}) %collective-permute-start.12) | collective-permute-done | bytes 786464 | tf_op jit(solution)/shard_map/w6/ppermute | solution.py:280
  60.1 1.2 %collective-permute-done.13.refs_3_ = bf16[256,1536]{1,0:T(8,128)(2,1)S(1)} collective-permute-done((bf16[256,1536]{1,0:T(8,128)(2,1)S(1)}, bf16[256,1536]{1,0:T(8,128)(2,1)S(1)}, u32[]{:S(2)}, u32[]{:S(2)}) %collective-permute-start.13) | collective-permute-done | bytes 786464 | tf_op jit(solution)/shard_map/w7/ppermute | solution.py:280
  61.3 4.5 %project_early.1.refs_2_ = f32[896,1536]{1,0:T(8,128)S(1)} custom-call(bf16[896,2048]{1,0:T(8,128)(2,1)S(1)} %get-tuple-element.33.refs_0_.refs_3_, bf16[1024,1536]{1,0:T(8,128)(2,1)S(1)} %get-tuple-element.34.refs_1_, bf16[256,1536]{1,0:T(8,128)(2,1)S(1)} %collective-permute-done.12.refs_2_, bf16[256,1536]{1,0:T(8,128)(2,1)S(1)} %collective-permute-done.13.refs_3_), custom_call_target="tpu_custom_call" | custom-call | flops 4000000000 | bytes 1000000 | tf_op jit(solution)/shard_map/project_early/pallas_call | solution.py:312
  65.9 3.9 %collective-permute-done.1.refs_0_ = bf16[256,1536]{1,0:T(8,128)(2,1)S(1)} collective-permute-done((bf16[256,1536]{1,0:T(8,128)(2,1)S(1)}, bf16[256,1536]{1,0:T(8,128)(2,1)S(1)}, u32[]{:S(2)}, u32[]{:S(2)}) %collective-permute-start.1) | collective-permute-done | bytes 786464 | tf_op jit(solution)/shard_map/w3/ppermute | solution.py:280
  69.8 0.0 collective-permute-done.9.refs_1_
  69.8 7.9 %attend_0.1 = (bf16[224,512]{1,0:T(8,128)(2,1)S(1)}, bf16[224,512]{1,0:T(8,128)(2,1)S(1)}, bf16[224,512]{1,0:T(8,128)(2,1)S(1)}, bf16[224,512]{1,0:T(8,128)(2,1)S(1)}) custom-call(bf16[256,1536]{1,0:T(8,128)(2,1)S(1)} %collective-permute-done.1.refs_0_, bf16[256,1536]{1,0:T(8,128)(2,1)S(1)} %collective-permute-done.9.refs_1_, ...), custom_call_target="tpu_custom_call" | custom-call | flops 1000000 | bytes 1000000 | tf_op jit(solution)/shard_map/attend_0/pallas_call | solution.py:340
  77.7 3.0 %collective-permute-start.14 = (bf16[224,512]{1,0:T(8,128)(2,1)S(1)}, bf16[224,512]{1,0:T(8,128)(2,1)S(1)}, u32[]{:S(2)}, u32[]{:S(2)}) collective-permute-start(bf16[224,512]{1,0:T(8,128)(2,1)S(1)} %get-tuple-element.40), channel_id=1, source_target_pairs={{0,1},{1,0},{2,5},{3,4},{4,3},{5,2},{6,7},{7,6},{8,9},{9,8},{10,13... | collective-permute-start | bytes 688136 | tf_op jit(solution)/shard_map/back_0_1/ppermute | solution.py:374
  80.6 0.7 collective-permute-start.15
  81.3 0.1 collective-permute-start.16
  81.4 1.9 %collective-permute-start.17 = (bf16[224,512]{1,0:T(8,128)(2,1)S(1)}, bf16[224,512]{1,0:T(8,128)(2,1)S(1)}, u32[]{:S(2)}, u32[]{:S(2)}) collective-permute-start(bf16[224,512]{1,0:T(8,128)(2,1)S(1)} %get-tuple-element.42), channel_id=1, source_target_pairs={{0,2},{1,3},{2,6},{3,7},{4,0},{5,1},{6,4},{7,5},{8,10},{9,11},{10,... | collective-permute-start | bytes 688136 | tf_op jit(solution)/shard_map/back_0_2/ppermute | solution.py:374
  83.3 3.1 %collective-permute-done.14.refs_1_ = bf16[224,512]{1,0:T(8,128)(2,1)S(1)} collective-permute-done((bf16[224,512]{1,0:T(8,128)(2,1)S(1)}, bf16[224,512]{1,0:T(8,128)(2,1)S(1)}, u32[]{:S(2)}, u32[]{:S(2)}) %collective-permute-start.14) | collective-permute-done | bytes 229408 | tf_op jit(solution)/shard_map/back_0_1/ppermute | solution.py:374
  86.5 0.0 collective-permute-done.15.refs_2_
  86.5 5.4 %collective-permute-done.16.refs_3_ = bf16[224,512]{1,0:T(8,128)(2,1)S(1)} collective-permute-done((bf16[224,512]{1,0:T(8,128)(2,1)S(1)}, bf16[224,512]{1,0:T(8,128)(2,1)S(1)}, u32[]{:S(2)}, u32[]{:S(2)}) %collective-permute-start.16) | collective-permute-done | bytes 229408 | tf_op jit(solution)/shard_map/back_0_3/ppermute | solution.py:374
  91.9 0.0 collective-permute-done.17.refs_4_
  91.9 1.0 %join.1 = bf16[1,224,2048]{2,1,0:T(8,128)(2,1)} custom-call(bf16[224,512]{1,0:T(8,128)(2,1)S(1)} %get-tuple-element.39.refs_0_, bf16[224,512]{1,0:T(8,128)(2,1)S(1)} %collective-permute-done.14.refs_1_, bf16[224,512]{1,0:T(8,128)(2,1)S(1)} %collective-permute-done.15.refs_2_, bf16[224,512]{1,0:T(8,128)(2,1)S(1)} %collective-permute-done.16.refs_3_, ...), custom_call_target="tpu_custom_call" | custom-call | tf_op jit(solution)/shard_map/join/pallas_call | solution.py:376
  (5 shorter events, 0.0 us)
Async XLA Ops:
  1.1 2.0 %copy-start = (bf16[1,224,2048]{2,1,0:T(8,128)(2,1)S(1)}, bf16[1,224,2048]{2,1,0:T(8,128)(2,1)}, u32[]{:S(2)}) copy-start(bf16[1,224,2048]{2,1,0:T(8,128)(2,1)} %param.5) | copy-start | bytes 2752516
  2.5 4.5 %collective-permute-start = (bf16[256,1536]{1,0:T(8,128)(2,1)S(1)}, bf16[256,1536]{1,0:T(8,128)(2,1)S(1)}, u32[]{:S(2)}, u32[]{:S(2)}) collective-permute-start(bf16[256,1536]{1,0:T(8,128)(2,1)S(1)} %pad_maximum_fusion), channel_id=1, source_target_pairs={{0,4},{1,5},{2,6},{3,7},{4,0},{5,1},{6,2},{7,3},{8,12},{9,13},{10,... | collective-permute-start | bytes 2359304 | tf_op jit(solution)/shard_map/w1/ppermute | solution.py:280
  3.0 26.2 %collective-permute-start.2 = (bf16[224,2048]{1,0:T(8,128)(2,1)S(1)}, bf16[224,2048]{1,0:T(8,128)(2,1)S(1)}, u32[]{:S(2)}, u32[]{:S(2)}) collective-permute-start(bf16[224,2048]{1,0:T(8,128)(2,1)S(1)} %bitcast.1), channel_id=1, source_target_pairs={{2,0},{3,1},{4,6},{5,7},{10,8},{11,9},{12,14},{13,15},{18,16},{19,... | collective-permute-start | bytes 2752520 | tf_op jit(solution)/shard_map/t2/ppermute | solution.py:280
  4.4 18.0 %collective-permute-start.4 = (bf16[256,1536]{1,0:T(8,128)(2,1)S(1)}, bf16[256,1536]{1,0:T(8,128)(2,1)S(1)}, u32[]{:S(2)}, u32[]{:S(2)}) collective-permute-start(bf16[256,1536]{1,0:T(8,128)(2,1)S(1)} %pad_maximum_fusion.1.refs_8_), channel_id=1, source_target_pairs={{0,8},{1,9},{2,10},{3,11},{4,12},{5,13},{6,14},{7,15},{8,0},{9,1},... | collective-permute-start | bytes 2359304 | tf_op jit(solution)/shard_map/w2/ppermute | solution.py:280
  7.0 18.1 %collective-permute-start.3 = (bf16[256,1536]{1,0:T(8,128)(2,1)S(1)}, bf16[256,1536]{1,0:T(8,128)(2,1)S(1)}, u32[]{:S(2)}, u32[]{:S(2)}) collective-permute-start(bf16[256,1536]{1,0:T(8,128)(2,1)S(1)} %collective-permute-done.refs_9_), channel_id=1, source_target_pairs={{0,16},{1,17},{2,18},{3,19},{4,20},{5,21},{6,22},{7,23},{8,24},{9,... | collective-permute-start | bytes 2359304 | tf_op jit(solution)/shard_map/w5/ppermute | solution.py:280
  8.5 42.0 %copy-start.1 = (bf16[2048]{0:T(1024)(128)(2,1)S(1)}, bf16[2048]{0:T(1024)(128)(2,1)}, u32[]{:S(2)}) copy-start(bf16[2048]{0:T(1024)(128)(2,1)} %param.6) | copy-start | bytes 12292
  10.5 23.1 %collective-permute-start.5 = (bf16[224,2048]{1,0:T(8,128)(2,1)S(1)}, bf16[224,2048]{1,0:T(8,128)(2,1)S(1)}, u32[]{:S(2)}, u32[]{:S(2)}) collective-permute-start(bf16[224,2048]{1,0:T(8,128)(2,1)S(1)} %bitcast.2), channel_id=1, source_target_pairs={{0,1},{1,0},{6,7},{7,6},{8,9},{9,8},{14,15},{15,14},{16,17},{17,16... | collective-permute-start | bytes 2752520 | tf_op jit(solution)/shard_map/t1/ppermute | solution.py:280
  14.0 19.6 %collective-permute-start.6 = (bf16[224,2048]{1,0:T(8,128)(2,1)S(1)}, bf16[224,2048]{1,0:T(8,128)(2,1)S(1)}, u32[]{:S(2)}, u32[]{:S(2)}) collective-permute-start(bf16[224,2048]{1,0:T(8,128)(2,1)S(1)} %bitcast.3), channel_id=1, source_target_pairs={{0,4},{1,5},{6,2},{7,3},{8,12},{9,13},{14,10},{15,11},{16,20},{17,... | collective-permute-start | bytes 2752520 | tf_op jit(solution)/shard_map/u0/ppermute | solution.py:280
  29.2 15.3 %collective-permute-start.10 = (bf16[224,2048]{1,0:T(8,128)(2,1)S(1)}, bf16[224,2048]{1,0:T(8,128)(2,1)S(1)}, u32[]{:S(2)}, u32[]{:S(2)}) collective-permute-start(bf16[224,2048]{1,0:T(8,128)(2,1)S(1)} %collective-permute-done.2.refs_2_), channel_id=1, source_target_pairs={{0,1},{1,0},{6,7},{7,6},{8,9},{9,8},{14,15},{15,14},{16,17},{17,16... | collective-permute-start | bytes 2752520 | tf_op jit(solution)/shard_map/t3/ppermute | solution.py:280
  31.1 18.7 %collective-permute-start.8 = (bf16[224,2048]{1,0:T(8,128)(2,1)S(1)}, bf16[224,2048]{1,0:T(8,128)(2,1)S(1)}, u32[]{:S(2)}, u32[]{:S(2)}) collective-permute-start(bf16[224,2048]{1,0:T(8,128)(2,1)S(1)} %collective-permute-done.2.refs_2_), channel_id=1, source_target_pairs={{0,4},{1,5},{6,2},{7,3},{8,12},{9,13},{14,10},{15,11},{16,20},{17,... | collective-permute-start | bytes 2752520 | tf_op jit(solution)/shard_map/u2/ppermute | solution.py:280
  33.6 16.8 %collective-permute-start.7 = (bf16[224,2048]{1,0:T(8,128)(2,1)S(1)}, bf16[224,2048]{1,0:T(8,128)(2,1)S(1)}, u32[]{:S(2)}, u32[]{:S(2)}) collective-permute-start(bf16[224,2048]{1,0:T(8,128)(2,1)S(1)} %collective-permute-done.5.refs_1_), channel_id=1, source_target_pairs={{0,4},{1,5},{6,2},{7,3},{8,12},{9,13},{14,10},{15,11},{16,20},{17,... | collective-permute-start | bytes 2752520 | tf_op jit(solution)/shard_map/u1/ppermute | solution.py:280
  44.5 6.0 %collective-permute-start.11 = (bf16[224,2048]{1,0:T(8,128)(2,1)S(1)}, bf16[224,2048]{1,0:T(8,128)(2,1)S(1)}, u32[]{:S(2)}, u32[]{:S(2)}) collective-permute-start(bf16[224,2048]{1,0:T(8,128)(2,1)S(1)} %collective-permute-done.10.refs_3_), channel_id=1, source_target_pairs={{0,4},{1,5},{6,2},{7,3},{8,12},{9,13},{14,10},{15,11},{16,20},{17,... | collective-permute-start | bytes 2752520 | tf_op jit(solution)/shard_map/u3/ppermute | solution.py:280
  45.9 14.2 %collective-permute-start.12 = (bf16[256,1536]{1,0:T(8,128)(2,1)S(1)}, bf16[256,1536]{1,0:T(8,128)(2,1)S(1)}, u32[]{:S(2)}, u32[]{:S(2)}) collective-permute-start(bf16[256,1536]{1,0:T(8,128)(2,1)S(1)} %collective-permute-done.4.refs_10_), channel_id=1, source_target_pairs={{0,16},{1,17},{2,18},{3,19},{4,20},{5,21},{6,22},{7,23},{8,24},{9,... | collective-permute-start | bytes 2359304 | tf_op jit(solution)/shard_map/w6/ppermute | solution.py:280
  48.4 13.0 %collective-permute-start.13 = (bf16[256,1536]{1,0:T(8,128)(2,1)S(1)}, bf16[256,1536]{1,0:T(8,128)(2,1)S(1)}, u32[]{:S(2)}, u32[]{:S(2)}) collective-permute-start(bf16[256,1536]{1,0:T(8,128)(2,1)S(1)} %collective-permute-done.3.refs_11_), channel_id=1, source_target_pairs={{0,8},{1,9},{2,10},{3,11},{4,12},{5,13},{6,14},{7,15},{8,0},{9,1},... | collective-permute-start | bytes 2359304 | tf_op jit(solution)/shard_map/w7/ppermute | solution.py:280
  49.9 19.9 %collective-permute-start.1 = (bf16[256,1536]{1,0:T(8,128)(2,1)S(1)}, bf16[256,1536]{1,0:T(8,128)(2,1)S(1)}, u32[]{:S(2)}, u32[]{:S(2)}) collective-permute-start(bf16[256,1536]{1,0:T(8,128)(2,1)S(1)} %collective-permute-done.refs_9_), channel_id=1, source_target_pairs={{0,8},{1,9},{2,10},{3,11},{4,12},{5,13},{6,14},{7,15},{8,0},{9,1},... | collective-permute-start | bytes 2359304 | tf_op jit(solution)/shard_map/w3/ppermute | solution.py:280
  50.4 19.4 %collective-permute-start.9 = (bf16[256,1536]{1,0:T(8,128)(2,1)S(1)}, bf16[256,1536]{1,0:T(8,128)(2,1)S(1)}, u32[]{:S(2)}, u32[]{:S(2)}) collective-permute-start(bf16[256,1536]{1,0:T(8,128)(2,1)S(1)} %pad_maximum_fusion.1.refs_8_), channel_id=1, source_target_pairs={{0,16},{1,17},{2,18},{3,19},{4,20},{5,21},{6,22},{7,23},{8,24},{9,... | collective-permute-start | bytes 2359304 | tf_op jit(solution)/shard_map/w4/ppermute | solution.py:280
  77.7 8.8 %collective-permute-start.14 = (bf16[224,512]{1,0:T(8,128)(2,1)S(1)}, bf16[224,512]{1,0:T(8,128)(2,1)S(1)}, u32[]{:S(2)}, u32[]{:S(2)}) collective-permute-start(bf16[224,512]{1,0:T(8,128)(2,1)S(1)} %get-tuple-element.40), channel_id=1, source_target_pairs={{0,1},{1,0},{2,5},{3,4},{4,3},{5,2},{6,7},{7,6},{8,9},{9,8},{10,13... | collective-permute-start | bytes 688136 | tf_op jit(solution)/shard_map/back_0_1/ppermute | solution.py:374
  80.6 5.8 %collective-permute-start.15 = (bf16[224,512]{1,0:T(8,128)(2,1)S(1)}, bf16[224,512]{1,0:T(8,128)(2,1)S(1)}, u32[]{:S(2)}, u32[]{:S(2)}) collective-permute-start(bf16[224,512]{1,0:T(8,128)(2,1)S(1)} %get-tuple-element.39.refs_0_), channel_id=1, source_target_pairs={{2,4},{3,5},{4,2},{5,3},{10,12},{11,13},{12,10},{13,11},{18,20},{1... | collective-permute-start | bytes 688136 | tf_op jit(solution)/shard_map/back_0_0/ppermute | solution.py:374
  81.3 10.5 %collective-permute-start.16 = (bf16[224,512]{1,0:T(8,128)(2,1)S(1)}, bf16[224,512]{1,0:T(8,128)(2,1)S(1)}, u32[]{:S(2)}, u32[]{:S(2)}) collective-permute-start(bf16[224,512]{1,0:T(8,128)(2,1)S(1)} %get-tuple-element.41), channel_id=1, source_target_pairs={{0,3},{1,2},{2,7},{3,6},{4,1},{5,0},{6,5},{7,4},{8,11},{9,10},{10,... | collective-permute-start | bytes 688136 | tf_op jit(solution)/shard_map/back_0_3/ppermute | solution.py:374
  81.4 10.5 %collective-permute-start.17 = (bf16[224,512]{1,0:T(8,128)(2,1)S(1)}, bf16[224,512]{1,0:T(8,128)(2,1)S(1)}, u32[]{:S(2)}, u32[]{:S(2)}) collective-permute-start(bf16[224,512]{1,0:T(8,128)(2,1)S(1)} %get-tuple-element.42), channel_id=1, source_target_pairs={{0,2},{1,3},{2,6},{3,7},{4,0},{5,1},{6,4},{7,5},{8,10},{9,11},{10,... | collective-permute-start | bytes 688136 | tf_op jit(solution)/shard_map/back_0_2/ppermute | solution.py:374

commit v9 on v8

--- a/solution.py
+++ b/solution.py
@@ -110,18 +110,17 @@
 
 
 def early_kernel(*refs):
-    normed, first, shards, out, weights, sems = refs[0], refs[1], refs[2:-3], *refs[-3:]
-    columns = out.shape[1]
-    loads = load_shards(shards, weights, sems, [(0, 0, columns)])
-    for load in loads:
-        load.wait()
-    middle, end = first.shape[0], first.shape[0] + weights.shape[0]
+    normed, first, shards, out = refs[0], refs[1], refs[2:-1], refs[-1]
     step = 2 * HEAD_DIM
-    for lane in range(0, columns, step):
+    for lane in range(0, out.shape[1], step):
         lanes = slice(lane, lane + step)
-        out[:, lanes] = jnp.dot(
-            normed[:, :middle], first[:, lanes], preferred_element_type=jnp.float32
-        ) + jnp.dot(normed[:, middle:end], weights[:, lanes], preferred_element_type=jnp.float32)
+        row = first.shape[0]
+        total = jnp.dot(normed[:, :row], first[:, lanes], preferred_element_type=jnp.float32)
+        for shard in shards:
+            end = row + shard.shape[0]
+            total += jnp.dot(normed[:, row:end], shard[:, lanes], preferred_element_type=jnp.float32)
+            row = end
+        out[:, lanes] = total
 
 
 def late_kernel(rows, cols, total, count, first_head, heads, *refs):
@@ -312,12 +311,8 @@
     partial = pl.pallas_call(
         early_kernel,
         out_shape=jax.ShapeDtypeStruct((length, 3 * cols), jnp.float32),
-        in_specs=[vmem] * 2 + [any_space] * (n - 4),
+        in_specs=[vmem] * (n - 2),
         out_specs=vmem,
-        scratch_shapes=[
-            pltpu.VMEM(((n - 4) * depth, 3 * cols), jnp.bfloat16),
-            pltpu.SemaphoreType.DMA((n - 4,)),
-        ],
         compiler_params=pltpu.CompilerParams(vmem_limit_bytes=VMEM_LIMIT),
         cost_estimate=pl.CostEstimate(
             flops=plan["early_flops"], bytes_accessed=1_000_000, transcendentals=0

time: 94 us -> 94 us (level)
  no operation moved by 1% of the time
where the time goes in v9:
time: 94 us; the launch traced here: 92.9 us
  waiting for transfers between devices  43.9 us (47%)
  starting transfers between devices  27.7 us (29%)
  Pallas kernels  16.6 us (18%)
  local copies, waits for them, and re-layouts  2.45 us (3%)
  other arithmetic  2.1 us (2%)
    ppermute x14, waiting for transfers between devices, fast(): values[name] = lax.ppermute(operand, ('dp', 'ctx'), perm)  35.4 us
    ppermute x14, starting transfers between devices, fast(): values[name] = lax.ppermute(operand, ('dp', 'ctx'), perm)  22 us
    ppermute x4, waiting for transfers between devices, fast(): moved[k] = lax.ppermute(pieces[k], ('dp', 'ctx'), perm)  8.53 us
    pallas_call x1, Pallas kernels, fast(): pl.pallas_call(functools.partial(late_kernel, rows, cols, ctx, late, firs...  7.89 us
    ppermute x4, starting transfers between devices, fast(): moved[k] = lax.ppermute(pieces[k], ('dp', 'ctx'), perm)  5.65 us
    pallas_call x1, Pallas kernels, fast(): pl.pallas_call(early_kernel, out_shape=jax.ShapeDtypeStruct((length, 3 *...  4.41 us
    pallas_call x1, Pallas kernels, fast(): pl.pallas_call(functools.partial(norm_kernel, rows, shard_order), out_sha...  3.26 us
    dynamic_slice x2, local copies, waits for them, and re-layouts, columns(): lax.dynamic_slice_in_dim(w, heads * cols, cols, 1)  2.43 us
  transfers between devices with their start and end apart: 18, of which 10 were waited for; matrix products, arithmetic and copies ran while one was open for 2% of the time, Pallas kernels for 8%

profile of v9, /device:TPU:0, one launch (start us, length us, event | category | flops | bytes accessed | tf_op | source)
XLA Modules:
  0.0 92.9 jit_solution(3341838151766092361)
XLA Ops:
  0.0 1.1 %constant_dynamic-slice_fusion.2 = (bf16[256,512]{1,0:T(8,128)(2,1)S(1)}, bf16[256,512]{1,0:T(8,128)(2,1)S(1)}) fusion(bf16[256,2048]{1,0:T(8,128)(2,1)} %param.7, s32[]{:T(128)S(6)} %select_n.24, s32[]{:T(128)S(6)} %select_n.23), kind=kLoop, calls=%fused_computation.10 | loop fusion | bytes 1048584 | tf_op jit(solution)/shard_map/dynamic_slice | solution.py:257
  1.1 0.0 copy-start
  1.1 1.4 %constant_dynamic-slice_fusion = (bf16[256,512]{1,0:T(8,128)(2,1)S(1)}, bf16[256,512]{1,0:T(8,128)(2,1)S(1)}, bf16[256,512]{1,0:T(8,128)(2,1)S(1)}, bf16[256,512]{1,0:T(8,128)(2,1)S(1)}) fusion(bf16[256,2048]{1,0:T(8,128)(2,1)} %param.9, s32[]{:T(128)S(6)} %select_n.24, s32[]{:T(128)S(6)} %select_n.23, bf16[256,2048]{1,0:T(8,128)(2,1)} %param.8), kind=kLoop, calls=%fused_computation.8 | loop fusion | bytes 2097160 | tf_op jit(solution)/shard_map/dynamic_slice | solution.py:257
  2.5 0.1 pad_maximum_fusion
  2.5 0.5 collective-permute-start
  3.0 1.3 %collective-permute-start.2 = (bf16[224,2048]{1,0:T(8,128)(2,1)S(1)}, bf16[224,2048]{1,0:T(8,128)(2,1)S(1)}, u32[]{:S(2)}, u32[]{:S(2)}) collective-permute-start(bf16[224,2048]{1,0:T(8,128)(2,1)S(1)} %bitcast.1), channel_id=1, source_target_pairs={{2,0},{3,1},{4,6},{5,7},{10,8},{11,9},{12,14},{13,15},{18,16},{19,... | collective-permute-start | bytes 2752520 | tf_op jit(solution)/shard_map/t2/ppermute | solution.py:279
  4.3 0.1 pad_maximum_fusion.1.refs_8_
  4.4 2.6 %collective-permute-start.4 = (bf16[256,1536]{1,0:T(8,128)(2,1)S(1)}, bf16[256,1536]{1,0:T(8,128)(2,1)S(1)}, u32[]{:S(2)}, u32[]{:S(2)}) collective-permute-start(bf16[256,1536]{1,0:T(8,128)(2,1)S(1)} %pad_maximum_fusion.1.refs_8_), channel_id=1, source_target_pairs={{0,8},{1,9},{2,10},{3,11},{4,12},{5,13},{6,14},{7,15},{8,0},{9,1},... | collective-permute-start | bytes 2359304 | tf_op jit(solution)/shard_map/w2/ppermute | solution.py:279
  7.0 0.0 collective-permute-done.refs_9_
  7.0 1.5 %collective-permute-start.3 = (bf16[256,1536]{1,0:T(8,128)(2,1)S(1)}, bf16[256,1536]{1,0:T(8,128)(2,1)S(1)}, u32[]{:S(2)}, u32[]{:S(2)}) collective-permute-start(bf16[256,1536]{1,0:T(8,128)(2,1)S(1)} %collective-permute-done.refs_9_), channel_id=1, source_target_pairs={{0,16},{1,17},{2,18},{3,19},{4,20},{5,21},{6,22},{7,23},{8,24},{9,... | collective-permute-start | bytes 2359304 | tf_op jit(solution)/shard_map/w5/ppermute | solution.py:279
  8.5 0.0 copy-start.1
  8.5 1.7 %fusion = (f32[896,64]{1,0:T(8,128)S(1)}, f32[896,64]{1,0:T(8,128)S(1)}, f32[896,64]{1,0:T(8,128)S(1)}) fusion(f32[64]{0:T(128)S(1)} %multiply_power_fusion, f32[896]{0:T(1024)S(1)} %iota_convert_fusion), kind=kLoop, calls=%fused_computation.6 | loop fusion | flops 114688 | bytes 691968 | tf_op jit(solution)/shard_map/neg | solution.py:41
  10.2 0.3 pad_maximum_fusion.2
  10.5 3.5 %collective-permute-start.5 = (bf16[224,2048]{1,0:T(8,128)(2,1)S(1)}, bf16[224,2048]{1,0:T(8,128)(2,1)S(1)}, u32[]{:S(2)}, u32[]{:S(2)}) collective-permute-start(bf16[224,2048]{1,0:T(8,128)(2,1)S(1)} %bitcast.2), channel_id=1, source_target_pairs={{0,1},{1,0},{6,7},{7,6},{8,9},{9,8},{14,15},{15,14},{16,17},{17,16... | collective-permute-start | bytes 2752520 | tf_op jit(solution)/shard_map/t1/ppermute | solution.py:279
  14.0 2.1 %collective-permute-start.6 = (bf16[224,2048]{1,0:T(8,128)(2,1)S(1)}, bf16[224,2048]{1,0:T(8,128)(2,1)S(1)}, u32[]{:S(2)}, u32[]{:S(2)}) collective-permute-start(bf16[224,2048]{1,0:T(8,128)(2,1)S(1)} %bitcast.3), channel_id=1, source_target_pairs={{0,4},{1,5},{6,2},{7,3},{8,12},{9,13},{14,10},{15,11},{16,20},{17,... | collective-permute-start | bytes 2752520 | tf_op jit(solution)/shard_map/u0/ppermute | solution.py:279
  16.1 6.2 %collective-permute-done.4.refs_10_ = bf16[256,1536]{1,0:T(8,128)(2,1)S(1)} collective-permute-done((bf16[256,1536]{1,0:T(8,128)(2,1)S(1)}, bf16[256,1536]{1,0:T(8,128)(2,1)S(1)}, u32[]{:S(2)}, u32[]{:S(2)}) %collective-permute-start.4) | collective-permute-done | bytes 786464 | tf_op jit(solution)/shard_map/w2/ppermute | solution.py:279
  22.4 2.8 %collective-permute-done.3.refs_11_ = bf16[256,1536]{1,0:T(8,128)(2,1)S(1)} collective-permute-done((bf16[256,1536]{1,0:T(8,128)(2,1)S(1)}, bf16[256,1536]{1,0:T(8,128)(2,1)S(1)}, u32[]{:S(2)}, u32[]{:S(2)}) %collective-permute-start.3) | collective-permute-done | bytes 786464 | tf_op jit(solution)/shard_map/w5/ppermute | solution.py:279
  25.1 4.1 %collective-permute-done.2.refs_2_ = bf16[224,2048]{1,0:T(8,128)(2,1)S(1)} collective-permute-done((bf16[224,2048]{1,0:T(8,128)(2,1)S(1)}, bf16[224,2048]{1,0:T(8,128)(2,1)S(1)}, u32[]{:S(2)}, u32[]{:S(2)}) %collective-permute-start.2) | collective-permute-done | bytes 917536 | tf_op jit(solution)/shard_map/t2/ppermute | solution.py:279
  29.2 1.9 %collective-permute-start.10 = (bf16[224,2048]{1,0:T(8,128)(2,1)S(1)}, bf16[224,2048]{1,0:T(8,128)(2,1)S(1)}, u32[]{:S(2)}, u32[]{:S(2)}) collective-permute-start(bf16[224,2048]{1,0:T(8,128)(2,1)S(1)} %collective-permute-done.2.refs_2_), channel_id=1, source_target_pairs={{0,1},{1,0},{6,7},{7,6},{8,9},{9,8},{14,15},{15,14},{16,17},{17,16... | collective-permute-start | bytes 2752520 | tf_op jit(solution)/shard_map/t3/ppermute | solution.py:279
  31.1 1.3 %collective-permute-start.8 = (bf16[224,2048]{1,0:T(8,128)(2,1)S(1)}, bf16[224,2048]{1,0:T(8,128)(2,1)S(1)}, u32[]{:S(2)}, u32[]{:S(2)}) collective-permute-start(bf16[224,2048]{1,0:T(8,128)(2,1)S(1)} %collective-permute-done.2.refs_2_), channel_id=1, source_target_pairs={{0,4},{1,5},{6,2},{7,3},{8,12},{9,13},{14,10},{15,11},{16,20},{17,... | collective-permute-start | bytes 2752520 | tf_op jit(solution)/shard_map/u2/ppermute | solution.py:279
  32.5 1.1 %collective-permute-done.5.refs_1_ = bf16[224,2048]{1,0:T(8,128)(2,1)S(1)} collective-permute-done((bf16[224,2048]{1,0:T(8,128)(2,1)S(1)}, bf16[224,2048]{1,0:T(8,128)(2,1)S(1)}, u32[]{:S(2)}, u32[]{:S(2)}) %collective-permute-start.5) | collective-permute-done | bytes 917536 | tf_op jit(solution)/shard_map/t1/ppermute | solution.py:279
  33.6 0.0 collective-permute-done.6.refs_4_
  33.6 1.3 %collective-permute-start.7 = (bf16[224,2048]{1,0:T(8,128)(2,1)S(1)}, bf16[224,2048]{1,0:T(8,128)(2,1)S(1)}, u32[]{:S(2)}, u32[]{:S(2)}) collective-permute-start(bf16[224,2048]{1,0:T(8,128)(2,1)S(1)} %collective-permute-done.5.refs_1_), channel_id=1, source_target_pairs={{0,4},{1,5},{6,2},{7,3},{8,12},{9,13},{14,10},{15,11},{16,20},{17,... | collective-permute-start | bytes 2752520 | tf_op jit(solution)/shard_map/u1/ppermute | solution.py:279
  34.9 9.6 %collective-permute-done.10.refs_3_ = bf16[224,2048]{1,0:T(8,128)(2,1)S(1)} collective-permute-done((bf16[224,2048]{1,0:T(8,128)(2,1)S(1)}, bf16[224,2048]{1,0:T(8,128)(2,1)S(1)}, u32[]{:S(2)}, u32[]{:S(2)}) %collective-permute-start.10) | collective-permute-done | bytes 917536 | tf_op jit(solution)/shard_map/t3/ppermute | solution.py:279
  44.5 1.3 %collective-permute-start.11 = (bf16[224,2048]{1,0:T(8,128)(2,1)S(1)}, bf16[224,2048]{1,0:T(8,128)(2,1)S(1)}, u32[]{:S(2)}, u32[]{:S(2)}) collective-permute-start(bf16[224,2048]{1,0:T(8,128)(2,1)S(1)} %collective-permute-done.10.refs_3_), channel_id=1, source_target_pairs={{0,4},{1,5},{6,2},{7,3},{8,12},{9,13},{14,10},{15,11},{16,20},{17,... | collective-permute-start | bytes 2752520 | tf_op jit(solution)/shard_map/u3/ppermute | solution.py:279
  45.9 2.5 %collective-permute-start.12 = (bf16[256,1536]{1,0:T(8,128)(2,1)S(1)}, bf16[256,1536]{1,0:T(8,128)(2,1)S(1)}, u32[]{:S(2)}, u32[]{:S(2)}) collective-permute-start(bf16[256,1536]{1,0:T(8,128)(2,1)S(1)} %collective-permute-done.4.refs_10_), channel_id=1, source_target_pairs={{0,16},{1,17},{2,18},{3,19},{4,20},{5,21},{6,22},{7,23},{8,24},{9,... | collective-permute-start | bytes 2359304 | tf_op jit(solution)/shard_map/w6/ppermute | solution.py:279
  48.4 1.5 %collective-permute-start.13 = (bf16[256,1536]{1,0:T(8,128)(2,1)S(1)}, bf16[256,1536]{1,0:T(8,128)(2,1)S(1)}, u32[]{:S(2)}, u32[]{:S(2)}) collective-permute-start(bf16[256,1536]{1,0:T(8,128)(2,1)S(1)} %collective-permute-done.3.refs_11_), channel_id=1, source_target_pairs={{0,8},{1,9},{2,10},{3,11},{4,12},{5,13},{6,14},{7,15},{8,0},{9,1},... | collective-permute-start | bytes 2359304 | tf_op jit(solution)/shard_map/w7/ppermute | solution.py:279
  49.9 0.0 collective-permute-done.8.refs_6_
  49.9 0.5 collective-permute-start.1
  50.4 0.0 collective-permute-done.7.refs_5_
  50.4 0.1 collective-permute-start.9
  50.5 0.0 collective-permute-done.11.refs_7_
  50.5 3.3 %normalize.1 = (bf16[896,2048]{1,0:T(8,128)(2,1)S(1)}, bf16[1024,1536]{1,0:T(8,128)(2,1)S(1)}) custom-call(bf16[224,2048]{1,0:T(8,128)(2,1)S(1)} %bitcast.4, bf16[224,2048]{1,0:T(8,128)(2,1)S(1)} %collective-permute-done.5.refs_1_, bf16[224,2048]{1,0:T(8,128)(2,1)S(1)} %collective-permute-done.2.refs_2_, ...), custom_call_target="tpu_custom_call" | custom-call | flops 4000000000 | bytes 1000000 | tf_op jit(solution)/shard_map/normalize/pallas_call | solution.py:292
  53.8 6.3 %collective-permute-done.12.refs_2_ = bf16[256,1536]{1,0:T(8,128)(2,1)S(1)} collective-permute-done((bf16[256,1536]{1,0:T(8,128)(2,1)S(1)}, bf16[256,1536]{1,0:T(8,128)(2,1)S(1)}, u32[]{:S(2)}, u32[]{:S(2)}) %collective-permute-start.12) | collective-permute-done | bytes 786464 | tf_op jit(solution)/shard_map/w6/ppermute | solution.py:279
  60.1 1.2 %collective-permute-done.13.refs_3_ = bf16[256,1536]{1,0:T(8,128)(2,1)S(1)} collective-permute-done((bf16[256,1536]{1,0:T(8,128)(2,1)S(1)}, bf16[256,1536]{1,0:T(8,128)(2,1)S(1)}, u32[]{:S(2)}, u32[]{:S(2)}) %collective-permute-start.13) | collective-permute-done | bytes 786464 | tf_op jit(solution)/shard_map/w7/ppermute | solution.py:279
  61.3 4.4 %project_early.1.refs_2_ = f32[896,1536]{1,0:T(8,128)S(1)} custom-call(bf16[896,2048]{1,0:T(8,128)(2,1)S(1)} %get-tuple-element.33.refs_0_.refs_3_, bf16[1024,1536]{1,0:T(8,128)(2,1)S(1)} %get-tuple-element.34.refs_1_, bf16[256,1536]{1,0:T(8,128)(2,1)S(1)} %collective-permute-done.12.refs_2_, bf16[256,1536]{1,0:T(8,128)(2,1)S(1)} %collective-permute-done.13.refs_3_), custom_call_target="tpu_custom_call" | custom-call | flops 4000000000 | bytes 1000000 | tf_op jit(solution)/shard_map/project_early/pallas_call | solution.py:311
  65.8 4.0 %collective-permute-done.1.refs_0_ = bf16[256,1536]{1,0:T(8,128)(2,1)S(1)} collective-permute-done((bf16[256,1536]{1,0:T(8,128)(2,1)S(1)}, bf16[256,1536]{1,0:T(8,128)(2,1)S(1)}, u32[]{:S(2)}, u32[]{:S(2)}) %collective-permute-start.1) | collective-permute-done | bytes 786464 | tf_op jit(solution)/shard_map/w3/ppermute | solution.py:279
  69.8 0.0 collective-permute-done.9.refs_1_
  69.8 7.9 %attend_0.1 = (bf16[224,512]{1,0:T(8,128)(2,1)S(1)}, bf16[224,512]{1,0:T(8,128)(2,1)S(1)}, bf16[224,512]{1,0:T(8,128)(2,1)S(1)}, bf16[224,512]{1,0:T(8,128)(2,1)S(1)}) custom-call(bf16[256,1536]{1,0:T(8,128)(2,1)S(1)} %collective-permute-done.1.refs_0_, bf16[256,1536]{1,0:T(8,128)(2,1)S(1)} %collective-permute-done.9.refs_1_, ...), custom_call_target="tpu_custom_call" | custom-call | flops 1000000 | bytes 1000000 | tf_op jit(solution)/shard_map/attend_0/pallas_call | solution.py:335
  77.7 3.0 %collective-permute-start.14 = (bf16[224,512]{1,0:T(8,128)(2,1)S(1)}, bf16[224,512]{1,0:T(8,128)(2,1)S(1)}, u32[]{:S(2)}, u32[]{:S(2)}) collective-permute-start(bf16[224,512]{1,0:T(8,128)(2,1)S(1)} %get-tuple-element.40), channel_id=1, source_target_pairs={{0,1},{1,0},{2,5},{3,4},{4,3},{5,2},{6,7},{7,6},{8,9},{9,8},{10,13... | collective-permute-start | bytes 688136 | tf_op jit(solution)/shard_map/back_0_1/ppermute | solution.py:369
  80.6 0.7 collective-permute-start.15
  81.3 0.1 collective-permute-start.16
  81.4 1.9 %collective-permute-start.17 = (bf16[224,512]{1,0:T(8,128)(2,1)S(1)}, bf16[224,512]{1,0:T(8,128)(2,1)S(1)}, u32[]{:S(2)}, u32[]{:S(2)}) collective-permute-start(bf16[224,512]{1,0:T(8,128)(2,1)S(1)} %get-tuple-element.42), channel_id=1, source_target_pairs={{0,2},{1,3},{2,6},{3,7},{4,0},{5,1},{6,4},{7,5},{8,10},{9,11},{10,... | collective-permute-start | bytes 688136 | tf_op jit(solution)/shard_map/back_0_2/ppermute | solution.py:369
  83.3 3.1 %collective-permute-done.14.refs_1_ = bf16[224,512]{1,0:T(8,128)(2,1)S(1)} collective-permute-done((bf16[224,512]{1,0:T(8,128)(2,1)S(1)}, bf16[224,512]{1,0:T(8,128)(2,1)S(1)}, u32[]{:S(2)}, u32[]{:S(2)}) %collective-permute-start.14) | collective-permute-done | bytes 229408 | tf_op jit(solution)/shard_map/back_0_1/ppermute | solution.py:369
  86.5 0.0 collective-permute-done.15.refs_2_
  86.5 5.4 %collective-permute-done.16.refs_3_ = bf16[224,512]{1,0:T(8,128)(2,1)S(1)} collective-permute-done((bf16[224,512]{1,0:T(8,128)(2,1)S(1)}, bf16[224,512]{1,0:T(8,128)(2,1)S(1)}, u32[]{:S(2)}, u32[]{:S(2)}) %collective-permute-start.16) | collective-permute-done | bytes 229408 | tf_op jit(solution)/shard_map/back_0_3/ppermute | solution.py:369
  91.9 0.0 collective-permute-done.17.refs_4_
  91.9 1.0 %join.1 = bf16[1,224,2048]{2,1,0:T(8,128)(2,1)} custom-call(bf16[224,512]{1,0:T(8,128)(2,1)S(1)} %get-tuple-element.39.refs_0_, bf16[224,512]{1,0:T(8,128)(2,1)S(1)} %collective-permute-done.14.refs_1_, bf16[224,512]{1,0:T(8,128)(2,1)S(1)} %collective-permute-done.15.refs_2_, bf16[224,512]{1,0:T(8,128)(2,1)S(1)} %collective-permute-done.16.refs_3_, ...), custom_call_target="tpu_custom_call" | custom-call | tf_op jit(solution)/shard_map/join/pallas_call | solution.py:371
  (5 shorter events, 0.0 us)
Async XLA Ops:
  1.1 2.0 %copy-start = (bf16[1,224,2048]{2,1,0:T(8,128)(2,1)S(1)}, bf16[1,224,2048]{2,1,0:T(8,128)(2,1)}, u32[]{:S(2)}) copy-start(bf16[1,224,2048]{2,1,0:T(8,128)(2,1)} %param.5) | copy-start | bytes 2752516
  2.5 4.5 %collective-permute-start = (bf16[256,1536]{1,0:T(8,128)(2,1)S(1)}, bf16[256,1536]{1,0:T(8,128)(2,1)S(1)}, u32[]{:S(2)}, u32[]{:S(2)}) collective-permute-start(bf16[256,1536]{1,0:T(8,128)(2,1)S(1)} %pad_maximum_fusion), channel_id=1, source_target_pairs={{0,4},{1,5},{2,6},{3,7},{4,0},{5,1},{6,2},{7,3},{8,12},{9,13},{10,... | collective-permute-start | bytes 2359304 | tf_op jit(solution)/shard_map/w1/ppermute | solution.py:279
  3.0 26.2 %collective-permute-start.2 = (bf16[224,2048]{1,0:T(8,128)(2,1)S(1)}, bf16[224,2048]{1,0:T(8,128)(2,1)S(1)}, u32[]{:S(2)}, u32[]{:S(2)}) collective-permute-start(bf16[224,2048]{1,0:T(8,128)(2,1)S(1)} %bitcast.1), channel_id=1, source_target_pairs={{2,0},{3,1},{4,6},{5,7},{10,8},{11,9},{12,14},{13,15},{18,16},{19,... | collective-permute-start | bytes 2752520 | tf_op jit(solution)/shard_map/t2/ppermute | solution.py:279
  4.4 18.0 %collective-permute-start.4 = (bf16[256,1536]{1,0:T(8,128)(2,1)S(1)}, bf16[256,1536]{1,0:T(8,128)(2,1)S(1)}, u32[]{:S(2)}, u32[]{:S(2)}) collective-permute-start(bf16[256,1536]{1,0:T(8,128)(2,1)S(1)} %pad_maximum_fusion.1.refs_8_), channel_id=1, source_target_pairs={{0,8},{1,9},{2,10},{3,11},{4,12},{5,13},{6,14},{7,15},{8,0},{9,1},... | collective-permute-start | bytes 2359304 | tf_op jit(solution)/shard_map/w2/ppermute | solution.py:279
  7.0 18.1 %collective-permute-start.3 = (bf16[256,1536]{1,0:T(8,128)(2,1)S(1)}, bf16[256,1536]{1,0:T(8,128)(2,1)S(1)}, u32[]{:S(2)}, u32[]{:S(2)}) collective-permute-start(bf16[256,1536]{1,0:T(8,128)(2,1)S(1)} %collective-permute-done.refs_9_), channel_id=1, source_target_pairs={{0,16},{1,17},{2,18},{3,19},{4,20},{5,21},{6,22},{7,23},{8,24},{9,... | collective-permute-start | bytes 2359304 | tf_op jit(solution)/shard_map/w5/ppermute | solution.py:279
  8.5 42.0 %copy-start.1 = (bf16[2048]{0:T(1024)(128)(2,1)S(1)}, bf16[2048]{0:T(1024)(128)(2,1)}, u32[]{:S(2)}) copy-start(bf16[2048]{0:T(1024)(128)(2,1)} %param.6) | copy-start | bytes 12292
  10.5 23.1 %collective-permute-start.5 = (bf16[224,2048]{1,0:T(8,128)(2,1)S(1)}, bf16[224,2048]{1,0:T(8,128)(2,1)S(1)}, u32[]{:S(2)}, u32[]{:S(2)}) collective-permute-start(bf16[224,2048]{1,0:T(8,128)(2,1)S(1)} %bitcast.2), channel_id=1, source_target_pairs={{0,1},{1,0},{6,7},{7,6},{8,9},{9,8},{14,15},{15,14},{16,17},{17,16... | collective-permute-start | bytes 2752520 | tf_op jit(solution)/shard_map/t1/ppermute | solution.py:279
  14.0 19.6 %collective-permute-start.6 = (bf16[224,2048]{1,0:T(8,128)(2,1)S(1)}, bf16[224,2048]{1,0:T(8,128)(2,1)S(1)}, u32[]{:S(2)}, u32[]{:S(2)}) collective-permute-start(bf16[224,2048]{1,0:T(8,128)(2,1)S(1)} %bitcast.3), channel_id=1, source_target_pairs={{0,4},{1,5},{6,2},{7,3},{8,12},{9,13},{14,10},{15,11},{16,20},{17,... | collective-permute-start | bytes 2752520 | tf_op jit(solution)/shard_map/u0/ppermute | solution.py:279
  29.2 15.3 %collective-permute-start.10 = (bf16[224,2048]{1,0:T(8,128)(2,1)S(1)}, bf16[224,2048]{1,0:T(8,128)(2,1)S(1)}, u32[]{:S(2)}, u32[]{:S(2)}) collective-permute-start(bf16[224,2048]{1,0:T(8,128)(2,1)S(1)} %collective-permute-done.2.refs_2_), channel_id=1, source_target_pairs={{0,1},{1,0},{6,7},{7,6},{8,9},{9,8},{14,15},{15,14},{16,17},{17,16... | collective-permute-start | bytes 2752520 | tf_op jit(solution)/shard_map/t3/ppermute | solution.py:279
  31.1 18.7 %collective-permute-start.8 = (bf16[224,2048]{1,0:T(8,128)(2,1)S(1)}, bf16[224,2048]{1,0:T(8,128)(2,1)S(1)}, u32[]{:S(2)}, u32[]{:S(2)}) collective-permute-start(bf16[224,2048]{1,0:T(8,128)(2,1)S(1)} %collective-permute-done.2.refs_2_), channel_id=1, source_target_pairs={{0,4},{1,5},{6,2},{7,3},{8,12},{9,13},{14,10},{15,11},{16,20},{17,... | collective-permute-start | bytes 2752520 | tf_op jit(solution)/shard_map/u2/ppermute | solution.py:279
  33.6 16.8 %collective-permute-start.7 = (bf16[224,2048]{1,0:T(8,128)(2,1)S(1)}, bf16[224,2048]{1,0:T(8,128)(2,1)S(1)}, u32[]{:S(2)}, u32[]{:S(2)}) collective-permute-start(bf16[224,2048]{1,0:T(8,128)(2,1)S(1)} %collective-permute-done.5.refs_1_), channel_id=1, source_target_pairs={{0,4},{1,5},{6,2},{7,3},{8,12},{9,13},{14,10},{15,11},{16,20},{17,... | collective-permute-start | bytes 2752520 | tf_op jit(solution)/shard_map/u1/ppermute | solution.py:279
  44.5 6.0 %collective-permute-start.11 = (bf16[224,2048]{1,0:T(8,128)(2,1)S(1)}, bf16[224,2048]{1,0:T(8,128)(2,1)S(1)}, u32[]{:S(2)}, u32[]{:S(2)}) collective-permute-start(bf16[224,2048]{1,0:T(8,128)(2,1)S(1)} %collective-permute-done.10.refs_3_), channel_id=1, source_target_pairs={{0,4},{1,5},{6,2},{7,3},{8,12},{9,13},{14,10},{15,11},{16,20},{17,... | collective-permute-start | bytes 2752520 | tf_op jit(solution)/shard_map/u3/ppermute | solution.py:279
  45.9 14.2 %collective-permute-start.12 = (bf16[256,1536]{1,0:T(8,128)(2,1)S(1)}, bf16[256,1536]{1,0:T(8,128)(2,1)S(1)}, u32[]{:S(2)}, u32[]{:S(2)}) collective-permute-start(bf16[256,1536]{1,0:T(8,128)(2,1)S(1)} %collective-permute-done.4.refs_10_), channel_id=1, source_target_pairs={{0,16},{1,17},{2,18},{3,19},{4,20},{5,21},{6,22},{7,23},{8,24},{9,... | collective-permute-start | bytes 2359304 | tf_op jit(solution)/shard_map/w6/ppermute | solution.py:279
  48.4 13.0 %collective-permute-start.13 = (bf16[256,1536]{1,0:T(8,128)(2,1)S(1)}, bf16[256,1536]{1,0:T(8,128)(2,1)S(1)}, u32[]{:S(2)}, u32[]{:S(2)}) collective-permute-start(bf16[256,1536]{1,0:T(8,128)(2,1)S(1)} %collective-permute-done.3.refs_11_), channel_id=1, source_target_pairs={{0,8},{1,9},{2,10},{3,11},{4,12},{5,13},{6,14},{7,15},{8,0},{9,1},... | collective-permute-start | bytes 2359304 | tf_op jit(solution)/shard_map/w7/ppermute | solution.py:279
  49.9 19.9 %collective-permute-start.1 = (bf16[256,1536]{1,0:T(8,128)(2,1)S(1)}, bf16[256,1536]{1,0:T(8,128)(2,1)S(1)}, u32[]{:S(2)}, u32[]{:S(2)}) collective-permute-start(bf16[256,1536]{1,0:T(8,128)(2,1)S(1)} %collective-permute-done.refs_9_), channel_id=1, source_target_pairs={{0,8},{1,9},{2,10},{3,11},{4,12},{5,13},{6,14},{7,15},{8,0},{9,1},... | collective-permute-start | bytes 2359304 | tf_op jit(solution)/shard_map/w3/ppermute | solution.py:279
  50.4 19.4 %collective-permute-start.9 = (bf16[256,1536]{1,0:T(8,128)(2,1)S(1)}, bf16[256,1536]{1,0:T(8,128)(2,1)S(1)}, u32[]{:S(2)}, u32[]{:S(2)}) collective-permute-start(bf16[256,1536]{1,0:T(8,128)(2,1)S(1)} %pad_maximum_fusion.1.refs_8_), channel_id=1, source_target_pairs={{0,16},{1,17},{2,18},{3,19},{4,20},{5,21},{6,22},{7,23},{8,24},{9,... | collective-permute-start | bytes 2359304 | tf_op jit(solution)/shard_map/w4/ppermute | solution.py:279
  77.7 8.8 %collective-permute-start.14 = (bf16[224,512]{1,0:T(8,128)(2,1)S(1)}, bf16[224,512]{1,0:T(8,128)(2,1)S(1)}, u32[]{:S(2)}, u32[]{:S(2)}) collective-permute-start(bf16[224,512]{1,0:T(8,128)(2,1)S(1)} %get-tuple-element.40), channel_id=1, source_target_pairs={{0,1},{1,0},{2,5},{3,4},{4,3},{5,2},{6,7},{7,6},{8,9},{9,8},{10,13... | collective-permute-start | bytes 688136 | tf_op jit(solution)/shard_map/back_0_1/ppermute | solution.py:369
  80.6 5.8 %collective-permute-start.15 = (bf16[224,512]{1,0:T(8,128)(2,1)S(1)}, bf16[224,512]{1,0:T(8,128)(2,1)S(1)}, u32[]{:S(2)}, u32[]{:S(2)}) collective-permute-start(bf16[224,512]{1,0:T(8,128)(2,1)S(1)} %get-tuple-element.39.refs_0_), channel_id=1, source_target_pairs={{2,4},{3,5},{4,2},{5,3},{10,12},{11,13},{12,10},{13,11},{18,20},{1... | collective-permute-start | bytes 688136 | tf_op jit(solution)/shard_map/back_0_0/ppermute | solution.py:369
  81.3 10.5 %collective-permute-start.16 = (bf16[224,512]{1,0:T(8,128)(2,1)S(1)}, bf16[224,512]{1,0:T(8,128)(2,1)S(1)}, u32[]{:S(2)}, u32[]{:S(2)}) collective-permute-start(bf16[224,512]{1,0:T(8,128)(2,1)S(1)} %get-tuple-element.41), channel_id=1, source_target_pairs={{0,3},{1,2},{2,7},{3,6},{4,1},{5,0},{6,5},{7,4},{8,11},{9,10},{10,... | collective-permute-start | bytes 688136 | tf_op jit(solution)/shard_map/back_0_3/ppermute | solution.py:369
  81.4 10.5 %collective-permute-start.17 = (bf16[224,512]{1,0:T(8,128)(2,1)S(1)}, bf16[224,512]{1,0:T(8,128)(2,1)S(1)}, u32[]{:S(2)}, u32[]{:S(2)}) collective-permute-start(bf16[224,512]{1,0:T(8,128)(2,1)S(1)} %get-tuple-element.42), channel_id=1, source_target_pairs={{0,2},{1,3},{2,6},{3,7},{4,0},{5,1},{6,4},{7,5},{8,10},{9,11},{10,... | collective-permute-start | bytes 688136 | tf_op jit(solution)/shard_map/back_0_2/ppermute | solution.py:369
